TPU v7x, 32 devices: a whole 2x2x4 slice. The times are simulated.
32 devices in a mesh: wide: 16 (over z, y, x), narrow: 2 (over core).
Axes of the slice: x: 2, y: 2, z: 4, core: 2. Of those that a mesh axis runs over, the one named last changes fastest.
Arguments:
- x_src: bfloat16 [2048, 16384], P('narrow', 'wide'), may hold values from -6 to 6
- cond: bfloat16 [128, 1024], P('narrow', 'wide'), may hold values from -6 to 6
- lengths: int32 [128], replicated, may hold values from 0 to 1024, as said below
- bucket: int32 [128], replicated, may hold values from 0 to 15
- w_mod: bfloat16 [1024, 6144], replicated, may hold values from -0.1875 to 0.1875
- b_mod: bfloat16 [6144], replicated, may hold values from -3 to 3
- w_qkv: bfloat16 [1024, 3072], replicated, may hold values from -0.1875 to 0.1875
- b_qv: bfloat16 [2048], replicated, may hold values from -0.29882812 to 0.29882812
- w_proj: bfloat16 [1024, 1024], replicated, may hold values from -3 to 3
- b_proj: bfloat16 [1024], replicated, may hold values from -2 to 2
- w_fc1: bfloat16 [1024, 4096], replicated, may hold values from -0.1875 to 0.1875
- b_fc1: bfloat16 [4096], replicated, may hold values from -2 to 2
- w_fc2: bfloat16 [4096, 1024], replicated, may hold values from -0.09375 to 0.09375
- b_fc2: bfloat16 [1024], replicated, may hold values from -2 to 2
- grad_out: bfloat16 [32768, 1024], P(('wide', 'narrow')), may hold values from -6 to 6
Outputs:
- y_dest: bfloat16 [32768, 1024], P(('wide', 'narrow'))
- dx_src: bfloat16 [2048, 16384], P('narrow', 'wide')
- dcond: bfloat16 [128, 1024], P('narrow', 'wide')
- grad_w_mod: float32 [1024, 6144], P(('wide', 'narrow'))
- grad_b_mod: float32 [6144], P(('wide', 'narrow'))
- grad_w_qkv: float32 [1024, 3072], P(('wide', 'narrow'))
- grad_b_qv: float32 [2048], P(('wide', 'narrow'))
- grad_w_proj: float32 [1024, 1024], P(('wide', 'narrow'))
- grad_b_proj: float32 [1024], P(('wide', 'narrow'))
- grad_w_fc1: float32 [1024, 4096], P(('wide', 'narrow'))
- grad_b_fc1: float32 [4096], P(('wide', 'narrow'))
- grad_w_fc2: float32 [4096, 1024], P(('wide', 'narrow'))
- grad_b_fc2: float32 [1024], P(('wide', 'narrow'))
Inputs may be any that keep to these rules, and one draw needn't show every extreme that they name: `lengths`: every entry is 0 (an empty place), 256 or 1024. In each half, the live places of one bucket hold at most 1024 tokens and at most 4 places; in each half some bucket holds exactly 1024 tokens in places of 1024, and another exactly 4 places.
All inputs are finite; a program needn't handle non-finite values.
Results may differ from a plain program's by a relative error of at most 0.012.
The roundings to bfloat16 on the way count: a program that leaves them out, or rounds other values in their place, can miss the bound.
Values may be sent and summed in bfloat16 or wider, within the bound.
No kernel may reach another device: no remote copies, remote signals or barrier semaphores. Data moves between devices by JAX's collectives and lax.ppermute only.
A program may use at most 320 MiB of HBM per device.

v0:
```python
import math

import jax
import jax.numpy as jnp
from jax import lax
from jax.sharding import PartitionSpec as P

HEADS = 16
HEAD_DIM = 64


EPS = 1e-06
HIGH = lax.Precision.HIGHEST
MASKED = -1000000000.0


def plan_tables(sample_len, sample_bucket, wide_count):
    units = sample_len // wide_count
    count_all = sample_len.shape[0]
    order_idx = jnp.arange(count_all, dtype=jnp.int32)
    earlier = (order_idx[:, None] < order_idx[None, :]) & (
        sample_bucket[:, None] == sample_bucket[None, :]
    )
    live_flag = (sample_len > 0).astype(jnp.int32)
    offset = jnp.cumsum(units) - units
    dest_off = jnp.sum(jnp.where(earlier, units[:, None], 0), axis=0)
    slot_num = jnp.sum(jnp.where(earlier, live_flag[:, None], 0), axis=0)
    return (units, offset, dest_off, slot_num, live_flag)


def row_tables(tables, sample_bucket, group_idx, row_count, wide_count):
    units, offset, dest_off, slot_num, live_flag = tables
    position = jnp.arange(row_count, dtype=jnp.int32)
    start_row = dest_off * wide_count
    member = (
        (sample_bucket[None, :] == group_idx)
        & (live_flag[None, :] > 0)
        & (position[:, None] >= start_row[None, :])
        & (position[:, None] < (start_row + units * wide_count)[None, :])
    )
    hit_int = member.astype(jnp.int32)
    row_valid = jnp.sum(hit_int, axis=1)
    row_slot = jnp.sum(hit_int * slot_num[None, :], axis=1)
    return (row_valid, row_slot)


def normalize(values):
    centre = values - jnp.mean(values, axis=1, keepdims=True)
    spread = jnp.mean(centre * centre, axis=1, keepdims=True)
    return centre * lax.rsqrt(spread + EPS)


def gelu_tanh(values):
    return jax.nn.gelu(values, approximate=True)


def contract_rows(left, right):
    return lax.dot_general(
        left, right, (((0,), (0,)), ((), ())), preferred_element_type=jnp.float32
    )


def times_transpose(left, weight):
    return lax.dot_general(
        left, weight, (((1,), (1,)), ((), ())), preferred_element_type=jnp.float32
    )


def tiling(tok_count):
    q_block = min(512, tok_count)
    head_group = math.gcd(HEADS, 4)
    return (q_block, head_group, tok_count // q_block, HEADS // head_group, head_group * HEAD_DIM)


def tiles_to_rows(stacked, block_count, group_count):
    q_block, span = (stacked.shape[1], stacked.shape[2])
    return (
        stacked.reshape(block_count, group_count, q_block, span)
        .transpose(0, 2, 1, 3)
        .reshape(block_count * q_block, group_count * span)
    )


def keys_to_rows(stacked, block_count, group_count):
    tok_count, span = (stacked.shape[1], stacked.shape[2])
    summed = jnp.sum(stacked.reshape(block_count, group_count, tok_count, span), axis=0)
    return summed.transpose(1, 0, 2).reshape(tok_count, group_count * span)


def tile_operands(
    queries, keys_low, values_low, segment, tile_idx, group_count, q_block, head_group, span
):
    tok_count = keys_low.shape[0]
    block_idx = tile_idx // group_count
    group_idx = tile_idx % group_count
    q_tile = lax.dynamic_slice(
        queries, (block_idx * q_block, group_idx * span), (q_block, span)
    ).reshape(q_block, head_group, HEAD_DIM)
    k_tile = lax.dynamic_slice(keys_low, (0, group_idx * span), (tok_count, span)).reshape(
        tok_count, head_group, HEAD_DIM
    )
    v_tile = lax.dynamic_slice(values_low, (0, group_idx * span), (tok_count, span)).reshape(
        tok_count, head_group, HEAD_DIM
    )
    seg_tile = lax.dynamic_slice_in_dim(segment, block_idx * q_block, q_block)
    scores = jnp.einsum("qhd,khd->hqk", q_tile, k_tile, preferred_element_type=jnp.float32) * (
        1.0 / math.sqrt(HEAD_DIM)
    )
    scores = jnp.where((seg_tile[:, None] == segment[None, :])[None], scores, MASKED)
    return (q_tile, k_tile, v_tile, scores, block_idx, group_idx)


def attend_forward(queries, keys_low, values_low, segment):
    tok_count = queries.shape[0]
    q_block, head_group, block_count, group_count, span = tiling(tok_count)

    def one_tile(tile_idx):
        q_tile, k_tile, v_tile, scores, block_idx, group_idx = tile_operands(
            queries, keys_low, values_low, segment, tile_idx, group_count, q_block, head_group, span
        )
        top = jnp.max(scores, axis=2, keepdims=True)
        expo = jnp.exp(scores - top)
        total = jnp.sum(expo, axis=2, keepdims=True)
        probs = (expo / total).astype(jnp.bfloat16)
        out_tile = jnp.einsum(
            "hqk,khd->qhd", probs, v_tile, preferred_element_type=jnp.float32
        ).reshape(q_block, span)
        return (out_tile, (top + jnp.log(total))[:, :, 0])

    stacked, log_sums = lax.map(one_tile, jnp.arange(block_count * group_count, dtype=jnp.int32))
    return (tiles_to_rows(stacked, block_count, group_count), log_sums)


def attend_backward(queries, keys_low, values_low, segment, log_sums, grad_att):
    tok_count = queries.shape[0]
    q_block, head_group, block_count, group_count, span = tiling(tok_count)
    scale = 1.0 / math.sqrt(HEAD_DIM)

    def one_tile(tile_idx):
        q_tile, k_tile, v_tile, scores, block_idx, group_idx = tile_operands(
            queries, keys_low, values_low, segment, tile_idx, group_count, q_block, head_group, span
        )
        do_tile = lax.dynamic_slice(
            grad_att, (block_idx * q_block, group_idx * span), (q_block, span)
        ).reshape(q_block, head_group, HEAD_DIM)
        probs = jnp.exp(scores - log_sums[tile_idx][:, :, None])
        grad_probs = jnp.einsum("qhd,khd->hqk", do_tile, v_tile, preferred_element_type=jnp.float32)
        inner = jnp.sum(probs * grad_probs, axis=2, keepdims=True)
        grad_scores = (probs * (grad_probs - inner)).astype(jnp.bfloat16)
        grad_q = (
            jnp.einsum("hqk,khd->qhd", grad_scores, k_tile, preferred_element_type=jnp.float32)
            * scale
        )
        grad_k = (
            jnp.einsum("hqk,qhd->khd", grad_scores, q_tile, preferred_element_type=jnp.float32)
            * scale
        )
        grad_v = jnp.einsum(
            "hqk,qhd->khd", probs.astype(jnp.bfloat16), do_tile, preferred_element_type=jnp.float32
        )
        return (
            grad_q.reshape(q_block, span),
            grad_k.reshape(tok_count, span),
            grad_v.reshape(tok_count, span),
        )

    grad_q, grad_k, grad_v = lax.map(
        one_tile, jnp.arange(block_count * group_count, dtype=jnp.int32)
    )
    return (
        tiles_to_rows(grad_q, block_count, group_count),
        keys_to_rows(grad_k, block_count, group_count),
        keys_to_rows(grad_v, block_count, group_count),
    )


def local(
    x_src,
    cond,
    lengths,
    bucket,
    w_mod,
    b_mod,
    w_qkv,
    b_qv,
    w_proj,
    b_proj,
    w_fc1,
    b_fc1,
    w_fc2,
    b_fc2,
    grad_out,
):
    wide_count = lax.axis_size("wide")
    half_count = lax.axis_size("narrow")
    group_idx = lax.axis_index("wide")
    half_idx = lax.axis_index("narrow")
    tok_rows, feat_dim = x_src.shape
    sample_count = lengths.shape[0] // half_count
    slot_count = sample_count // wide_count
    cap_rows = tok_rows // wide_count
    sample_len = lax.dynamic_slice_in_dim(lengths, half_idx * sample_count, sample_count)
    sample_bucket = lax.dynamic_slice_in_dim(bucket, half_idx * sample_count, sample_count)
    tables = plan_tables(sample_len, sample_bucket, wide_count)
    units, offset, dest_off, slot_num, live_flag = tables
    cell_idx = jnp.arange(cap_rows, dtype=jnp.int32)[:, None, None]
    target = jnp.arange(wide_count, dtype=jnp.int32)[None, :, None]
    to_target = (sample_bucket[None, None, :] == target) & (live_flag[None, None, :] > 0)
    send_hit = (
        to_target
        & (cell_idx >= dest_off[None, None, :])
        & (cell_idx < (dest_off + units)[None, None, :])
    ).astype(jnp.int32)
    send_valid = jnp.sum(send_hit, axis=2)
    send_source = jnp.sum(send_hit * (offset - dest_off)[None, None, :], axis=2) + cell_idx[:, :, 0]
    send_source = jnp.where(send_valid > 0, send_source, 0)
    picked = jnp.take(x_src, send_source.reshape(-1), axis=0).reshape(
        cap_rows, wide_count, feat_dim
    )
    send_rows = jnp.where(send_valid[:, :, None] > 0, picked, jnp.zeros((), jnp.bfloat16))
    slot_ids = jnp.arange(slot_count, dtype=jnp.int32)[:, None, None]
    cond_hit = (to_target & (slot_num[None, None, :] == slot_ids)).astype(jnp.bfloat16)
    send_cond = jnp.einsum(
        "qws,sf->qwf", cond_hit, cond, preferred_element_type=jnp.float32
    ).astype(jnp.bfloat16)
    recv_rows, recv_cond = (
        lax.all_to_all(send_rows, "wide", split_axis=1, concat_axis=1, tiled=True),
        lax.all_to_all(send_cond, "wide", split_axis=1, concat_axis=1, tiled=True),
    )
    rows_in = recv_rows.reshape(tok_rows, feat_dim)
    cond_in = recv_cond.reshape(slot_count, feat_dim)
    row_valid, row_slot = row_tables(tables, sample_bucket, group_idx, tok_rows, wide_count)
    select = (
        (row_slot[:, None] == jnp.arange(slot_count, dtype=jnp.int32)[None, :])
        & (row_valid[:, None] > 0)
    ).astype(jnp.float32)
    segment = jnp.where(row_valid > 0, row_slot, -1)
    x_val = rows_in.astype(jnp.float32)
    act_cond, silu_back = jax.vjp(jax.nn.silu, cond_in.astype(jnp.float32))
    act_low = act_cond.astype(jnp.bfloat16)
    modulate = jnp.dot(act_low, w_mod, preferred_element_type=jnp.float32) + b_mod.astype(
        jnp.float32
    )
    per_row = jnp.dot(select, modulate, precision=HIGH)
    shift_one, scale_one, gate_one, shift_two, scale_two, gate_two = jnp.split(per_row, 6, axis=1)
    norm_one, norm_back_one = jax.vjp(normalize, x_val)
    attn_in = (norm_one * (1.0 + scale_one) + shift_one).astype(jnp.bfloat16)
    bias_full = jnp.concatenate(
        [
            b_qv[:feat_dim].astype(jnp.float32),
            jnp.zeros((feat_dim,), jnp.float32),
            b_qv[feat_dim:].astype(jnp.float32),
        ]
    )
    mixed_low = (jnp.dot(attn_in, w_qkv, preferred_element_type=jnp.float32) + bias_full).astype(
        jnp.bfloat16
    )
    queries = mixed_low[:, :feat_dim]
    keys_low = mixed_low[:, feat_dim : 2 * feat_dim]
    values_low = mixed_low[:, 2 * feat_dim :]
    attended, log_sums = attend_forward(queries, keys_low, values_low, segment)
    attended_low = attended.astype(jnp.bfloat16)
    branch_one = jnp.dot(attended_low, w_proj, preferred_element_type=jnp.float32) + b_proj.astype(
        jnp.float32
    )
    resid_one = x_val + gate_one * branch_one
    norm_two, norm_back_two = jax.vjp(normalize, resid_one)
    mlp_in = (norm_two * (1.0 + scale_two) + shift_two).astype(jnp.bfloat16)
    hidden_pre = jnp.dot(mlp_in, w_fc1, preferred_element_type=jnp.float32) + b_fc1.astype(
        jnp.float32
    )
    hidden_act, gelu_back = jax.vjp(gelu_tanh, hidden_pre)
    hidden_low = hidden_act.astype(jnp.bfloat16)
    branch_two = jnp.dot(hidden_low, w_fc2, preferred_element_type=jnp.float32) + b_fc2.astype(
        jnp.float32
    )
    y_dest = (resid_one + gate_two * branch_two).astype(jnp.bfloat16)
    grad_y = grad_out.astype(jnp.float32)
    grad_branch_two = (grad_y * gate_two).astype(jnp.bfloat16)
    grad_gate_two = grad_y * branch_two
    d_fc2 = contract_rows(hidden_low, grad_branch_two)
    d_bfc2 = jnp.sum(grad_branch_two.astype(jnp.float32), axis=0)
    grad_pre = gelu_back(times_transpose(grad_branch_two, w_fc2))[0].astype(jnp.bfloat16)
    d_fc1 = contract_rows(mlp_in, grad_pre)
    d_bfc1 = jnp.sum(grad_pre.astype(jnp.float32), axis=0)
    grad_mlp_in = times_transpose(grad_pre, w_fc1)
    grad_resid = grad_y + norm_back_two(grad_mlp_in * (1.0 + scale_two))[0]
    grad_branch_one = (grad_resid * gate_one).astype(jnp.bfloat16)
    grad_gate_one = grad_resid * branch_one
    d_proj = contract_rows(attended_low, grad_branch_one)
    d_bproj = jnp.sum(grad_branch_one.astype(jnp.float32), axis=0)
    grad_att = times_transpose(grad_branch_one, w_proj).astype(jnp.bfloat16)
    grad_q, grad_k, grad_v = attend_backward(
        queries, keys_low, values_low, segment, log_sums, grad_att
    )
    grad_mixed = jnp.concatenate([grad_q, grad_k, grad_v], axis=1).astype(jnp.bfloat16)
    d_qkv = contract_rows(attn_in, grad_mixed)
    bias_sums = jnp.sum(grad_mixed.astype(jnp.float32), axis=0)
    d_bqv = jnp.concatenate([bias_sums[:feat_dim], bias_sums[2 * feat_dim :]])
    grad_attn_in = times_transpose(grad_mixed, w_qkv)
    grad_rows = (grad_resid + norm_back_one(grad_attn_in * (1.0 + scale_one))[0]).astype(
        jnp.bfloat16
    )
    grad_per_row = jnp.concatenate(
        [
            grad_attn_in,
            grad_attn_in * norm_one,
            grad_gate_one,
            grad_mlp_in,
            grad_mlp_in * norm_two,
            grad_gate_two,
        ],
        axis=1,
    )
    grad_mod = jnp.dot(select.T, grad_per_row, precision=HIGH).astype(jnp.bfloat16)
    d_mod = contract_rows(act_low, grad_mod)
    d_bmod = jnp.sum(grad_mod.astype(jnp.float32), axis=0)
    grad_cond = silu_back(times_transpose(grad_mod, w_mod))[0].astype(jnp.bfloat16)
    back_rows = grad_rows.reshape(cap_rows, wide_count, feat_dim)
    back_cond = grad_cond.reshape(slot_count, wide_count, feat_dim // wide_count)
    returned_rows, returned_cond = (
        lax.all_to_all(back_rows, "wide", split_axis=1, concat_axis=1, tiled=True),
        lax.all_to_all(back_cond, "wide", split_axis=1, concat_axis=1, tiled=True),
    )
    src_pos = jnp.arange(tok_rows, dtype=jnp.int32)[:, None]
    back_hit = (
        (live_flag[None, :] > 0)
        & (src_pos >= offset[None, :])
        & (src_pos < (offset + units)[None, :])
    ).astype(jnp.int32)
    back_valid = jnp.sum(back_hit, axis=1)
    back_index = (
        jnp.sum(back_hit * ((dest_off - offset) * wide_count + sample_bucket)[None, :], axis=1)
        + src_pos[:, 0] * wide_count
    )
    back_index = jnp.where(back_valid > 0, back_index, 0)
    flat_rows = returned_rows.reshape(cap_rows * wide_count, feat_dim)
    dx_src = jnp.where(
        back_valid[:, None] > 0,
        jnp.take(flat_rows, back_index, axis=0),
        jnp.zeros((), jnp.bfloat16),
    )
    flat_cond = returned_cond.reshape(slot_count * wide_count, feat_dim // wide_count)
    cond_index = jnp.where(live_flag > 0, slot_num * wide_count + sample_bucket, 0)
    dcond = jnp.where(
        live_flag[:, None] > 0, jnp.take(flat_cond, cond_index, axis=0), jnp.zeros((), jnp.bfloat16)
    )
    s_mod, s_bmod, s_qkv, s_bqv, s_proj, s_bproj, s_fc1, s_bfc1, s_fc2, s_bfc2 = (
        lax.psum_scatter(d_mod, ("wide", "narrow"), scatter_dimension=0, tiled=True),
        lax.psum_scatter(d_bmod, ("wide", "narrow"), scatter_dimension=0, tiled=True),
        lax.psum_scatter(d_qkv, ("wide", "narrow"), scatter_dimension=0, tiled=True),
        lax.psum_scatter(d_bqv, ("wide", "narrow"), scatter_dimension=0, tiled=True),
        lax.psum_scatter(d_proj, ("wide", "narrow"), scatter_dimension=0, tiled=True),
        lax.psum_scatter(d_bproj, ("wide", "narrow"), scatter_dimension=0, tiled=True),
        lax.psum_scatter(d_fc1, ("wide", "narrow"), scatter_dimension=0, tiled=True),
        lax.psum_scatter(d_bfc1, ("wide", "narrow"), scatter_dimension=0, tiled=True),
        lax.psum_scatter(d_fc2, ("wide", "narrow"), scatter_dimension=0, tiled=True),
        lax.psum_scatter(d_bfc2, ("wide", "narrow"), scatter_dimension=0, tiled=True),
    )
    return (
        y_dest,
        dx_src,
        dcond,
        s_mod,
        s_bmod,
        s_qkv,
        s_bqv,
        s_proj,
        s_bproj,
        s_fc1,
        s_bfc1,
        s_fc2,
        s_bfc2,
    )


def solution(mesh):
    placed = (
        P("narrow", "wide"),
        P("narrow", "wide"),
        P(),
        P(),
        P(),
        P(),
        P(),
        P(),
        P(),
        P(),
        P(),
        P(),
        P(),
        P(),
        P(("wide", "narrow"), None),
    )
    return jax.shard_map(
        local,
        mesh=mesh,
        in_specs=placed,
        out_specs=(
            P(("wide", "narrow"), None),
            P("narrow", "wide"),
            P("narrow", "wide"),
            P(("wide", "narrow"), None),
            P(("wide", "narrow")),
            P(("wide", "narrow"), None),
            P(("wide", "narrow")),
            P(("wide", "narrow"), None),
            P(("wide", "narrow")),
            P(("wide", "narrow"), None),
            P(("wide", "narrow")),
            P(("wide", "narrow"), None),
            P(("wide", "narrow")),
        ),
        check_vma=False,
    )
```

profile of v0, /device:TPU:0, one launch (start us, length us, event | category | flops | bytes accessed | tf_op | source)
XLA Modules:
  0.0 1402.7 jit_solution(15417652348541866081)
XLA Ops:
  11.1 8.3 all-to-all-start.1
  23.7 7.9 gather_fusion.1
  53.2 13.5 fusion.26
  66.7 20.3 %all-to-all-done = bf16[64,16,1024]{2,0,1:T(8,128)(2,1)} async-done(((bf16[64,16,1024]{2,0,1:T(8,128)(2,1)}), bf16[64,16,1024]{2,0,1:T(8,128)(2,1)}, u32[]{:S(2)}, u32[]{:S(2)}) %all-to-all-start) | async-done | bytes 2097184 | tf_op jit(solution)/shard_map/all_to_all | solution.py:227
  126.4 109.3 %while.30 = (s32[]{:T(128)}, bf16[8,512,256]{1,2,0:T(8,128)(2,1)}, f32[8,4,512]{2,1,0:T(4,128)S(1)}, s32[8]{0:T(128)S(1)}, bf16[1024,1024]{0,1:T(8,128)(2,1)}, /...) while((s32[]{:T(128)}, bf16[8,512,256]{1,2,0:T(8,128)(2,1)}, ...), condition=%wide.region_12.14_spmd, body=%wide.region_9.13_spmd.sunk | while | flops 562558976 | bytes 32057820 | solution.py:130
  252.7 7.5 convert_reduce_fusion.2
  260.3 11.9 fusion.60
  272.2 28.9 %convert_reduce_fusion = (f32[4096]{0:T(1024)}, bf16[1024,4096]{1,0:T(8,128)(2,1)}, bf16[1024,4096]{1,0:T(8,128)(2,1)}) fusion(f32[1024,4096]{1,0:T(8,128)} %fusion.60, f32[4096]{0:T(1024)S(1)} %copy-done.46, bf16[1024,1024]{1,0:T(8,128)(2,1)} %get-tuple-element.432, bf16[4096,1024]{1,0:T(8,128)(2,1)} %param.33), kind=kOutput, calls=%fused_computation.42 | convolution fusion | flops 8694788096 | bytes 44072960 | tf_op jit(solution)/shard_map/dot_general | solution.py:64
  301.1 17.6 %multiply_reduce_fusion.2 = (f32[1024]{0:T(1024)S(1)}, f32[1024,1024]{1,0:T(8,128)}) fusion(f32[1024,1024]{1,0:T(8,128)} %copy-done.2, f32[1024]{0:T(1024)S(1)} %broadcast_multiply_fusion.1, f32[1024,6144]{1,0:T(8,128)} %fusion.26, bf16[1024,4096]{1,0:T(8,128)(2,1)} %get-tuple-element.434, bf16[1024,4096]{1,0:T(8,128)(2,1)} %param.31), kind=kOutput, calls=%fused_computation.72 | convolution fusion | flops 8595176448 | bytes 29368320 | tf_op jit(solution)/shard_map/dot_general | solution.py:64
  318.8 19.5 %fusion.54 = (f32[1024]{0:T(1024)S(1)}, f32[1024,1024]{1,0:T(8,128)}, bf16[1024,1024]{1,0:T(8,128)(2,1)}, f32[1024,1024]{1,0:T(8,128)}) fusion(f32[1024]{0:T(1024)S(1)} %multiply_multiply_fusion.3, f32[1024,1024]{1,0:T(8,128)S(1)} %copy-done.3, f32[1024]{0:T(1024)S(1)} %broadcast_multiply_fusion.1, f32[1024]{0:T(1024)S(1)} %fusion.45, ...), kind=kOutput, calls=%fused_computation.171 | convolution fusion | flops 8602516480 | bytes 44060672 | tf_op jit(solution)/shard_map/dot_general | solution.py:274
  356.6 184.9 %while.31 = (s32[]{:T(128)}, bf16[8,512,256]{1,2,0:T(8,128)(2,1)}, f32[8,1024,256]{1,2,0:T(8,128)}, f32[8,1024,256]{1,2,0:T(8,128)}, s32[8]{0:T(128)S(1)}, /*ind...) while((s32[]{:T(128)}, bf16[8,512,256]{1,2,0:T(8,128)(2,1)}, ...), condition=%wide.region_20.22_spmd, body=%wide.region_18.21_spmd.sunk | while | flops 1374681088 | bytes 78449184 | solution.py:167
  569.3 12.1 fusion.49
  581.5 16.2 %fusion.62 = f32[1024,4096]{1,0:T(8,128)} fusion(bf16[1024,1024]{1,0:T(8,128)(2,1)} %copy-done.19, bf16[1024,4096]{1,0:T(8,128)(2,1)} %get-tuple-element.434), kind=kOutput, calls=%fused_computation.181 | convolution fusion | flops 8589934592 | bytes 27262976 | tf_op jit(solution)/shard_map/dot_general | solution.py:58
  597.8 16.7 %fusion.63 = f32[4096,1024]{1,0:T(8,128)} fusion(bf16[1024,4096]{1,0:T(8,128)(2,1)} %get-tuple-element.470, bf16[1024,1024]{1,0:T(8,128)(2,1)} %get-tuple-element.432), kind=kOutput, calls=%fused_computation.182 | convolution fusion | flops 8589934592 | bytes 27262976 | tf_op jit(solution)/shard_map/dot_general | solution.py:58
  614.7 12.6 constant_dynamic-update-slice_fusion.5
  651.3 12.9 convert_reduce_fusion.8
  664.2 10.7 fusion.48
  675.0 8.1 fusion.40
  683.9 10.0 all-to-all-start.3
  709.3 83.8 %all-reduce.5 = (f32[6144]{0:T(1024)S(1)}, f32[2048]{0:T(1024)S(1)}, f32[1024]{0:T(1024)S(1)}, f32[4096]{0:T(1024)S(1)}, f32[1024]{0:T(1024)S(1)}) all-reduce(f32[6144]{0:T(1024)S(1)} %get-tuple-element.493, f32[2048]{0:T(1024)S(1)} %pad_maximum_fusion.2, ...), channel_id=3, replica_groups=mesh['wide'=16,'narrow'=2] {'wide','narrow'}, use_global_device_ids=true, to_apply=%region_28.30.clone | all-reduce | flops 14336 | bytes 114688
  801.6 8.1 gather_fusion.2
  812.8 140.5 %reduce-scatter.12.cloned.1.call-done = f32[32,4096]{1,0:T(8,128)} async-done(((f32[1024,4096]{1,0:T(8,128)}), f32[32,4096]{1,0:T(8,128)}) %reduce-scatter.12.cloned.1.call-update) | async-done | bytes 524304 | tf_op jit(solution)/shard_map/reduce_scatter | solution.py:355
  953.3 187.5 %reduce-scatter.14.cloned.1.call-done = f32[128,1024]{1,0:T(8,128)} async-done(((f32[4096,1024]{1,0:T(8,128)}), f32[128,1024]{1,0:T(8,128)}) %reduce-scatter.14.cloned.1.call-update) | async-done | bytes 524304 | tf_op jit(solution)/shard_map/reduce_scatter | solution.py:357
  1140.7 255.0 %reduce-scatter.6.cloned.1.call-done = f32[32,6144]{1,0:T(8,128)} async-done(((f32[1024,6144]{1,0:T(8,128)}), f32[32,6144]{1,0:T(8,128)}) %reduce-scatter.6.cloned.1.call-update) | async-done | bytes 786448 | tf_op jit(solution)/shard_map/reduce_scatter | solution.py:349
  (461 shorter events, 424.1 us)
Async XLA Ops:
  7.2 235.0 %copy-start = (bf16[1024,1024]{1,0:T(8,128)(2,1)S(1)}, bf16[1024,1024]{1,0:T(8,128)(2,1)}, u32[]{:S(2)}) copy-start(bf16[1024,1024]{1,0:T(8,128)(2,1)} %param.29) | copy-start | bytes 6291460
  9.5 36.3 %copy-start.48 = (pred[64]{0:T(512)(128)(4,1)}, pred[64]{0:T(512)(128)(4,1)S(1)}, u32[]{:S(2)}) copy-start(pred[64]{0:T(512)(128)(4,1)S(1)} %get-tuple-element.484) | copy-start | bytes 196
  11.1 26.2 %all-to-all-start.1 = ((bf16[16,2,128]{2,1,0:T(2,128)(2,1)}), bf16[16,2,128]{2,1,0:T(2,128)(2,1)S(1)}, u32[]{:S(2)}, u32[]{:S(2)}) async-start(bf16[16,2,128]{2,1,0:T(2,128)(2,1)} %reshape.510), calls=%async_computation.1 | async-start | bytes 16384 | tf_op jit(solution)/shard_map/all_to_all | solution.py:228
  37.3 49.8 %all-to-all-start = ((bf16[64,16,1024]{2,0,1:T(8,128)(2,1)}), bf16[64,16,1024]{2,0,1:T(8,128)(2,1)}, u32[]{:S(2)}, u32[]{:S(2)}) async-start(bf16[64,16,1024]{2,0,1:T(8,128)(2,1)} %copy_select_fusion), calls=%async_computation | async-start | bytes 4194304 | tf_op jit(solution)/shard_map/all_to_all | solution.py:227
  44.2 768.6 %reduce-scatter.10.cloned.1.call-start = ((), (), s32[]{:S(2)}) async-start(), calls=%async_computation.11 | async-start | bytes 4325376 | tf_op jit(solution)/shard_map/reduce_scatter | solution.py:353
  44.6 197.6 %copy-start.36 = (f32[1024]{0:T(1024)}, f32[1024]{0:T(1024)S(1)}, u32[]{:S(2)}) copy-start(f32[1024]{0:T(1024)S(1)} %convert_element_type.158) | copy-start | bytes 12292
  242.7 17.5 %slice-start = ((s8[8388608]{0:T(1024)(128)(4,1)}), s8[4194304]{0:T(1024)(128)(4,1)S(1)}, s32[]{:S(2)}) async-start(s8[8388608]{0:T(1024)(128)(4,1)} %bitcast.194), calls=%async_computation.14 | async-start | bytes 8388608
  249.6 69.2 %copy-start.27 = (f32[1024]{0:T(1024)}, f32[1024]{0:T(1024)S(1)}, u32[]{:S(2)}) copy-start(f32[1024]{0:T(1024)S(1)} %broadcast_multiply_fusion.1) | copy-start | bytes 12292
  252.7 66.1 %copy-start.31 = (f32[1024]{0:T(1024)}, f32[1024]{0:T(1024)S(1)}, u32[]{:S(2)}) copy-start(f32[1024]{0:T(1024)S(1)} %fusion.45) | copy-start | bytes 12292
  301.1 17.7 %copy-start.3 = (f32[1024,1024]{1,0:T(8,128)S(1)}, f32[1024,1024]{1,0:T(8,128)}, u32[]{:S(2)}) copy-start(f32[1024,1024]{1,0:T(8,128)} %copy-done.2) | copy-start | bytes 12582916
  301.1 17.7 %copy-start.42 = (f32[1024]{0:T(1024)S(1)}, f32[1024]{0:T(1024)}, u32[]{:S(2)}) copy-start(f32[1024]{0:T(1024)} %convert_element_type.162) | copy-start | bytes 12292
  355.0 457.8 %reduce-scatter.8.cloned.1.call-start = ((), (), s32[]{:S(2)}) async-start(), calls=%async_computation.10 | async-start | bytes 12976128 | tf_op jit(solution)/shard_map/reduce_scatter | solution.py:351
  550.7 64.0 %copy-start.15 = (bf16[1024,1024]{1,0:T(8,128)(2,1)}, bf16[1024,1024]{1,0:T(8,128)(2,1)S(1)}, u32[]{:S(2)}) copy-start(bf16[1024,1024]{1,0:T(8,128)(2,1)S(1)} %copy.138) | copy-start | bytes 6291460
  581.5 371.8 %reduce-scatter.12.cloned.1.call-start = ((), (), s32[]{:S(2)}) async-start(), calls=%async_computation.12 | async-start | bytes 17301504 | tf_op jit(solution)/shard_map/reduce_scatter | solution.py:355
  597.8 542.9 %reduce-scatter.14.cloned.1.call-start = ((), (), s32[]{:S(2)}) async-start(), calls=%async_computation.13 | async-start | bytes 17301504 | tf_op jit(solution)/shard_map/reduce_scatter | solution.py:357
  614.6 12.7 copy-start.30
  614.6 781.1 %reduce-scatter.6.cloned.1.call-start = ((), (), s32[]{:S(2)}) async-start(), calls=%async_computation.9 | async-start | bytes 25952256 | tf_op jit(solution)/shard_map/reduce_scatter | solution.py:349
  614.6 12.6 copy-start.7
  651.3 12.9 copy-start.24
  683.9 17.3 %all-to-all-start.3 = ((bf16[16,2,128]{2,1,0:T(2,128)(2,1)}), bf16[16,2,128]{2,1,0:T(2,128)(2,1)S(1)}, u32[]{:S(2)}, u32[]{:S(2)}) async-start(bf16[16,2,128]{2,1,0:T(2,128)(2,1)} %reshape.512), calls=%async_computation.3 | async-start | bytes 16384 | tf_op jit(solution)/shard_map/all_to_all | solution.py:323
  701.2 96.3 %all-to-all-start.2 = ((bf16[64,16,1024]{2,0,1:T(8,128)(2,1)}), bf16[64,16,1024]{2,0,1:T(8,128)(2,1)}, u32[]{:S(2)}, u32[]{:S(2)}) async-start(bf16[64,16,1024]{2,0,1:T(8,128)(2,1)} %copy.139), calls=%async_computation.2 | async-start | bytes 4194304 | tf_op jit(solution)/shard_map/all_to_all | solution.py:322
  705.7 91.1 %copy-start.49 = (pred[64]{0:T(512)(128)(4,1)S(1)}, pred[64]{0:T(512)(128)(4,1)}, u32[]{:S(2)}) copy-start(pred[64]{0:T(512)(128)(4,1)} %copy-done.48) | copy-start | bytes 196
  705.7 91.1 %copy-start.52 = (pred[64]{0:T(512)(128)(4,1)S(1)}, pred[64]{0:T(512)(128)(4,1)}, u32[]{:S(2)}) copy-start(pred[64]{0:T(512)(128)(4,1)} %get-tuple-element.437) | copy-start | bytes 196
  801.6 594.1 %copy-start.1 = (bf16[1024,1024]{1,0:T(8,128)(2,1)S(1)}, bf16[1024,1024]{1,0:T(8,128)(2,1)}, u32[]{:S(2)}) copy-start(bf16[1024,1024]{1,0:T(8,128)(2,1)} %param.29) | copy-start | bytes 6291460
  (45 other events, 313.3 us)
Sparse Core Ops, SparseCore 0:
  355.1 144.8 reduce-scatter.9
  581.6 186.0 reduce-scatter.7
  770.7 182.5 reduce-scatter.11
  956.1 184.5 reduce-scatter.13
  1148.7 246.9 reduce-scatter.5
where the time goes:
time: 1410 us; the launch traced here: 1400 us
  waiting for transfers between devices  606 us (43%)
  matrix products  322 us (23%)
  local copies, waits for them, and re-layouts  172 us (12%)
  other arithmetic  120 us (9%)
  blocking collectives  83.8 us (6%)
  loops' own time  53.8 us (4%)
  starting transfers between devices  30.1 us (2%)
  between operations  15.1 us (1%)
    reduce_scatter x1, waiting for transfers between devices, local(): lax.psum_scatter(d_mod, ('wide', 'narrow'), scatter_dimension=0, tiled=True)  255 us
    reduce_scatter x1, waiting for transfers between devices, local(): lax.psum_scatter(d_fc2, ('wide', 'narrow'), scatter_dimension=0, tiled=True)  187 us
    reduce_scatter x1, waiting for transfers between devices, local(): lax.psum_scatter(d_fc1, ('wide', 'narrow'), scatter_dimension=0, tiled=True)  140 us
    unnamed x1, blocking collectives  83.8 us
    dot_general x5, matrix products, times_transpose(): lax.dot_general(left, weight, (((1,), (1,)), ((), ())), preferred_element...  72.6 us
    dot_general x5, matrix products, contract_rows(): lax.dot_general(left, right, (((0,), (0,)), ((), ())), preferred_element_...  60.2 us
    another operation x1, loops' own time, attend_backward(): lax.map(one_tile, jnp.arange(block_count * group_count, dtype=jnp.int32))  32.2 us
  transfers between devices with their start and end apart: 9, of which 5 were waited for; matrix products, arithmetic and copies ran while one was open for 26% of the time, Pallas kernels for 0%

commit v1 on v0

v1 whole, which is shorter than its diff:
```python
import functools
import math

import jax
import jax.numpy as jnp
from jax import lax
from jax.experimental import pallas as pl
from jax.experimental.pallas import tpu as pltpu
from jax.sharding import PartitionSpec as P

HEADS = 16
HEAD_DIM = 64
EPS = 1e-06
MASKED = -1000000000.0
LOG2E = 1.4426950408889634
BLK = 256
TILE = 16
VMEM_LIMIT = 58 * 2**20
BF16 = jnp.bfloat16
F32 = jnp.float32


def params(**more):
    return pltpu.CompilerParams(vmem_limit_bytes=VMEM_LIMIT, **more)


def dot(left, right, left_dim, right_dim):
    return lax.dot_general(
        left, right, (((left_dim,), (right_dim,)), ((), ())), preferred_element_type=F32
    )


def norm_parts(values):
    centre = values - jnp.mean(values, axis=1, keepdims=True)
    spread = jnp.mean(centre * centre, axis=1, keepdims=True)
    inverse = lax.rsqrt(spread + EPS)
    return centre * inverse, inverse


def norm_back(grad, normed, inverse):
    return (
        grad
        - jnp.mean(grad, axis=1, keepdims=True)
        - normed * jnp.mean(grad * normed, axis=1, keepdims=True)
    ) * inverse


def regroup_kernel(
    len_ref, buck_ref, me_ref, x_ref, cond_ref,
    send_ref, scond_ref, seg_ref, src_ref, cidx_ref,
    off_ref, slot_ref, cond_in, cond_out, *, wide, slots,
):
    places = len_ref.shape[0]
    cells = send_ref.shape[1]
    send_ref[...] = jnp.zeros_like(send_ref)
    cond_out[...] = jnp.zeros_like(cond_out)
    cond_in[...] = cond_ref[...].astype(F32)
    for i in range(wide):
        off_ref[i] = 0
        slot_ref[i] = 0
    for i in range(seg_ref.shape[0]):
        seg_ref[i] = -1

    @pl.loop(0, src_ref.shape[0])
    def _(i):
        src_ref[i] = -1

    def place(j, offset):
        units = len_ref[j] // wide
        b = buck_ref[j]
        cidx_ref[j] = -1

        @pl.when(units > 0)
        def _():
            start = off_ref[b]
            slot = slot_ref[b]
            off_ref[b] = start + units
            slot_ref[b] = slot + 1
            cidx_ref[j] = b * slots + slot
            cond_out[pl.ds(b * slots + slot, 1), :] = cond_in[pl.ds(j, 1), :]

            @pl.loop(0, units // TILE)
            def _(t):
                a = pl.multiple_of(offset + t * TILE, TILE)
                c = pl.multiple_of(start + t * TILE, TILE)
                send_ref[b, pl.ds(c, TILE), :] = x_ref[pl.ds(a, TILE), :]
                src_ref[a // TILE] = (b * cells + c) // TILE

            @pl.when(b == me_ref[0])
            def _():
                @pl.loop(0, units * wide // BLK)
                def _(t):
                    seg_ref[start * wide // BLK + t] = slot

        return offset + units

    lax.fori_loop(0, places, place, 0)
    scond_ref[...] = cond_out[...].astype(BF16)


def regroup(x_src, cond, lens, buck, me, wide):
    rows, feat = x_src.shape
    places, part = cond.shape
    slots = places // wide
    smem = pl.BlockSpec(memory_space=pltpu.SMEM)
    vmem = pl.BlockSpec(memory_space=pltpu.VMEM)
    return pl.pallas_call(
        functools.partial(regroup_kernel, wide=wide, slots=slots),
        in_specs=[smem, smem, smem, vmem, vmem],
        out_specs=[vmem, vmem, smem, smem, smem],
        out_shape=[
            jax.ShapeDtypeStruct((wide, rows // wide, feat), BF16),
            jax.ShapeDtypeStruct((places, part), BF16),
            jax.ShapeDtypeStruct((rows // BLK,), jnp.int32),
            jax.ShapeDtypeStruct((rows // TILE,), jnp.int32),
            jax.ShapeDtypeStruct((places,), jnp.int32),
        ],
        scratch_shapes=[
            pltpu.SMEM((wide,), jnp.int32),
            pltpu.SMEM((wide,), jnp.int32),
            pltpu.VMEM((places, part), F32),
            pltpu.VMEM((places, part), F32),
        ],
        compiler_params=params(),
    )(lens, buck, me, x_src, cond)


def restore_kernel(src_ref, cidx_ref, back_ref, bcond_ref, dx_ref, dcond_ref, cond_in, cond_out):
    cond_in[...] = bcond_ref[...].astype(F32)

    @pl.loop(0, src_ref.shape[0])
    def _(i):
        at = src_ref[i]
        rows = back_ref[pl.ds(pl.multiple_of(jnp.maximum(at, 0) * TILE, TILE), TILE), :]
        dx_ref[pl.ds(pl.multiple_of(i * TILE, TILE), TILE), :] = jnp.where(
            at >= 0, rows, jnp.zeros_like(rows)
        )

    @pl.loop(0, cidx_ref.shape[0])
    def _(j):
        at = cidx_ref[j]
        row = cond_in[pl.ds(jnp.maximum(at, 0), 1), :]
        cond_out[pl.ds(j, 1), :] = jnp.where(at >= 0, row, 0.0)

    dcond_ref[...] = cond_out[...].astype(BF16)


def restore(src, cidx, back, bcond):
    smem = pl.BlockSpec(memory_space=pltpu.SMEM)
    vmem = pl.BlockSpec(memory_space=pltpu.VMEM)
    return pl.pallas_call(
        restore_kernel,
        in_specs=[smem, smem, vmem, vmem],
        out_specs=[vmem, vmem],
        out_shape=[
            jax.ShapeDtypeStruct(back.shape, BF16),
            jax.ShapeDtypeStruct(bcond.shape, BF16),
        ],
        scratch_shapes=[pltpu.VMEM(bcond.shape, F32), pltpu.VMEM(bcond.shape, F32)],
        compiler_params=params(),
    )(src, cidx, back, bcond)


def regroup_any(x_src, cond, lens, buck, me, wide):
    rows, feat = x_src.shape
    places = lens.shape[0]
    slots, cells = places // wide, rows // wide
    units = lens // wide
    order = jnp.arange(places, dtype=jnp.int32)
    earlier = (order[:, None] < order[None, :]) & (buck[:, None] == buck[None, :])
    live = (lens > 0).astype(jnp.int32)
    offset = jnp.cumsum(units) - units
    start = jnp.sum(jnp.where(earlier, units[:, None], 0), axis=0)
    slot = jnp.sum(jnp.where(earlier, live[:, None], 0), axis=0)
    cell = jnp.arange(cells, dtype=jnp.int32)[None, :, None]
    to_target = (buck[None, :] == jnp.arange(wide, dtype=jnp.int32)[:, None]) & (live[None, :] > 0)
    hit = (
        to_target[:, None, :]
        & (cell >= start[None, None, :])
        & (cell < (start + units)[None, None, :])
    ).astype(jnp.int32)
    valid = jnp.sum(hit, axis=2)
    source = jnp.sum(hit * (offset - start)[None, None, :], axis=2) + cell[:, :, 0]
    source = jnp.where(valid > 0, source, 0)
    picked = jnp.take(x_src, source.reshape(-1), axis=0).reshape(wide, cells, feat)
    send = jnp.where(valid[:, :, None] > 0, picked, jnp.zeros((), BF16))
    cond_hit = to_target[:, None, :] & (
        slot[None, None, :] == jnp.arange(slots, dtype=jnp.int32)[None, :, None]
    )
    scond = jnp.einsum("wqs,sf->wqf", cond_hit.astype(BF16), cond, preferred_element_type=F32)
    scond = scond.astype(BF16).reshape(cond.shape)
    first = jnp.arange(rows // BLK, dtype=jnp.int32)[:, None] * BLK
    mine = (
        ((buck == me[0]) & (live > 0))[None, :]
        & (first >= (start * wide)[None, :])
        & (first < ((start + units) * wide)[None, :])
    )
    seg = jnp.sum(jnp.where(mine, slot[None, :] + 1, 0), axis=1) - 1
    spot = jnp.arange(rows, dtype=jnp.int32)[:, None]
    inside = (live[None, :] > 0) & (spot >= offset[None, :]) & (spot < (offset + units)[None, :])
    src = jnp.sum(jnp.where(inside, (buck * cells + start - offset)[None, :] + spot + 1, 0), axis=1)
    cidx = jnp.where(live > 0, buck * slots + slot, -1)
    return send, scond, seg.astype(jnp.int32), src - 1, cidx


def restore_any(src, cidx, back, bcond):
    dx = jnp.take(back, jnp.maximum(src, 0), axis=0)
    dcond = jnp.take(bcond, jnp.maximum(cidx, 0), axis=0)
    zero = jnp.zeros((), BF16)
    return jnp.where(src[:, None] >= 0, dx, zero), jnp.where(cidx[:, None] >= 0, dcond, zero)


def qkv_kernel(x_ref, mod_ref, w_ref, b_ref, q_ref, a_ref):
    feat = x_ref.shape[-1]
    x = x_ref[...].reshape(BLK, feat).astype(F32)
    normed, _ = norm_parts(x)
    a1 = (normed * (1.0 + mod_ref[0, 1:2, :]) + mod_ref[0, 0:1, :]).astype(BF16)
    a1_t = a1.T
    a_ref[...] = a1_t
    for i in range(3):
        part = slice(i * feat, (i + 1) * feat)
        q_ref[part, :] = (dot(w_ref[part, :], a1_t, 1, 0) + b_ref[part, :]).astype(BF16)


def row_spec(view):
    return pl.BlockSpec((view[0], 1, view[2], view[3]), lambda k: (0, k, 0, 0))


def whole(*shape):
    return pl.BlockSpec(shape, lambda k: (0,) * len(shape))


def qkv_forward(x_view, mod_blocks, w_t, bias):
    feat = x_view.shape[-1]
    blocks = x_view.shape[1]
    return pl.pallas_call(
        qkv_kernel,
        grid=(blocks,),
        in_specs=[
            row_spec(x_view.shape),
            pl.BlockSpec((1, 6, feat), lambda k: (k, 0, 0)),
            whole(3 * feat, feat),
            whole(3 * feat, 1),
        ],
        out_specs=[
            pl.BlockSpec((3 * feat, BLK), lambda k: (0, k)),
            pl.BlockSpec((feat, BLK), lambda k: (0, k)),
        ],
        out_shape=[
            jax.ShapeDtypeStruct((3 * feat, blocks * BLK), BF16),
            jax.ShapeDtypeStruct((feat, blocks * BLK), BF16),
        ],
        compiler_params=params(),
        cost_estimate=pl.CostEstimate(
            flops=6 * feat * feat * blocks * BLK, bytes_accessed=20 * 2**20, transcendentals=0
        ),
    )(x_view, mod_blocks, w_t, bias)


def masks(seg_ref, query_block, blocks):
    base = LOG2E / math.sqrt(HEAD_DIM)
    same = [seg_ref[query_block] == seg_ref[kb] for kb in range(blocks)]
    scales = [jnp.where(s, base, 0.0) for s in same]
    shifts = [jnp.where(s, 0.0, MASKED * LOG2E) for s in same]
    return scales, shifts


def attend_kernel(seg_ref, q_ref, k_ref, v_ref, o_ref, lse_ref, *, blocks, heads):
    for h in range(heads):
        hs = slice(h * HEAD_DIM, (h + 1) * HEAD_DIM)
        keys = k_ref[hs, :].T
        v_t = v_ref[hs, :]
        for qb in range(blocks):
            qs = slice(qb * BLK, (qb + 1) * BLK)
            q_t = q_ref[hs, qs]
            scales, shifts = masks(seg_ref, qb, blocks)
            scores = [dot(keys[kb * BLK : (kb + 1) * BLK], q_t, 1, 0) for kb in range(blocks)]
            top = None
            for kb in range(blocks):
                peak = jnp.max(scores[kb], axis=0, keepdims=True) * scales[kb] + shifts[kb]
                top = peak if top is None else jnp.maximum(top, peak)
            total = jnp.zeros((1, BLK), F32)
            parts = []
            for kb in range(blocks):
                expo = jnp.exp2(scores[kb] * scales[kb] - (top - shifts[kb]))
                total = total + jnp.sum(expo, axis=0, keepdims=True)
                parts.append(expo.astype(BF16))
            out = dot(v_t, jnp.concatenate(parts, axis=0), 1, 0)
            o_ref[hs, qs] = (out / total).astype(BF16)
            lse_ref[h, :, qs] = top + jnp.log2(total)


def attend(seg, qkv_t, heads=2):
    feat3, rows = qkv_t.shape
    feat = feat3 // 3
    span = heads * HEAD_DIM
    groups = feat // span
    return pl.pallas_call(
        functools.partial(attend_kernel, blocks=rows // BLK, heads=heads),
        grid_spec=pltpu.PrefetchScalarGridSpec(
            num_scalar_prefetch=1,
            grid=(groups,),
            in_specs=[
                pl.BlockSpec((span, rows), lambda g, s: (g, 0)),
                pl.BlockSpec((span, rows), lambda g, s: (groups + g, 0)),
                pl.BlockSpec((span, rows), lambda g, s: (2 * groups + g, 0)),
            ],
            out_specs=[
                pl.BlockSpec((span, rows), lambda g, s: (g, 0)),
                pl.BlockSpec((heads, 1, rows), lambda g, s: (g, 0, 0)),
            ],
        ),
        out_shape=[
            jax.ShapeDtypeStruct((feat, rows), BF16),
            jax.ShapeDtypeStruct((feat // HEAD_DIM, 1, rows), F32),
        ],
        compiler_params=params(),
        cost_estimate=pl.CostEstimate(
            flops=16 * feat * rows * rows, bytes_accessed=8 * 2**20, transcendentals=16 * rows * rows
        ),
    )(seg, qkv_t, qkv_t, qkv_t)


def attend_back_kernel(
    seg_ref, q_ref, k_ref, v_ref, o_ref, do_ref, lse_ref, out_ref, *, blocks, heads
):
    scale = 1.0 / math.sqrt(HEAD_DIM)
    for h in range(heads):
        hs = slice(h * HEAD_DIM, (h + 1) * HEAD_DIM)
        k_t = k_ref[hs, :]
        keys, values = k_t.T, v_ref[hs, :].T
        inner = jnp.sum(
            o_ref[hs, :].astype(F32) * do_ref[hs, :].astype(F32), axis=0, keepdims=True
        )
        grad_k = grad_v = None
        for qb in range(blocks):
            qs = slice(qb * BLK, (qb + 1) * BLK)
            q_t, do_t = q_ref[hs, qs], do_ref[hs, qs]
            scales, shifts = masks(seg_ref, qb, blocks)
            probs, grads = [], []
            for kb in range(blocks):
                ks = slice(kb * BLK, (kb + 1) * BLK)
                score = dot(keys[ks], q_t, 1, 0)
                grad_p = dot(values[ks], do_t, 1, 0)
                prob = jnp.exp2(score * scales[kb] - (lse_ref[h, :, qs] - shifts[kb]))
                probs.append(prob.astype(BF16))
                grads.append((prob * (grad_p - inner[:, qs])).astype(BF16))
            probs = jnp.concatenate(probs, axis=0)
            grads = jnp.concatenate(grads, axis=0)
            out_ref[0, hs, qs] = (dot(k_t, grads, 1, 0) * scale).astype(BF16)
            more_k, more_v = dot(q_t, grads, 1, 1), dot(do_t, probs, 1, 1)
            grad_k = more_k if grad_k is None else grad_k + more_k
            grad_v = more_v if grad_v is None else grad_v + more_v
        out_ref[1, hs, :] = (grad_k * scale).astype(BF16)
        out_ref[2, hs, :] = grad_v.astype(BF16)


def attend_back(seg, qkv_t, o_t, do_t, lse, heads=2):
    feat3, rows = qkv_t.shape
    feat = feat3 // 3
    span = heads * HEAD_DIM
    groups = feat // span
    return pl.pallas_call(
        functools.partial(attend_back_kernel, blocks=rows // BLK, heads=heads),
        grid_spec=pltpu.PrefetchScalarGridSpec(
            num_scalar_prefetch=1,
            grid=(groups,),
            in_specs=[
                pl.BlockSpec((span, rows), lambda g, s: (g, 0)),
                pl.BlockSpec((span, rows), lambda g, s: (groups + g, 0)),
                pl.BlockSpec((span, rows), lambda g, s: (2 * groups + g, 0)),
                pl.BlockSpec((span, rows), lambda g, s: (g, 0)),
                pl.BlockSpec((span, rows), lambda g, s: (g, 0)),
                pl.BlockSpec((heads, 1, rows), lambda g, s: (g, 0, 0)),
            ],
            out_specs=pl.BlockSpec((3, span, rows), lambda g, s: (0, g, 0)),
        ),
        out_shape=jax.ShapeDtypeStruct((3, feat, rows), BF16),
        compiler_params=params(),
        cost_estimate=pl.CostEstimate(
            flops=24 * feat * rows * rows, bytes_accessed=16 * 2**20, transcendentals=16 * rows * rows
        ),
    )(seg, qkv_t, qkv_t, qkv_t, o_t, do_t, lse)


def proj_kernel(o_ref, w_ref, b_ref, x_ref, mod_ref, attn_ref, x1_ref, a_ref, at_ref):
    feat = x_ref.shape[-1]
    attn = dot(o_ref[...], w_ref[...], 0, 0) + b_ref[...]
    attn_ref[...] = attn
    x1 = x_ref[...].reshape(BLK, feat).astype(F32) + mod_ref[0, 2:3, :] * attn
    x1_ref[...] = x1
    normed, _ = norm_parts(x1)
    a2 = (normed * (1.0 + mod_ref[0, 4:5, :]) + mod_ref[0, 3:4, :]).astype(BF16)
    a_ref[...] = a2
    at_ref[...] = a2.T


def proj_forward(o_t, w_proj, b_proj, x_view, mod_blocks):
    feat = x_view.shape[-1]
    blocks = x_view.shape[1]
    rows = blocks * BLK
    by_row = pl.BlockSpec((BLK, feat), lambda k: (k, 0))
    by_column = pl.BlockSpec((feat, BLK), lambda k: (0, k))
    return pl.pallas_call(
        proj_kernel,
        grid=(blocks,),
        in_specs=[
            by_column,
            whole(feat, feat),
            whole(1, feat),
            row_spec(x_view.shape),
            pl.BlockSpec((1, 6, feat), lambda k: (k, 0, 0)),
        ],
        out_specs=[by_row, by_row, by_row, by_column],
        out_shape=[
            jax.ShapeDtypeStruct((rows, feat), F32),
            jax.ShapeDtypeStruct((rows, feat), F32),
            jax.ShapeDtypeStruct((rows, feat), BF16),
            jax.ShapeDtypeStruct((feat, rows), BF16),
        ],
        compiler_params=params(),
        cost_estimate=pl.CostEstimate(
            flops=2 * feat * feat * rows, bytes_accessed=20 * 2**20, transcendentals=0
        ),
    )(o_t, w_proj, b_proj, x_view, mod_blocks)


def gelu_both(u):
    c = math.sqrt(2.0 / math.pi)
    square = u * u
    t = jnp.tanh(u * (c + (c * 0.044715) * square))
    half = 0.5 + 0.5 * t
    slope = half + (0.5 * u) * (1.0 - t * t) * (c + (3.0 * c * 0.044715) * square)
    return u * half, slope


def mlp_kernel(
    a_ref, at_ref, df_ref, dg_ref, w1_ref, w2_ref, b1_ref,
    f_ref, da_ref, d1_ref, d2_ref, db_ref, g_ref, du_ref,
):
    step = pl.program_id(0)
    rows = a_ref.shape[0]

    @pl.when(step == 0)
    def _():
        f_ref[...] = jnp.zeros_like(f_ref)
        da_ref[...] = jnp.zeros_like(da_ref)

    w1, w2 = w1_ref[...], w2_ref[...]
    bias = jnp.zeros((1, w1.shape[1]), F32)
    for r in range(rows // BLK):
        rs = slice(r * BLK, (r + 1) * BLK)
        u = dot(a_ref[rs, :], w1, 1, 0) + b1_ref[...]
        g, slope = gelu_both(u)
        g = g.astype(BF16)
        du = (dg_ref[rs, :] * slope).astype(BF16)
        g_ref[rs, :] = g
        du_ref[rs, :] = du
        bias = bias + jnp.sum(du.astype(F32), axis=0, keepdims=True)
        f_ref[rs, :] += dot(g, w2, 1, 0)
        da_ref[rs, :] += dot(du, w1, 1, 1)
    db_ref[...] = bias
    du = du_ref[...]
    d1_ref[0] = dot(at_ref[...], du, 1, 0).astype(BF16)
    d2_ref[...] = dot(g_ref[...], df_ref[...], 0, 0).astype(BF16)


def mlp(a2, a2_t, df, dg, w1, w2, b1, width=512):
    rows, feat = a2.shape
    hidden = w1.shape[1]
    per = feat // width
    one = pl.Buffered(1)

    def fixed(*shape):
        return pl.BlockSpec(shape, lambda j: (0,) * len(shape), pipeline_mode=one)

    return pl.pallas_call(
        mlp_kernel,
        grid=(hidden // width,),
        in_specs=[
            fixed(rows, feat),
            fixed(feat, rows),
            fixed(rows, feat),
            pl.BlockSpec((rows, width), lambda j: (0, j)),
            pl.BlockSpec((feat, width), lambda j: (0, j)),
            pl.BlockSpec((width, feat), lambda j: (j, 0)),
            pl.BlockSpec((1, width), lambda j: (0, j)),
        ],
        out_specs=[
            whole(rows, feat),
            whole(rows, feat),
            pl.BlockSpec((1, feat, width), lambda j: (j // per, 0, j % per)),
            pl.BlockSpec((width, feat), lambda j: (j, 0)),
            pl.BlockSpec((1, width), lambda j: (0, j)),
        ],
        out_shape=[
            jax.ShapeDtypeStruct((rows, feat), F32),
            jax.ShapeDtypeStruct((rows, feat), F32),
            jax.ShapeDtypeStruct((hidden // feat, feat, feat), BF16),
            jax.ShapeDtypeStruct((hidden, feat), BF16),
            jax.ShapeDtypeStruct((1, hidden), F32),
        ],
        scratch_shapes=[pltpu.VMEM((rows, width), BF16), pltpu.VMEM((rows, width), BF16)],
        compiler_params=params(),
        cost_estimate=pl.CostEstimate(
            flops=10 * rows * feat * hidden, bytes_accessed=64 * 2**20, transcendentals=rows * hidden
        ),
    )(a2, a2_t, df, dg, w1, w2, b1)


def middle_kernel(
    f_ref, b2_ref, x1_ref, attn_ref, dy_ref, da_ref, mod_ref, o_ref, w_ref,
    y_ref, dx_ref, do_ref, dw_ref, db_ref, sums_ref, acc_ref,
):
    k = pl.program_id(0)

    @pl.when(k == 0)
    def _():
        acc_ref[...] = jnp.zeros_like(acc_ref)
        db_ref[...] = jnp.zeros_like(db_ref)

    f = f_ref[...] + b2_ref[...]
    x1 = x1_ref[...]
    dy = dy_ref[...].astype(F32)
    y_ref[...] = (x1 + mod_ref[0, 5:6, :] * f).astype(BF16)
    normed, inverse = norm_parts(x1)
    da = da_ref[...]
    dx1 = dy + norm_back(da * (1.0 + mod_ref[0, 4:5, :]), normed, inverse)
    dx_ref[...] = dx1
    dattn = (mod_ref[0, 2:3, :] * dx1).astype(BF16)
    db_ref[...] += jnp.sum(dattn.astype(F32), axis=0, keepdims=True)
    sums_ref[0, 0:1, :] = jnp.sum(dx1 * attn_ref[...], axis=0, keepdims=True)
    sums_ref[0, 1:2, :] = jnp.sum(da, axis=0, keepdims=True)
    sums_ref[0, 2:3, :] = jnp.sum(da * normed, axis=0, keepdims=True)
    sums_ref[0, 3:4, :] = jnp.sum(dy * f, axis=0, keepdims=True)
    do_ref[...] = dot(w_ref[...], dattn, 1, 1).astype(BF16)
    acc_ref[...] += dot(o_ref[...], dattn, 1, 0)

    @pl.when(k == pl.num_programs(0) - 1)
    def _():
        dw_ref[...] = acc_ref[...].astype(BF16)


def middle(f, b2, x1, attn, dy, da2, mod_blocks, o_t, w_proj):
    rows, feat = x1.shape
    by_row = pl.BlockSpec((BLK, feat), lambda k: (k, 0))
    by_column = pl.BlockSpec((feat, BLK), lambda k: (0, k))
    blocks = rows // BLK
    return pl.pallas_call(
        middle_kernel,
        grid=(blocks,),
        in_specs=[
            by_row, whole(1, feat), by_row, by_row, by_row, by_row,
            pl.BlockSpec((1, 6, feat), lambda k: (k, 0, 0)),
            by_column, whole(feat, feat),
        ],
        out_specs=[
            by_row, by_row, by_column, whole(feat, feat), whole(1, feat),
            pl.BlockSpec((1, 4, feat), lambda k: (k, 0, 0)),
        ],
        out_shape=[
            jax.ShapeDtypeStruct((rows, feat), BF16),
            jax.ShapeDtypeStruct((rows, feat), F32),
            jax.ShapeDtypeStruct((feat, rows), BF16),
            jax.ShapeDtypeStruct((feat, feat), BF16),
            jax.ShapeDtypeStruct((1, feat), F32),
            jax.ShapeDtypeStruct((blocks, 4, feat), F32),
        ],
        scratch_shapes=[pltpu.VMEM((feat, feat), F32)],
        compiler_params=params(),
        cost_estimate=pl.CostEstimate(
            flops=4 * feat * feat * rows, bytes_accessed=32 * 2**20, transcendentals=0
        ),
    )(f, b2, x1, attn, dy, da2, mod_blocks, o_t, w_proj)


def rows_back_kernel(dq_ref, w_ref, x_ref, dx_ref, mod_ref, out_ref, sums_ref):
    feat = x_ref.shape[-1]
    da = dot(dq_ref[0], w_ref[0:feat, :], 0, 0)
    for i in (1, 2):
        da = da + dot(dq_ref[i], w_ref[i * feat : (i + 1) * feat, :], 0, 0)
    normed, inverse = norm_parts(x_ref[...].reshape(BLK, feat).astype(F32))
    out = dx_ref[...] + norm_back(da * (1.0 + mod_ref[0, 1:2, :]), normed, inverse)
    out_ref[...] = out.astype(BF16).reshape(out_ref.shape)
    sums_ref[0, 0:1, :] = jnp.sum(da, axis=0, keepdims=True)
    sums_ref[0, 1:2, :] = jnp.sum(da * normed, axis=0, keepdims=True)


def rows_back(dqkv_t, w_t, x_view, dx1, mod_blocks):
    rows, feat = dx1.shape
    blocks = rows // BLK
    return pl.pallas_call(
        rows_back_kernel,
        grid=(blocks,),
        in_specs=[
            pl.BlockSpec((3, feat, BLK), lambda k: (0, 0, k)),
            whole(3 * feat, feat),
            row_spec(x_view.shape),
            pl.BlockSpec((BLK, feat), lambda k: (k, 0)),
            pl.BlockSpec((1, 6, feat), lambda k: (k, 0, 0)),
        ],
        out_specs=[row_spec(x_view.shape), pl.BlockSpec((1, 2, feat), lambda k: (k, 0, 0))],
        out_shape=[
            jax.ShapeDtypeStruct(x_view.shape, BF16),
            jax.ShapeDtypeStruct((blocks, 2, feat), F32),
        ],
        compiler_params=params(),
        cost_estimate=pl.CostEstimate(
            flops=6 * feat * feat * rows, bytes_accessed=20 * 2**20, transcendentals=0
        ),
    )(dqkv_t, w_t, x_view, dx1, mod_blocks)


def swap(values, axis, bit):
    count = lax.axis_size(axis)
    return lax.ppermute(values, axis, [(i, i ^ bit) for i in range(count)])


def add_low(left, right):
    return (left.astype(F32) + right.astype(F32)).astype(BF16)


def pick(values, index, dim):
    return lax.dynamic_index_in_dim(values, index, dim, keepdims=False)


def bits_of(wide):
    return [1 << i for i in range(wide.bit_length() - 1)]


def chain_orders(wide):
    bits = bits_of(wide)
    near, far = bits[:3], bits[3:]
    return [near[i:] + near[:i] + far for i in range(3)]


def scatter_chain(values, order):
    wide = values.shape[0]
    bits = bits_of(wide)
    values = values.reshape((2,) * len(bits) + values.shape[1:])
    dims = list(reversed(bits))
    me = lax.axis_index("wide")
    for bit in order:
        dim = dims.index(bit)
        own = (me // bit) % 2
        got = swap(pick(values, 1 - own, dim), "wide", bit)
        values = add_low(pick(values, own, dim), got)
        dims.pop(dim)
    return values


def scatter_sum(send, keep):
    got = swap(send, "narrow", 1)
    wide, rows = keep.shape[:2]
    third = rows // 3 // TILE * TILE
    cuts = [0, third, 2 * third, rows]
    parts = []
    for i, order in enumerate(chain_orders(wide)):
        cut = slice(cuts[i], cuts[i + 1])
        parts.append(scatter_chain(add_low(keep[:, cut], got[:, cut]), order))
    return jnp.concatenate(parts, axis=0)


def gather_slots(values):
    for bit in reversed(bits_of(lax.axis_size("wide"))):
        values = jnp.concatenate([values, swap(values, "wide", bit)], axis=0)
    return jnp.concatenate([values, swap(values, "narrow", 1)], axis=0)


def local(
    x_src,
    cond,
    lengths,
    bucket,
    w_mod,
    b_mod,
    w_qkv,
    b_qv,
    w_proj,
    b_proj,
    w_fc1,
    b_fc1,
    w_fc2,
    b_fc2,
    grad_out,
):
    wide = lax.axis_size("wide")
    halves = lax.axis_size("narrow")
    devices = wide * halves
    group = lax.axis_index("wide")
    half = lax.axis_index("narrow")
    rows, feat = x_src.shape
    hidden = w_fc1.shape[1]
    places = lengths.shape[0] // halves
    slots = places // wide
    blocks = rows // BLK
    per_block = BLK // wide
    tiled = per_block % TILE == 0

    lens = lax.dynamic_slice_in_dim(lengths, half * places, places)
    buck = lax.dynamic_slice_in_dim(bucket, half * places, places)
    split = regroup if tiled else regroup_any
    send, scond, seg, src, cidx = split(x_src, cond, lens, buck, group.reshape(1), wide)
    exchange = functools.partial(
        lax.all_to_all, axis_name="wide", split_axis=0, concat_axis=0, tiled=True
    )
    came = exchange(send)
    came_cond = exchange(scond.reshape(wide, slots, feat // wide))
    cond_in = came_cond.transpose(1, 0, 2).reshape(slots, feat)
    x_view = came.reshape(wide, blocks, per_block, feat)
    if not tiled:
        x_view = x_view.transpose(1, 0, 2, 3).reshape(1, blocks, BLK, feat)

    act, silu_back = jax.vjp(jax.nn.silu, cond_in.astype(F32))
    act_low = act.astype(BF16)
    modulate = jnp.dot(act_low, w_mod, preferred_element_type=F32) + b_mod.astype(F32)
    slot_ids = jnp.arange(slots, dtype=jnp.int32)
    in_slot = seg[:, None] == slot_ids[None, :]
    mod_blocks = jnp.sum(
        jnp.where(in_slot[:, :, None], modulate[None], 0.0), axis=1
    ).reshape(blocks, 6, feat)

    dy = (
        grad_out.reshape(blocks, per_block, wide, feat)
        .transpose(0, 2, 1, 3)
        .reshape(rows, feat)
    )
    gate_two = mod_blocks[:, 5:6, :]
    df = (
        (gate_two * dy.reshape(blocks, BLK, feat).astype(F32)).astype(BF16).reshape(rows, feat)
    )
    grad_b_fc2 = jnp.sum(df.astype(F32), axis=0)
    dg = dot(df, w_fc2, 1, 1)
    w_qkv_t = w_qkv.T
    bias_qkv = jnp.concatenate(
        [b_qv[:feat].astype(F32), jnp.zeros((feat,), F32), b_qv[feat:].astype(F32)]
    ).reshape(3 * feat, 1)

    qkv_t, a1_t = qkv_forward(x_view, mod_blocks, w_qkv_t, bias_qkv)
    o_t, lse = attend(seg, qkv_t)
    attn, x1, a2, a2_t = proj_forward(
        o_t, w_proj, b_proj.astype(F32).reshape(1, feat), x_view, mod_blocks
    )
    f, da2, d_fc1, d_fc2, grad_b_fc1 = mlp(
        a2, a2_t, df, dg, w_fc1, w_fc2, b_fc1.astype(F32).reshape(1, hidden)
    )

    part = feat // devices
    d_fc1 = d_fc1.reshape(hidden // feat, wide, halves, part, feat)
    d_fc2 = d_fc2.reshape(wide, halves, hidden // devices, feat)

    def mlp_half(which):
        one = pick(d_fc1, which, 2).transpose(1, 0, 2, 3).reshape(wide, -1, feat)
        return jnp.concatenate([pick(d_fc2, which, 1), one], axis=1)

    mlp_sum = scatter_sum(mlp_half(1 - half), mlp_half(half))

    y, dx1, do_t, d_proj, grad_b_proj, sums_two = middle(
        f, b_fc2.astype(F32).reshape(1, feat), x1, attn, dy, da2, mod_blocks, o_t, w_proj
    )
    y_dest = (
        y.reshape(blocks, wide, per_block, feat).transpose(0, 2, 1, 3).reshape(rows, feat)
    )
    dqkv_t = attend_back(seg, qkv_t, o_t, do_t, lse)

    a1_parts = a1_t.reshape(wide, halves, part, rows)
    d_proj = d_proj.reshape(wide, halves, part, feat)

    def qkv_half(which):
        mine = pick(a1_parts, which, 1).reshape(wide * part, rows)
        three = lax.dot_general(
            mine, dqkv_t, (((1,), (2,)), ((), ())), preferred_element_type=F32
        )
        three = three.reshape(wide, part, 3, feat).transpose(0, 2, 1, 3)
        return jnp.concatenate(
            [three.astype(BF16).reshape(wide, 3 * part, feat), pick(d_proj, which, 1)], axis=1
        )

    qkv_sum = scatter_sum(qkv_half(1 - half), qkv_half(half))
    sums_q = jnp.sum(dqkv_t.astype(F32), axis=2)
    grad_b_qv = jnp.concatenate([sums_q[0], sums_q[2]])

    drows, sums_one = rows_back(dqkv_t, w_qkv_t, x_view, dx1, mod_blocks)
    back = drows
    if not tiled:
        back = back.reshape(blocks, wide, per_block, feat).transpose(1, 0, 2, 3)
    back = exchange(back.reshape(wide, rows // wide, feat)).reshape(rows, feat)

    by_slot = in_slot.astype(F32)

    def slot_sums(sums):
        count = sums.shape[1]
        picked = jnp.where(in_slot[:, :, None, None], sums[:, None], 0.0)
        return jnp.sum(picked, axis=0).reshape(slots, count * feat).astype(BF16)

    dmod_two, dmod_one = slot_sums(sums_two), slot_sums(sums_one)
    dact = dot(dmod_two, w_mod[:, 2 * feat :], 1, 1) + dot(dmod_one, w_mod[:, : 2 * feat], 1, 1)
    dcond_in = silu_back(dact)[0].astype(BF16)
    back_cond = exchange(
        dcond_in.reshape(slots, wide, feat // wide).transpose(1, 0, 2)
    ).reshape(places, feat // wide)
    merge = restore if tiled else restore_any
    dx_src, dcond = merge(src, cidx, back, back_cond)

    me = group * halves + half
    two_all = gather_slots(jnp.concatenate([act_low, dmod_two], axis=1))
    one_all = gather_slots(dmod_one)
    act_mine = lax.dynamic_slice_in_dim(two_all[:, :feat], me * part, part, axis=1)
    dmod_all = jnp.concatenate([one_all, two_all[:, feat:]], axis=1)
    grad_w_mod = dot(act_mine, dmod_all, 0, 0)
    grad_b_mod = jnp.sum(
        lax.dynamic_slice_in_dim(dmod_all, me * 6 * part, 6 * part, axis=1).astype(F32), axis=0
    )

    biases = jnp.concatenate(
        [
            grad_b_fc1.reshape(devices, -1),
            grad_b_fc2.reshape(devices, -1),
            grad_b_proj.reshape(devices, -1),
            grad_b_qv.reshape(devices, -1),
        ],
        axis=1,
    )
    biases = jnp.sum(
        lax.all_to_all(biases, ("wide", "narrow"), split_axis=0, concat_axis=0, tiled=True), axis=0
    )
    at_two, at_proj, at_qv = 4 * part, 5 * part, 6 * part

    fc2_rows = hidden // devices
    grad_w_fc2 = mlp_sum[:fc2_rows].astype(F32)
    grad_w_fc1 = (
        mlp_sum[fc2_rows:]
        .reshape(hidden // feat, part, feat)
        .transpose(1, 0, 2)
        .reshape(part, hidden)
        .astype(F32)
    )
    grad_w_qkv = (
        qkv_sum[: 3 * part]
        .reshape(3, part, feat)
        .transpose(1, 0, 2)
        .reshape(part, 3 * feat)
        .astype(F32)
    )
    grad_w_proj = qkv_sum[3 * part :].astype(F32)
    return (
        y_dest,
        dx_src,
        dcond,
        grad_w_mod,
        grad_b_mod,
        grad_w_qkv,
        biases[at_qv:],
        grad_w_proj,
        biases[at_proj:at_qv],
        grad_w_fc1,
        biases[:at_two],
        grad_w_fc2,
        biases[at_two:at_proj],
    )


def solution(mesh):
    both = ("wide", "narrow")
    placed = (P("narrow", "wide"), P("narrow", "wide")) + (P(),) * 12 + (P(both, None),)
    matrix, vector = P(both, None), P(both)
    return jax.shard_map(
        local,
        mesh=mesh,
        in_specs=placed,
        out_specs=(
            matrix,
            P("narrow", "wide"),
            P("narrow", "wide"),
            matrix,
            vector,
            matrix,
            vector,
            matrix,
            vector,
            matrix,
            vector,
            matrix,
            vector,
        ),
        check_vma=False,
    )
```

time: 1410 us -> 684 us (0.49)
  waiting for transfers between devices: 606 us -> 211 us
  matrix products: 322 us -> 49 us
  Pallas kernels: 0 us -> 211 us
  local copies, waits for them, and re-layouts: 172 us -> 79.8 us
  other arithmetic: 120 us -> 47.9 us
  blocking collectives: 83.8 us -> 15.4 us
  loops' own time: 53.8 us -> 0 us
  starting transfers between devices: 30.1 us -> 57.7 us
    reduce_scatter x5 -> x0, waiting for transfers between devices: 583 us -> none  [the longest x1 255 us: local(): lax.psum_scatter(d_mod, ('wide', 'narrow'), scatter_dimension=0, tiled=True)]
    dot_general x74 -> x7, matrix products: 322 us -> 49 us  [the longest x4 26.7 us: dot(): lax.dot_general(left, right, (((left_dim,), (right_dim,)), ((), ())), pre...]
    pallas_call x0 -> x9, Pallas kernels: none -> 211 us  [the longest x1 62.9 us: mlp(): pl.pallas_call(mlp_kernel, grid=(hidden // width,), in_specs=[fixed(rows,...]
    ppermute x0 -> x36, waiting for transfers between devices: none -> 201 us  [swap(): return lax.ppermute(values, axis, [(i, i ^ bit) for i in range(count)])]
    unnamed x1 -> x0, blocking collectives: 83.8 us -> none
    dynamic_slice x88 -> x6, local copies, waits for them, and re-layouts: 62.5 us -> 3.4 us  [the longest x1 1.24 us: local(): lens = lax.dynamic_slice_in_dim(lengths, half * places, places)]
    another operation x2 -> x0, loops' own time: 53.8 us -> none  [the longest x1 32.2 us: attend_backward(): lax.map(one_tile, jnp.arange(block_count * group_count, dtype=jnp.int32))]
    reduce_sum x20 -> x7, other arithmetic: 59.3 us -> 7.96 us  [the longest x1 3.83 us: local(): sums_q = jnp.sum(dqkv_t.astype(F32), axis=2)]
  transfers between devices with their start and end apart: 9 -> 40, of which waited for: 5 -> 23; matrix products, arithmetic and copies ran while one was open for 26% -> 22% of each run, Pallas kernels for 0% -> 12%
where the time goes in v1:
time: 684 us; the launch traced here: 674 us
  Pallas kernels  211 us (31%)
  waiting for transfers between devices  211 us (31%)
  local copies, waits for them, and re-layouts  79.8 us (12%)
  starting transfers between devices  57.7 us (8%)
  matrix products  49 us (7%)
  other arithmetic  47.9 us (7%)
  blocking collectives  15.4 us (2%)
    ppermute x36, waiting for transfers between devices, swap(): return lax.ppermute(values, axis, [(i, i ^ bit) for i in range(count)])  201 us
    pallas_call x1, Pallas kernels, mlp(): pl.pallas_call(mlp_kernel, grid=(hidden // width,), in_specs=[fixed(rows,...  62.9 us
    pallas_call x1, Pallas kernels, attend_back(): pl.pallas_call(functools.partial(attend_back_kernel, blocks=rows // BLK,...  48.1 us
    pallas_call x1, Pallas kernels, attend(): pl.pallas_call(functools.partial(attend_kernel, blocks=rows // BLK, heads...  37.6 us
    ppermute x36, starting transfers between devices, swap(): return lax.ppermute(values, axis, [(i, i ^ bit) for i in range(count)])  36.4 us
    dot_general x4, matrix products, dot(): lax.dot_general(left, right, (((left_dim,), (right_dim,)), ((), ())), pre...  26.7 us
    convert_element_type x28, other arithmetic, add_low(): return (left.astype(F32) + right.astype(F32)).astype(BF16)  17.7 us
    pallas_call x1, Pallas kernels, middle(): pl.pallas_call(middle_kernel, grid=(blocks,), in_specs=[by_row, whole(1,...  16.4 us
  transfers between devices with their start and end apart: 40, of which 23 were waited for; matrix products, arithmetic and copies ran while one was open for 22% of the time, Pallas kernels for 12%

profile of v1, /device:TPU:0, one launch (start us, length us, event | category | flops | bytes accessed | tf_op | source)
XLA Modules:
  0.0 673.5 jit_solution(11036179643524273890)
XLA Ops:
  9.6 15.4 %all_to_all.29 = bf16[16,2,128]{2,1,0:T(2,128)(2,1)S(1)} all-to-all(bf16[16,2,128]{2,1,0:T(2,128)(2,1)S(1)} %reshape.353), channel_id=1, replica_groups=mesh['wide'=16,'narrow'=2] {'wide'}, dimensions={0} | all-to-all | bytes 16384 | tf_op jit(solution)/shard_map/all_to_all | solution.py:708
  31.2 8.6 %copy.196 = bf16[1024,3072]{0,1:T(8,128)(2,1)} copy(bf16[1024,3072]{1,0:T(8,128)(2,1)} %param.21) | data formatting | bytes 12582912 | tf_op args[6]
  55.5 16.1 %fusion.58.dg_ref = f32[1024,4096]{1,0:T(8,128)} fusion(bf16[1024,1024]{1,0:T(8,128)(2,1)} %fusion.6.df_ref, bf16[4096,1024]{1,0:T(8,128)(2,1)} %w2_ref.1), kind=kOutput, calls=%fused_computation.160 | convolution fusion | flops 8589934592 | bytes 27262976 | tf_op jit(solution)/shard_map/dot_general | solution.py:28
  71.9 13.5 %shard_map.247 = (bf16[3072,1024]{1,0:T(8,128)(2,1)}, bf16[1024,1024]{1,0:T(8,128)(2,1)}) custom-call(bf16[16,4,16,1024]{3,2,1,0:T(8,128)(2,1)} %bitcast.1.x_ref, f32[4,6,1024]{2,1,0:T(8,128)} %copy-done.13, bf16[3072,1024]{1,0:T(8,128)(2,1)} %bitcast.259, f32[3072,1]{1,0:T(8,128)} %copy.197.b_ref), custom_call_target="tpu_custom_call" | custom-call | flops 6442450944 | bytes 20971520 | tf_op jit(solution)/shard_map/pallas_call | solution.py:236
  85.4 37.6 %shard_map.248 = (bf16[1024,1024]{1,0:T(8,128)(2,1)}, f32[16,1,1024]{2,1,0:T(1,128)}) custom-call(s32[4]{0:T(128)} %get-tuple-element.41.seg_ref, bf16[3072,1024]{1,0:T(8,128)(2,1)} %get-tuple-element.44.q_ref.k_ref.v_ref, bf16[3072,1024]{1,0:T(8,128)(2,1)} %get-tuple-element.44.q_ref.k_ref.v_ref, bf16[3072,1024]{1,0:T(8,128)(2,1)} %get-tuple-element.44.q_ref.k_ref.v_ref), custom_call_target="tpu_custom_call" | custom-call | flops 17179869184 | bytes 8388608 | tf_op jit(solution)/shard_map/pallas_call | solution.py:298
  123.0 9.0 %shard_map.249 = (f32[1024,1024]{1,0:T(8,128)}, f32[1024,1024]{1,0:T(8,128)}, bf16[1024,1024]{1,0:T(8,128)(2,1)}, bf16[1024,1024]{1,0:T(8,128)(2,1)}) custom-call(bf16[1024,1024]{1,0:T(8,128)(2,1)} %get-tuple-element.45.o_ref, bf16[1024,1024]{1,0:T(8,128)(2,1)} %w_ref.3, f32[1,1024]{1,0:T(1,128)} %bitcast.293, bf16[16,4,16,1024]{3,2,1,0:T(8,128)(2,1)} %bitcast.1.x_ref, ...), custom_call_target="tpu_custom_call" | custom-call | flops 2147483648 | bytes 20971520 | tf_op jit(solution)/shard_map/pallas_call | solution.py:404
  132.0 62.9 %shard_map.250 = (f32[1024,1024]{1,0:T(8,128)}, f32[1024,1024]{1,0:T(8,128)}, bf16[4,1024,1024]{2,1,0:T(8,128)(2,1)}, bf16[4096,1024]{1,0:T(8,128)(2,1)}, f32[1,4096]{1,0:T(1,128)}) custom-call(bf16[1024,1024]{1,0:T(8,128)(2,1)} %get-tuple-element.46.a_ref, bf16[1024,1024]{1,0:T(8,128)(2,1)} %get-tuple-element.47.at_ref, bf16[1024,1024]{1,0:T(8,128)(2,1)} %fusion.6.df_ref, ...), custom_call_target="tpu_custom_call" | custom-call | flops 42949672960 | bytes 67108864 | tf_op jit(solution)/shard_map/pallas_call | solution.py:477
  209.0 8.2 %pad_maximum_fusion = bf16[16,256,1024]{2,1,0:T(8,128)(2,1)} fusion(bf16[16,128,1024]{2,1,0:T(8,128)(2,1)} %bitcast.244, bf16[16,128,1024]{2,1,0:T(8,128)(2,1)} %get-tuple-element.74), kind=kLoop, calls=%fused_computation.1 | loop fusion | flops 16777216 | bytes 16777216 | tf_op jit(solution)/shard_map/concatenate | solution.py:754
  217.2 16.4 %shard_map.251 = (bf16[1024,1024]{1,0:T(8,128)(2,1)}, f32[1024,1024]{1,0:T(8,128)}, bf16[1024,1024]{1,0:T(8,128)(2,1)}, bf16[1024,1024]{1,0:T(8,128)(2,1)}, f32[1,1024]{1,0:T(1,128)}, /*index=5*/f32[4,4,1024]{2,1,0:T(4,128)}) custom-call(f32[1024,1024]{1,0:T(8,128)} %get-tuple-element.48.f_ref, f32[1,1024]{1,0:T(1,128)} %bitcast.289, ...), custom_call_target="tpu_custom_call" | custom-call | flops 4294967296 | bytes 33554432 | tf_op jit(solution)/shard_map/pallas_call | solution.py:549
  233.6 48.1 %shard_map.252.dq_ref = bf16[3,1024,1024]{2,1,0:T(8,128)(2,1)} custom-call(s32[4]{0:T(128)} %get-tuple-element.41.seg_ref, bf16[3072,1024]{1,0:T(8,128)(2,1)} %get-tuple-element.44.q_ref.k_ref.v_ref, bf16[3072,1024]{1,0:T(8,128)(2,1)} %get-tuple-element.44.q_ref.k_ref.v_ref, bf16[3072,1024]{1,0:T(8,128)(2,1)} %get-tuple-element.44.q_ref.k_ref.v_ref, ...), custom_call_target="tpu_custom_call" | custom-call | flops 25769803776 | bytes 16777216 | tf_op jit(solution)/shard_map/pallas_call | solution.py:363
  296.2 13.7 %shard_map.253 = (bf16[16,4,16,1024]{3,2,1,0:T(8,128)(2,1)}, f32[4,2,1024]{2,1,0:T(2,128)}) custom-call(bf16[3,1024,1024]{2,1,0:T(8,128)(2,1)} %shard_map.252.dq_ref, bf16[3072,1024]{1,0:T(8,128)(2,1)} %bitcast.260, bf16[16,4,16,1024]{3,2,1,0:T(8,128)(2,1)} %bitcast.1.x_ref, f32[1024,1024]{1,0:T(8,128)} %get-tuple-element.57.dx_ref, f32[4,6,1024]{2,1,0:T(8,128)} %copy-done.13), custom_call_target="tpu_custom_call" | custom-call | flops 6442450944 | bytes 20971520 | tf_op jit(solution)/shard_map/pallas_call | solution.py:592
  320.6 9.7 %all-to-all-start.3 = ((bf16[16,2,128]{2,1,0:T(2,128)(2,1)}), bf16[16,2,128]{2,1,0:T(2,128)(2,1)S(1)}, u32[]{:S(2)}, u32[]{:S(2)}) async-start(bf16[16,2,128]{2,1,0:T(2,128)(2,1)} %reshape.355), calls=%async_computation.3 | async-start | bytes 16384 | tf_op jit(solution)/shard_map/all_to_all | solution.py:799
  355.4 59.0 %collective-permute-done = bf16[4,5120]{1,0:T(4,128)(2,1)S(1)} collective-permute-done((bf16[4,5120]{1,0:T(4,128)(2,1)S(1)}, bf16[4,5120]{1,0:T(4,128)(2,1)S(1)}, u32[]{:S(2)}, u32[]{:S(2)}) %collective-permute-start) | collective-permute-done | bytes 40992 | tf_op jit(solution)/shard_map/ppermute | solution.py:616
  414.6 10.4 %collective-permute-done.5 = bf16[4,2048]{0,1:T(8,128)(2,1)S(1)} collective-permute-done((bf16[4,2048]{0,1:T(8,128)(2,1)S(1)}, bf16[4,2048]{0,1:T(8,128)(2,1)S(1)}, u32[]{:S(2)}, u32[]{:S(2)}) %collective-permute-start.5) | collective-permute-done | bytes 16416 | tf_op jit(solution)/shard_map/ppermute | solution.py:616
  429.2 9.2 %collective-permute-done.6 = bf16[8,2048]{0,1:T(8,128)(2,1)S(1)} collective-permute-done((bf16[8,2048]{0,1:T(8,128)(2,1)S(1)}, bf16[8,2048]{0,1:T(8,128)(2,1)S(1)}, u32[]{:S(2)}, u32[]{:S(2)}) %collective-permute-start.6) | collective-permute-done | bytes 32800 | tf_op jit(solution)/shard_map/ppermute | solution.py:616
  442.7 9.1 %collective-permute-done.7 = bf16[16,2048]{0,1:T(8,128)(2,1)S(1)} collective-permute-done((bf16[16,2048]{0,1:T(8,128)(2,1)S(1)}, bf16[16,2048]{0,1:T(8,128)(2,1)S(1)}, u32[]{:S(2)}, u32[]{:S(2)}) %collective-permute-start.7) | collective-permute-done | bytes 65568 | tf_op jit(solution)/shard_map/ppermute | solution.py:616
  454.0 10.9 %collective-permute-done.8 = bf16[32,2048]{0,1:T(8,128)(2,1)S(1)} collective-permute-done((bf16[32,2048]{0,1:T(8,128)(2,1)}, bf16[32,2048]{0,1:T(8,128)(2,1)S(1)}, u32[]{:S(2)}, u32[]{:S(2)}) %collective-permute-start.8) | collective-permute-done | bytes 131104 | tf_op jit(solution)/shard_map/ppermute | solution.py:616
  471.1 8.2 %fusion.12 = bf16[16,32,3,1024]{3,1,2,0:T(8,128)(2,1)} fusion(bf16[3,1024,1024]{2,1,0:T(8,128)(2,1)} %shard_map.252.dq_ref, bf16[16,2,32,1024]{3,2,1,0:T(8,128)(2,1)} %bitcast.294, s32[]{:T(128)S(6)} %select_n.217), kind=kOutput, calls=%fused_computation.31 | convolution fusion | flops 3222798336 | bytes 10485764 | tf_op jit(solution)/shard_map/dot_general | solution.py:771
  505.5 8.4 %concatenate.86 = bf16[128,5120]{0,1:T(8,128)(2,1)} concatenate(bf16[4,5120]{0,1:T(8,128)(2,1)S(1)} %copy.201, bf16[4,5120]{0,1:T(8,128)(2,1)S(1)} %copy-done.5, bf16[8,5120]{0,1:T(8,128)(2,1)} %copy.203, bf16[16,5120]{0,1:T(8,128)(2,1)} %copy.204, bf16[32,5120]{0,1:T(8,128)(2,1)} %copy.205, bf16[64,5120]{0,1:T(8,128)(2,1)} %copy.206), dimensions={0} | concatenate | bytes 2621440 | tf_op jit(solution)/shard_map/concatenate | solution.py:667
  547.0 13.9 %collective-permute-done.16 = bf16[2,2,32,1024]{3,2,1,0:T(8,128)(2,1)S(1)} collective-permute-done((bf16[2,2,32,1024]{3,2,1,0:T(8,128)(2,1)S(1)}, bf16[2,2,32,1024]{3,2,1,0:T(8,128)(2,1)S(1)}, u32[]{:S(2)}, u32[]{:S(2)}) %collective-permute-start.16) | collective-permute-done | bytes 262176 | tf_op jit(solution)/shard_map/ppermute | solution.py:616
  597.6 16.0 %collective-permute-done.32 = bf16[2,2,2,80,1024]{4,3,0,1,2:T(8,128)(2,1)S(1)} collective-permute-done((bf16[2,2,2,80,1024]{4,3,0,1,2:T(8,128)(2,1)S(1)}, bf16[2,2,2,80,1024]{4,3,0,1,2:T(8,128)(2,1)S(1)}, u32[]{:S(2)}, u32[]{:S(2)}) %collective-permute-start.32) | collective-permute-done | bytes 1310752 | tf_op jit(solution)/shard_map/ppermute | solution.py:616
  620.8 11.0 %collective-permute-done.28 = bf16[2,2,2,96,1024]{4,3,0,1,2:T(8,128)(2,1)S(1)} collective-permute-done((bf16[2,2,2,96,1024]{4,3,0,1,2:T(8,128)(2,1)S(1)}, bf16[2,2,2,96,1024]{4,3,0,1,2:T(8,128)(2,1)S(1)}, u32[]{:S(2)}, u32[]{:S(2)}) %collective-permute-start.28) | collective-permute-done | bytes 1572896 | tf_op jit(solution)/shard_map/ppermute | solution.py:616
  635.2 8.4 %collective-permute-done.25 = bf16[2,2,80,1024]{3,2,1,0:T(8,128)(2,1)S(1)} collective-permute-done((bf16[2,2,80,1024]{3,2,1,0:T(8,128)(2,1)S(1)}, bf16[2,2,80,1024]{3,2,1,0:T(8,128)(2,1)S(1)}, u32[]{:S(2)}, u32[]{:S(2)}) %collective-permute-start.25) | collective-permute-done | bytes 655392 | tf_op jit(solution)/shard_map/ppermute | solution.py:616
  654.1 8.6 %collective-permute-done.35 = bf16[80,1024]{1,0:T(8,128)(2,1)S(1)} collective-permute-done((bf16[80,1024]{1,0:T(8,128)(2,1)S(1)}, bf16[80,1024]{1,0:T(8,128)(2,1)S(1)}, u32[]{:S(2)}, u32[]{:S(2)}) %collective-permute-start.35) | collective-permute-done | bytes 163872 | tf_op jit(solution)/shard_map/ppermute | solution.py:616
  (281 shorter events, 239.4 us)
Async XLA Ops:
  25.0 46.9 %all-to-all-start = ((bf16[16,64,1024]{2,1,0:T(8,128)(2,1)}), bf16[16,64,1024]{2,1,0:T(8,128)(2,1)}, u32[]{:S(2)}, u32[]{:S(2)}) async-start(bf16[16,64,1024]{2,1,0:T(8,128)(2,1)} %get-tuple-element.42), calls=%async_computation | async-start | bytes 4194304 | tf_op jit(solution)/shard_map/all_to_all | solution.py:707
  217.2 365.9 %collective-permute-start.23 = (bf16[16,256,1024]{2,1,0:T(8,128)(2,1)}, bf16[16,256,1024]{2,1,0:T(8,128)(2,1)}, u32[]{:S(2)}, u32[]{:S(2)}) collective-permute-start(bf16[16,256,1024]{2,1,0:T(8,128)(2,1)} %pad_maximum_fusion), channel_id=1, source_target_pairs={{0,1},{1,0},{2,3},{3,2},{4,5},{5,4},{6,7},{7,6},{8,9},{9,8},{10,11... | collective-permute-start | bytes 25165832 | tf_op jit(solution)/shard_map/ppermute | solution.py:616
  320.6 16.9 %all-to-all-start.3 = ((bf16[16,2,128]{2,1,0:T(2,128)(2,1)}), bf16[16,2,128]{2,1,0:T(2,128)(2,1)S(1)}, u32[]{:S(2)}, u32[]{:S(2)}) async-start(bf16[16,2,128]{2,1,0:T(2,128)(2,1)} %reshape.355), calls=%async_computation.3 | async-start | bytes 16384 | tf_op jit(solution)/shard_map/all_to_all | solution.py:799
  344.6 177.2 %collective-permute-start.10 = (bf16[16,128,1024]{2,1,0:T(8,128)(2,1)}, bf16[16,128,1024]{2,1,0:T(8,128)(2,1)}, u32[]{:S(2)}, u32[]{:S(2)}) collective-permute-start(bf16[16,128,1024]{2,1,0:T(8,128)(2,1)} %pad_maximum_fusion.1), channel_id=1, source_target_pairs={{0,1},{1,0},{2,3},{3,2},{4,5},{5,4},{6,7},{7,6},{8,9},{9,8},{10,11... | collective-permute-start | bytes 12582920 | tf_op jit(solution)/shard_map/ppermute | solution.py:616
  347.4 170.3 %all-to-all-start.2 = ((bf16[16,64,1024]{2,1,0:T(8,128)(2,1)}), bf16[16,64,1024]{2,1,0:T(8,128)(2,1)}, u32[]{:S(2)}, u32[]{:S(2)}) async-start(bf16[16,64,1024]{2,1,0:T(8,128)(2,1)} %bitcast.16), calls=%async_computation.2 | async-start | bytes 4194304 | tf_op jit(solution)/shard_map/all_to_all | solution.py:787
  352.1 62.4 %collective-permute-start = (bf16[4,5120]{1,0:T(4,128)(2,1)S(1)}, bf16[4,5120]{1,0:T(4,128)(2,1)S(1)}, u32[]{:S(2)}, u32[]{:S(2)}) collective-permute-start(bf16[4,5120]{1,0:T(4,128)(2,1)S(1)} %pad_maximum_fusion.16), channel_id=1, source_target_pairs={{0,16},{2,18},{4,20},{6,22},{8,24},{10,26},{12,28},{14,30},{16,0},... | collective-permute-start | bytes 122888 | tf_op jit(solution)/shard_map/ppermute | solution.py:616
  355.3 69.7 %collective-permute-start.5 = (bf16[4,2048]{0,1:T(8,128)(2,1)S(1)}, bf16[4,2048]{0,1:T(8,128)(2,1)S(1)}, u32[]{:S(2)}, u32[]{:S(2)}) collective-permute-start(bf16[4,2048]{0,1:T(8,128)(2,1)S(1)} %copy.212), channel_id=1, source_target_pairs={{0,16},{2,18},{4,20},{6,22},{8,24},{10,26},{12,28},{14,30},{16,0},... | collective-permute-start | bytes 49160 | tf_op jit(solution)/shard_map/ppermute | solution.py:616
  426.7 14.7 %collective-permute-start.2 = (bf16[16,5120]{1,0:T(8,128)(2,1)S(1)}, bf16[16,5120]{1,0:T(8,128)(2,1)S(1)}, u32[]{:S(2)}, u32[]{:S(2)}) collective-permute-start(bf16[16,5120]{1,0:T(8,128)(2,1)S(1)} %pad_maximum_fusion.14), channel_id=1, source_target_pairs={{0,4},{2,6},{4,0},{6,2},{8,12},{10,14},{12,8},{14,10},{16,20},{18,... | collective-permute-start | bytes 491528 | tf_op jit(solution)/shard_map/ppermute | solution.py:616
  442.2 25.0 %collective-permute-start.3 = (bf16[32,5120]{1,0:T(8,128)(2,1)}, bf16[32,5120]{1,0:T(8,128)(2,1)S(1)}, u32[]{:S(2)}, u32[]{:S(2)}) collective-permute-start(bf16[32,5120]{1,0:T(8,128)(2,1)} %pad_maximum_fusion.9), channel_id=1, source_target_pairs={{0,2},{2,0},{4,6},{6,4},{8,10},{10,8},{12,14},{14,12},{16,18},{18,... | collective-permute-start | bytes 983048 | tf_op jit(solution)/shard_map/ppermute | solution.py:616
  467.2 29.7 %collective-permute-start.9 = (bf16[64,2048]{0,1:T(8,128)(2,1)}, bf16[64,2048]{0,1:T(8,128)(2,1)}, u32[]{:S(2)}, u32[]{:S(2)}) collective-permute-start(bf16[64,2048]{0,1:T(8,128)(2,1)} %concatenate.90), channel_id=1, source_target_pairs={{0,1},{1,0},{2,3},{3,2},{4,5},{5,4},{6,7},{7,6},{8,9},{9,8},{10,11... | collective-permute-start | bytes 786440 | tf_op jit(solution)/shard_map/ppermute | solution.py:616
  470.6 32.6 %collective-permute-start.4 = (bf16[64,5120]{1,0:T(8,128)(2,1)}, bf16[64,5120]{1,0:T(8,128)(2,1)}, u32[]{:S(2)}, u32[]{:S(2)}) collective-permute-start(bf16[64,5120]{1,0:T(8,128)(2,1)} %concatenate.85), channel_id=1, source_target_pairs={{0,1},{1,0},{2,3},{3,2},{4,5},{5,4},{6,7},{7,6},{8,9},{9,8},{10,11... | collective-permute-start | bytes 1966088 | tf_op jit(solution)/shard_map/ppermute | solution.py:616
  524.4 13.9 %collective-permute-start.11 = (bf16[2,2,2,32,1024]{4,3,2,1,0:T(8,128)(2,1)S(1)}, bf16[2,2,2,32,1024]{4,3,2,1,0:T(8,128)(2,1)S(1)}, u32[]{:S(2)}, u32[]{:S(2)}) collective-permute-start(bf16[2,2,2,32,1024]{4,3,2,1,0:T(8,128)(2,1)S(1)} %dynamic-slice_bitcast_fusion.13), channel_id=1, source_target_pairs={{0,2},{2,0},{4,6},{6,4},{8,10},{10,8},{12,14},{14,12},{16,18},{18,... | collective-permute-start | bytes 1572872 | tf_op jit(solution)/shard_map/ppermute | solution.py:616
  525.0 15.1 %collective-permute-start.15 = (bf16[2,2,2,32,1024]{4,3,2,1,0:T(8,128)(2,1)S(1)}, bf16[2,2,2,32,1024]{4,3,2,1,0:T(8,128)(2,1)S(1)}, u32[]{:S(2)}, u32[]{:S(2)}) collective-permute-start(bf16[2,2,2,32,1024]{4,3,2,1,0:T(8,128)(2,1)S(1)} %dynamic-slice_bitcast_fusion.12), channel_id=1, source_target_pairs={{0,4},{2,6},{4,0},{6,2},{8,12},{10,14},{12,8},{14,10},{16,20},{18,... | collective-permute-start | bytes 1572872 | tf_op jit(solution)/shard_map/ppermute | solution.py:616
  529.3 33.3 %collective-permute-start.19 = (bf16[2,2,2,64,1024]{4,3,2,1,0:T(8,128)(2,1)S(1)}, bf16[2,2,2,64,1024]{4,3,2,1,0:T(8,128)(2,1)S(1)}, u32[]{:S(2)}, u32[]{:S(2)}) collective-permute-start(bf16[2,2,2,64,1024]{4,3,2,1,0:T(8,128)(2,1)S(1)} %dynamic-slice_bitcast_fusion.5), channel_id=1, source_target_pairs={{0,8},{2,10},{4,12},{6,14},{8,0},{10,2},{12,4},{14,6},{16,24},{18,... | collective-permute-start | bytes 3145736 | tf_op jit(solution)/shard_map/ppermute | solution.py:616
  540.4 20.5 %collective-permute-start.16 = (bf16[2,2,32,1024]{3,2,1,0:T(8,128)(2,1)S(1)}, bf16[2,2,32,1024]{3,2,1,0:T(8,128)(2,1)S(1)}, u32[]{:S(2)}, u32[]{:S(2)}) collective-permute-start(bf16[2,2,32,1024]{3,2,1,0:T(8,128)(2,1)S(1)} %dynamic-slice_bitcast_fusion.18), channel_id=1, source_target_pairs={{0,8},{2,10},{4,12},{6,14},{8,0},{10,2},{12,4},{14,6},{16,24},{18,... | collective-permute-start | bytes 786440 | tf_op jit(solution)/shard_map/ppermute | solution.py:616
  546.1 17.5 %collective-permute-start.13 = (bf16[2,32,1024]{2,1,0:T(8,128)(2,1)S(1)}, bf16[2,32,1024]{2,1,0:T(8,128)(2,1)S(1)}, u32[]{:S(2)}, u32[]{:S(2)}) collective-permute-start(bf16[2,32,1024]{2,1,0:T(8,128)(2,1)S(1)} %dynamic-slice_bitcast_fusion.25), channel_id=1, source_target_pairs={{0,8},{2,10},{4,12},{6,14},{8,0},{10,2},{12,4},{14,6},{16,24},{18,... | collective-permute-start | bytes 393224 | tf_op jit(solution)/shard_map/ppermute | solution.py:616
  576.8 18.9 %collective-permute-start.18 = (bf16[32,1024]{1,0:T(8,128)(2,1)S(1)}, bf16[32,1024]{1,0:T(8,128)(2,1)S(1)}, u32[]{:S(2)}, u32[]{:S(2)}) collective-permute-start(bf16[32,1024]{1,0:T(8,128)(2,1)S(1)} %dynamic-slice_bitcast_fusion.26), channel_id=1, source_target_pairs={{0,16},{2,18},{4,20},{6,22},{8,24},{10,26},{12,28},{14,30},{16,0},... | collective-permute-start | bytes 196616 | tf_op jit(solution)/shard_map/ppermute | solution.py:616
  588.1 25.5 %collective-permute-start.32 = (bf16[2,2,2,80,1024]{4,3,0,1,2:T(8,128)(2,1)S(1)}, bf16[2,2,2,80,1024]{4,3,0,1,2:T(8,128)(2,1)S(1)}, u32[]{:S(2)}, u32[]{:S(2)}) collective-permute-start(bf16[2,2,2,80,1024]{4,3,0,1,2:T(8,128)(2,1)S(1)} %bitcast.271), channel_id=1, source_target_pairs={{0,2},{2,0},{4,6},{6,4},{8,10},{10,8},{12,14},{14,12},{16,18},{18,... | collective-permute-start | bytes 3932168 | tf_op jit(solution)/shard_map/ppermute | solution.py:616
  589.2 29.7 %collective-permute-start.24 = (bf16[2,2,2,80,1024]{4,3,2,1,0:T(8,128)(2,1)S(1)}, bf16[2,2,2,80,1024]{4,3,2,1,0:T(8,128)(2,1)S(1)}, u32[]{:S(2)}, u32[]{:S(2)}) collective-permute-start(bf16[2,2,2,80,1024]{4,3,2,1,0:T(8,128)(2,1)S(1)} %dynamic-slice_bitcast_fusion.4), channel_id=1, source_target_pairs={{0,4},{2,6},{4,0},{6,2},{8,12},{10,14},{12,8},{14,10},{16,20},{18,... | collective-permute-start | bytes 3932168 | tf_op jit(solution)/shard_map/ppermute | solution.py:616
  594.4 37.4 %collective-permute-start.28 = (bf16[2,2,2,96,1024]{4,3,0,1,2:T(8,128)(2,1)S(1)}, bf16[2,2,2,96,1024]{4,3,0,1,2:T(8,128)(2,1)S(1)}, u32[]{:S(2)}, u32[]{:S(2)}) collective-permute-start(bf16[2,2,2,96,1024]{4,3,0,1,2:T(8,128)(2,1)S(1)} %bitcast.270), channel_id=1, source_target_pairs={{0,8},{2,10},{4,12},{6,14},{8,0},{10,2},{12,4},{14,6},{16,24},{18,... | collective-permute-start | bytes 4718600 | tf_op jit(solution)/shard_map/ppermute | solution.py:616
  614.3 19.4 %collective-permute-start.33 = (bf16[2,2,80,1024]{3,2,0,1:T(8,128)(2,1)S(1)}, bf16[2,2,80,1024]{3,2,0,1:T(8,128)(2,1)S(1)}, u32[]{:S(2)}, u32[]{:S(2)}) collective-permute-start(bf16[2,2,80,1024]{3,2,0,1:T(8,128)(2,1)S(1)} %dynamic-slice_bitcast_fusion.9), channel_id=1, source_target_pairs={{0,4},{2,6},{4,0},{6,2},{8,12},{10,14},{12,8},{14,10},{16,20},{18,... | collective-permute-start | bytes 1966088 | tf_op jit(solution)/shard_map/ppermute | solution.py:616
  619.5 24.0 %collective-permute-start.25 = (bf16[2,2,80,1024]{3,2,1,0:T(8,128)(2,1)S(1)}, bf16[2,2,80,1024]{3,2,1,0:T(8,128)(2,1)S(1)}, u32[]{:S(2)}, u32[]{:S(2)}) collective-permute-start(bf16[2,2,80,1024]{3,2,1,0:T(8,128)(2,1)S(1)} %dynamic-slice_bitcast_fusion.10), channel_id=1, source_target_pairs={{0,8},{2,10},{4,12},{6,14},{8,0},{10,2},{12,4},{14,6},{16,24},{18,... | collective-permute-start | bytes 1966088 | tf_op jit(solution)/shard_map/ppermute | solution.py:616
  632.6 18.3 %collective-permute-start.29 = (bf16[2,2,96,1024]{3,2,0,1:T(8,128)(2,1)S(1)}, bf16[2,2,96,1024]{3,2,0,1:T(8,128)(2,1)S(1)}, u32[]{:S(2)}, u32[]{:S(2)}) collective-permute-start(bf16[2,2,96,1024]{3,2,0,1:T(8,128)(2,1)S(1)} %dynamic-slice_bitcast_fusion.8), channel_id=1, source_target_pairs={{0,2},{2,0},{4,6},{6,4},{8,10},{10,8},{12,14},{14,12},{16,18},{18,... | collective-permute-start | bytes 2359304 | tf_op jit(solution)/shard_map/ppermute | solution.py:616
  633.9 15.7 %collective-permute-start.34 = (bf16[2,80,1024]{2,1,0:T(8,128)(2,1)S(1)}, bf16[2,80,1024]{2,1,0:T(8,128)(2,1)S(1)}, u32[]{:S(2)}, u32[]{:S(2)}) collective-permute-start(bf16[2,80,1024]{2,1,0:T(8,128)(2,1)S(1)} %dynamic-slice_bitcast_fusion.15), channel_id=1, source_target_pairs={{0,8},{2,10},{4,12},{6,14},{8,0},{10,2},{12,4},{14,6},{16,24},{18,... | collective-permute-start | bytes 983048 | tf_op jit(solution)/shard_map/ppermute | solution.py:616
  (52 other events, 638.9 us)

commit v2 on v1

--- a/solution.py
+++ b/solution.py
@@ -16,6 +16,7 @@
 BLK = 256
 TILE = 16
 VMEM_LIMIT = 58 * 2**20
+BACK_ROUNDS = 3
 BF16 = jnp.bfloat16
 F32 = jnp.float32
 
@@ -45,30 +46,14 @@
     ) * inverse
 
 
-def regroup_kernel(
-    len_ref, buck_ref, me_ref, x_ref, cond_ref,
-    send_ref, scond_ref, seg_ref, src_ref, cidx_ref,
-    off_ref, slot_ref, cond_in, cond_out, *, wide, slots,
-):
-    places = len_ref.shape[0]
-    cells = send_ref.shape[1]
-    send_ref[...] = jnp.zeros_like(send_ref)
-    cond_out[...] = jnp.zeros_like(cond_out)
-    cond_in[...] = cond_ref[...].astype(F32)
+def each_place(len_ref, buck_ref, off_ref, slot_ref, wide, visit):
     for i in range(wide):
         off_ref[i] = 0
         slot_ref[i] = 0
-    for i in range(seg_ref.shape[0]):
-        seg_ref[i] = -1
-
-    @pl.loop(0, src_ref.shape[0])
-    def _(i):
-        src_ref[i] = -1
 
     def place(j, offset):
         units = len_ref[j] // wide
         b = buck_ref[j]
-        cidx_ref[j] = -1
 
         @pl.when(units > 0)
         def _():
@@ -76,25 +61,56 @@
             slot = slot_ref[b]
             off_ref[b] = start + units
             slot_ref[b] = slot + 1
-            cidx_ref[j] = b * slots + slot
-            cond_out[pl.ds(b * slots + slot, 1), :] = cond_in[pl.ds(j, 1), :]
-
-            @pl.loop(0, units // TILE)
+            visit(j, b, units, offset, start, slot)
+
+        return offset + units
+
+    lax.fori_loop(0, len_ref.shape[0], place, 0)
+
+
+def regroup_rows_kernel(len_ref, buck_ref, x_ref, send_ref, src_ref, off_ref, slot_ref, *, wide):
+    cells = send_ref.shape[1]
+    send_ref[...] = jnp.zeros_like(send_ref)
+
+    @pl.loop(0, src_ref.shape[0])
+    def _(i):
+        src_ref[i] = -1
+
+    def visit(j, b, units, offset, start, slot):
+        @pl.loop(0, units // TILE)
+        def _(t):
+            a = pl.multiple_of(offset + t * TILE, TILE)
+            c = pl.multiple_of(start + t * TILE, TILE)
+            send_ref[b, pl.ds(c, TILE), :] = x_ref[pl.ds(a, TILE), :]
+            src_ref[a // TILE] = (b * cells + c) // TILE
+
+    each_place(len_ref, buck_ref, off_ref, slot_ref, wide, visit)
+
+
+def regroup_cond_kernel(
+    len_ref, buck_ref, me_ref, cond_ref, scond_ref, seg_ref, cidx_ref,
+    off_ref, slot_ref, cond_in, cond_out, *, wide, slots,
+):
+    cond_out[...] = jnp.zeros_like(cond_out)
+    cond_in[...] = cond_ref[...].astype(F32)
+    for i in range(seg_ref.shape[0]):
+        seg_ref[i] = -1
+
+    @pl.loop(0, cidx_ref.shape[0])
+    def _(j):
+        cidx_ref[j] = -1
+
+    def visit(j, b, units, offset, start, slot):
+        cidx_ref[j] = b * slots + slot
+        cond_out[pl.ds(b * slots + slot, 1), :] = cond_in[pl.ds(j, 1), :]
+
+        @pl.when(b == me_ref[0])
+        def _():
+            @pl.loop(0, units * wide // BLK)
             def _(t):
-                a = pl.multiple_of(offset + t * TILE, TILE)
-                c = pl.multiple_of(start + t * TILE, TILE)
-                send_ref[b, pl.ds(c, TILE), :] = x_ref[pl.ds(a, TILE), :]
-                src_ref[a // TILE] = (b * cells + c) // TILE
-
-            @pl.when(b == me_ref[0])
-            def _():
-                @pl.loop(0, units * wide // BLK)
-                def _(t):
-                    seg_ref[start * wide // BLK + t] = slot
-
-        return offset + units
-
-    lax.fori_loop(0, places, place, 0)
+                seg_ref[start * wide // BLK + t] = slot
+
+    each_place(len_ref, buck_ref, off_ref, slot_ref, wide, visit)
     scond_ref[...] = cond_out[...].astype(BF16)
 
 
@@ -104,30 +120,35 @@
     slots = places // wide
     smem = pl.BlockSpec(memory_space=pltpu.SMEM)
     vmem = pl.BlockSpec(memory_space=pltpu.VMEM)
-    return pl.pallas_call(
-        functools.partial(regroup_kernel, wide=wide, slots=slots),
-        in_specs=[smem, smem, smem, vmem, vmem],
-        out_specs=[vmem, vmem, smem, smem, smem],
+    counters = [pltpu.SMEM((wide,), jnp.int32), pltpu.SMEM((wide,), jnp.int32)]
+    scond, seg, cidx = pl.pallas_call(
+        functools.partial(regroup_cond_kernel, wide=wide, slots=slots),
+        in_specs=[smem, smem, smem, vmem],
+        out_specs=[vmem, smem, smem],
+        out_shape=[
+            jax.ShapeDtypeStruct((places, part), BF16),
+            jax.ShapeDtypeStruct((rows // BLK,), jnp.int32),
+            jax.ShapeDtypeStruct((places,), jnp.int32),
+        ],
+        scratch_shapes=counters + [pltpu.VMEM((places, part), F32), pltpu.VMEM((places, part), F32)],
+        compiler_params=params(),
+    )(lens, buck, me, cond)
+    send, src = pl.pallas_call(
+        functools.partial(regroup_rows_kernel, wide=wide),
+        in_specs=[smem, smem, vmem],
+        out_specs=[vmem, smem],
         out_shape=[
             jax.ShapeDtypeStruct((wide, rows // wide, feat), BF16),
-            jax.ShapeDtypeStruct((places, part), BF16),
-            jax.ShapeDtypeStruct((rows // BLK,), jnp.int32),
             jax.ShapeDtypeStruct((rows // TILE,), jnp.int32),
-            jax.ShapeDtypeStruct((places,), jnp.int32),
-        ],
-        scratch_shapes=[
-            pltpu.SMEM((wide,), jnp.int32),
-            pltpu.SMEM((wide,), jnp.int32),
-            pltpu.VMEM((places, part), F32),
-            pltpu.VMEM((places, part), F32),
-        ],
-        compiler_params=params(),
-    )(lens, buck, me, x_src, cond)
-
-
-def restore_kernel(src_ref, cidx_ref, back_ref, bcond_ref, dx_ref, dcond_ref, cond_in, cond_out):
-    cond_in[...] = bcond_ref[...].astype(F32)
-
+        ],
+        scratch_shapes=counters,
+        compiler_params=params(),
+        cost_estimate=pl.CostEstimate(flops=0, bytes_accessed=16 * 2**20, transcendentals=0),
+    )(lens, buck, x_src)
+    return send, scond, seg, src, cidx
+
+
+def restore_kernel(src_ref, back_ref, dx_ref):
     @pl.loop(0, src_ref.shape[0])
     def _(i):
         at = src_ref[i]
@@ -136,29 +157,16 @@
             at >= 0, rows, jnp.zeros_like(rows)
         )
 
-    @pl.loop(0, cidx_ref.shape[0])
-    def _(j):
-        at = cidx_ref[j]
-        row = cond_in[pl.ds(jnp.maximum(at, 0), 1), :]
-        cond_out[pl.ds(j, 1), :] = jnp.where(at >= 0, row, 0.0)
-
-    dcond_ref[...] = cond_out[...].astype(BF16)
-
-
-def restore(src, cidx, back, bcond):
-    smem = pl.BlockSpec(memory_space=pltpu.SMEM)
+
+def restore(src, back):
     vmem = pl.BlockSpec(memory_space=pltpu.VMEM)
     return pl.pallas_call(
         restore_kernel,
-        in_specs=[smem, smem, vmem, vmem],
-        out_specs=[vmem, vmem],
-        out_shape=[
-            jax.ShapeDtypeStruct(back.shape, BF16),
-            jax.ShapeDtypeStruct(bcond.shape, BF16),
-        ],
-        scratch_shapes=[pltpu.VMEM(bcond.shape, F32), pltpu.VMEM(bcond.shape, F32)],
-        compiler_params=params(),
-    )(src, cidx, back, bcond)
+        in_specs=[pl.BlockSpec(memory_space=pltpu.SMEM), vmem],
+        out_specs=vmem,
+        out_shape=jax.ShapeDtypeStruct(back.shape, BF16),
+        compiler_params=params(),
+    )(src, back)
 
 
 def regroup_any(x_src, cond, lens, buck, me, wide):
@@ -203,11 +211,9 @@
     return send, scond, seg.astype(jnp.int32), src - 1, cidx
 
 
-def restore_any(src, cidx, back, bcond):
+def restore_any(src, back):
     dx = jnp.take(back, jnp.maximum(src, 0), axis=0)
-    dcond = jnp.take(bcond, jnp.maximum(cidx, 0), axis=0)
-    zero = jnp.zeros((), BF16)
-    return jnp.where(src[:, None] >= 0, dx, zero), jnp.where(cidx[:, None] >= 0, dcond, zero)
+    return jnp.where(src[:, None] >= 0, dx, jnp.zeros((), BF16))
 
 
 def qkv_kernel(x_ref, mod_ref, w_ref, b_ref, q_ref, a_ref):
@@ -355,32 +361,105 @@
         out_ref[2, hs, :] = grad_v.astype(BF16)
 
 
-def attend_back(seg, qkv_t, o_t, do_t, lse, heads=2):
+def attend_back(seg, qkv_t, o_t, do_t, lse, first, count, heads=2):
     feat3, rows = qkv_t.shape
     feat = feat3 // 3
     span = heads * HEAD_DIM
     groups = feat // span
+    at = first // heads
     return pl.pallas_call(
         functools.partial(attend_back_kernel, blocks=rows // BLK, heads=heads),
         grid_spec=pltpu.PrefetchScalarGridSpec(
             num_scalar_prefetch=1,
-            grid=(groups,),
+            grid=(count // heads,),
             in_specs=[
-                pl.BlockSpec((span, rows), lambda g, s: (g, 0)),
-                pl.BlockSpec((span, rows), lambda g, s: (groups + g, 0)),
-                pl.BlockSpec((span, rows), lambda g, s: (2 * groups + g, 0)),
-                pl.BlockSpec((span, rows), lambda g, s: (g, 0)),
-                pl.BlockSpec((span, rows), lambda g, s: (g, 0)),
-                pl.BlockSpec((heads, 1, rows), lambda g, s: (g, 0, 0)),
+                pl.BlockSpec((span, rows), lambda g, s: (at + g, 0)),
+                pl.BlockSpec((span, rows), lambda g, s: (groups + at + g, 0)),
+                pl.BlockSpec((span, rows), lambda g, s: (2 * groups + at + g, 0)),
+                pl.BlockSpec((span, rows), lambda g, s: (at + g, 0)),
+                pl.BlockSpec((span, rows), lambda g, s: (at + g, 0)),
+                pl.BlockSpec((heads, 1, rows), lambda g, s: (at + g, 0, 0)),
             ],
             out_specs=pl.BlockSpec((3, span, rows), lambda g, s: (0, g, 0)),
         ),
-        out_shape=jax.ShapeDtypeStruct((3, feat, rows), BF16),
+        out_shape=jax.ShapeDtypeStruct((3, count * HEAD_DIM, rows), BF16),
         compiler_params=params(),
         cost_estimate=pl.CostEstimate(
-            flops=24 * feat * rows * rows, bytes_accessed=16 * 2**20, transcendentals=16 * rows * rows
+            flops=24 * count * HEAD_DIM * rows * rows,
+            bytes_accessed=count * 2**20,
+            transcendentals=count * rows * rows,
         ),
     )(seg, qkv_t, qkv_t, qkv_t, o_t, do_t, lse)
+
+
+class Halves:
+    def __init__(self, wide, part):
+        self.wide, self.part = wide, part
+        self.split = part % TILE == 0
+
+    def shapes(self, between, columns):
+        if self.split:
+            shape = (self.wide,) + between + (self.part, columns)
+            return [jax.ShapeDtypeStruct(shape, BF16)] * 2
+        return [jax.ShapeDtypeStruct(between + (2 * self.wide * self.part, columns), BF16)]
+
+    def specs(self, between, columns, index):
+        ones = (1,) * between
+        if self.split:
+            return [
+                pl.BlockSpec(
+                    (self.wide,) + ones + (self.part, columns),
+                    lambda *g: (0,) + index(*g)[:-1] + (0, index(*g)[-1]),
+                )
+            ] * 2
+        return [
+            pl.BlockSpec(
+                ones + (2 * self.wide * self.part, columns),
+                lambda *g: index(*g)[:-1] + (0, index(*g)[-1]),
+            )
+        ]
+
+    def store(self, half, value, refs):
+        if not self.split:
+            refs[0][...] = value.astype(BF16).reshape(refs[0].shape)
+            return
+        value = value.reshape(value.shape[0] // (2 * self.part), 2, self.part, value.shape[1])
+        even, odd = value[:, 0], value[:, 1]
+        refs[0][...] = jnp.where(half == 0, odd, even).astype(BF16).reshape(refs[0].shape)
+        refs[1][...] = jnp.where(half == 0, even, odd).astype(BF16).reshape(refs[1].shape)
+
+    def finish(self, arrays):
+        if self.split:
+            return [a.reshape(self.wide, -1, a.shape[-1]) for a in arrays]
+        return arrays
+
+
+def qkv_grad_kernel(half_ref, a_ref, *refs, pieces, halves):
+    ins, outs, sums_ref = refs[:pieces], refs[pieces:-1], refs[-1]
+    ones = jnp.ones((8, a_ref.shape[1]), BF16)
+    value = jnp.concatenate([dot(a_ref[...], r[0], 1, 1) for r in ins], axis=1)
+    halves.store(half_ref[0], value, outs)
+    sums_ref[0] = jnp.concatenate([dot(ones, r[0], 1, 1) for r in ins], axis=1)
+
+
+def qkv_grad(half, a1_t, dqkv, halves):
+    feat, rows = a1_t.shape
+    span = dqkv[0].shape[1]
+    columns = span * len(dqkv)
+    out = pl.pallas_call(
+        functools.partial(qkv_grad_kernel, pieces=len(dqkv), halves=halves),
+        grid=(3,),
+        in_specs=[pl.BlockSpec(memory_space=pltpu.SMEM), whole(feat, rows)]
+        + [pl.BlockSpec((1, span, rows), lambda i: (i, 0, 0))] * len(dqkv),
+        out_specs=halves.specs(1, columns, lambda i: (i, 0))
+        + [pl.BlockSpec((1, 8, columns), lambda i: (i, 0, 0))],
+        out_shape=halves.shapes((3,), columns) + [jax.ShapeDtypeStruct((3, 8, columns), F32)],
+        compiler_params=params(),
+        cost_estimate=pl.CostEstimate(
+            flops=6 * feat * rows * columns, bytes_accessed=12 * 2**20, transcendentals=0
+        ),
+    )(half, a1_t, *dqkv)
+    return halves.finish(out[:-1]), out[-1][:, 0, :]
 
 
 def proj_kernel(o_ref, w_ref, b_ref, x_ref, mod_ref, attn_ref, x1_ref, a_ref, at_ref):
@@ -435,9 +514,12 @@
 
 
 def mlp_kernel(
-    a_ref, at_ref, df_ref, dg_ref, w1_ref, w2_ref, b1_ref,
-    f_ref, da_ref, d1_ref, d2_ref, db_ref, g_ref, du_ref,
+    half_ref, a_ref, at_ref, df_ref, dg_ref, w1_ref, w2_ref, b1_ref, *refs, first, second
 ):
+    f_ref, da_ref, db_ref = refs[:3]
+    g_ref, du_ref = refs[-2:]
+    outs = refs[3:-2]
+    outs_one, outs_two = outs[: len(outs) // 2], outs[len(outs) // 2 :]
     step = pl.program_id(0)
     rows = a_ref.shape[0]
 
@@ -460,24 +542,35 @@
         f_ref[rs, :] += dot(g, w2, 1, 0)
         da_ref[rs, :] += dot(du, w1, 1, 1)
     db_ref[...] = bias
-    du = du_ref[...]
-    d1_ref[0] = dot(at_ref[...], du, 1, 0).astype(BF16)
-    d2_ref[...] = dot(g_ref[...], df_ref[...], 0, 0).astype(BF16)
-
-
-def mlp(a2, a2_t, df, dg, w1, w2, b1, width=512):
+    first.store(half_ref[0], dot(at_ref[...], du_ref[...], 1, 0), outs_one)
+    second.store(half_ref[0], dot(g_ref[...], df_ref[...], 0, 0), outs_two)
+
+
+def mlp(half, a2, a2_t, df, dg, w1, w2, b1, halves, width=512):
     rows, feat = a2.shape
     hidden = w1.shape[1]
     per = feat // width
+    wide = halves.wide
+    part = hidden // (2 * wide)
+    first = halves
+    second = Halves(wide, part)
+    second.split = halves.split
     one = pl.Buffered(1)
 
     def fixed(*shape):
         return pl.BlockSpec(shape, lambda j: (0,) * len(shape), pipeline_mode=one)
 
-    return pl.pallas_call(
-        mlp_kernel,
+    if halves.split:
+        two_specs = [pl.BlockSpec((width // (2 * part), part, feat), lambda j: (j, 0, 0))] * 2
+        two_shapes = [jax.ShapeDtypeStruct((wide, part, feat), BF16)] * 2
+    else:
+        two_specs = [pl.BlockSpec((width, feat), lambda j: (j, 0))]
+        two_shapes = [jax.ShapeDtypeStruct((hidden, feat), BF16)]
+    out = pl.pallas_call(
+        functools.partial(mlp_kernel, first=first, second=second),
         grid=(hidden // width,),
         in_specs=[
+            pl.BlockSpec(memory_space=pltpu.SMEM),
             fixed(rows, feat),
             fixed(feat, rows),
             fixed(rows, feat),
@@ -486,33 +579,34 @@
             pl.BlockSpec((width, feat), lambda j: (j, 0)),
             pl.BlockSpec((1, width), lambda j: (0, j)),
         ],
-        out_specs=[
-            whole(rows, feat),
-            whole(rows, feat),
-            pl.BlockSpec((1, feat, width), lambda j: (j // per, 0, j % per)),
-            pl.BlockSpec((width, feat), lambda j: (j, 0)),
-            pl.BlockSpec((1, width), lambda j: (0, j)),
-        ],
+        out_specs=[whole(rows, feat), whole(rows, feat), pl.BlockSpec((1, width), lambda j: (0, j))]
+        + halves.specs(1, width, lambda j: (j // per, j % per))
+        + two_specs,
         out_shape=[
             jax.ShapeDtypeStruct((rows, feat), F32),
             jax.ShapeDtypeStruct((rows, feat), F32),
-            jax.ShapeDtypeStruct((hidden // feat, feat, feat), BF16),
-            jax.ShapeDtypeStruct((hidden, feat), BF16),
             jax.ShapeDtypeStruct((1, hidden), F32),
-        ],
+        ]
+        + halves.shapes((hidden // feat,), feat)
+        + two_shapes,
         scratch_shapes=[pltpu.VMEM((rows, width), BF16), pltpu.VMEM((rows, width), BF16)],
         compiler_params=params(),
         cost_estimate=pl.CostEstimate(
             flops=10 * rows * feat * hidden, bytes_accessed=64 * 2**20, transcendentals=rows * hidden
         ),
-    )(a2, a2_t, df, dg, w1, w2, b1)
+    )(half, a2, a2_t, df, dg, w1, w2, b1)
+    f, da2, bias = out[:3]
+    rest = out[3:]
+    count = len(rest) // 2
+    return f, da2, bias, first.finish(rest[:count]), second.finish(rest[count:])
 
 
 def middle_kernel(
-    f_ref, b2_ref, x1_ref, attn_ref, dy_ref, da_ref, mod_ref, o_ref, w_ref,
-    y_ref, dx_ref, do_ref, dw_ref, db_ref, sums_ref, acc_ref,
+    half_ref, f_ref, b2_ref, x1_ref, attn_ref, dy_ref, da_ref, mod_ref, o_ref, w_ref,
+    y_ref, dx_ref, do_ref, db_ref, sums_ref, *rest, halves,
 ):
     k = pl.program_id(0)
+    outs, acc_ref = rest[:-1], rest[-1]
 
     @pl.when(k == 0)
     def _():
@@ -538,47 +632,54 @@
 
     @pl.when(k == pl.num_programs(0) - 1)
     def _():
-        dw_ref[...] = acc_ref[...].astype(BF16)
-
-
-def middle(f, b2, x1, attn, dy, da2, mod_blocks, o_t, w_proj):
+        halves.store(half_ref[0], acc_ref[...], outs)
+
+
+def middle(half, f, b2, x1, attn, dy, da2, mod_blocks, o_t, w_proj, halves):
     rows, feat = x1.shape
     by_row = pl.BlockSpec((BLK, feat), lambda k: (k, 0))
     by_column = pl.BlockSpec((feat, BLK), lambda k: (0, k))
     blocks = rows // BLK
-    return pl.pallas_call(
-        middle_kernel,
+    out = pl.pallas_call(
+        functools.partial(middle_kernel, halves=halves),
         grid=(blocks,),
         in_specs=[
+            pl.BlockSpec(memory_space=pltpu.SMEM),
             by_row, whole(1, feat), by_row, by_row, by_row, by_row,
             pl.BlockSpec((1, 6, feat), lambda k: (k, 0, 0)),
             by_column, whole(feat, feat),
         ],
         out_specs=[
-            by_row, by_row, by_column, whole(feat, feat), whole(1, feat),
+            by_row, by_row, by_column, whole(1, feat),
             pl.BlockSpec((1, 4, feat), lambda k: (k, 0, 0)),
-        ],
+        ] + halves.specs(0, feat, lambda k: (0,)),
         out_shape=[
             jax.ShapeDtypeStruct((rows, feat), BF16),
             jax.ShapeDtypeStruct((rows, feat), F32),
             jax.ShapeDtypeStruct((feat, rows), BF16),
-            jax.ShapeDtypeStruct((feat, feat), BF16),
             jax.ShapeDtypeStruct((1, feat), F32),
             jax.ShapeDtypeStruct((blocks, 4, feat), F32),
-        ],
+        ]
+        + halves.shapes((), feat),
         scratch_shapes=[pltpu.VMEM((feat, feat), F32)],
         compiler_params=params(),
         cost_estimate=pl.CostEstimate(
             flops=4 * feat * feat * rows, bytes_accessed=32 * 2**20, transcendentals=0
         ),
-    )(f, b2, x1, attn, dy, da2, mod_blocks, o_t, w_proj)
-
-
-def rows_back_kernel(dq_ref, w_ref, x_ref, dx_ref, mod_ref, out_ref, sums_ref):
+    )(half, f, b2, x1, attn, dy, da2, mod_blocks, o_t, w_proj)
+    return tuple(out[:5]) + (halves.finish(out[5:]),)
+
+
+def rows_back_kernel(w_ref, x_ref, dx_ref, mod_ref, *refs):
+    out_ref, sums_ref = refs[-2:]
     feat = x_ref.shape[-1]
-    da = dot(dq_ref[0], w_ref[0:feat, :], 0, 0)
-    for i in (1, 2):
-        da = da + dot(dq_ref[i], w_ref[i * feat : (i + 1) * feat, :], 0, 0)
+    span = refs[0].shape[1]
+    da = None
+    for i in range(3):
+        for g, ref in enumerate(refs[:-2]):
+            at = i * feat + g * span
+            more = dot(ref[i], w_ref[at : at + span, :], 0, 0)
+            da = more if da is None else da + more
     normed, inverse = norm_parts(x_ref[...].reshape(BLK, feat).astype(F32))
     out = dx_ref[...] + norm_back(da * (1.0 + mod_ref[0, 1:2, :]), normed, inverse)
     out_ref[...] = out.astype(BF16).reshape(out_ref.shape)
@@ -586,19 +687,20 @@
     sums_ref[0, 1:2, :] = jnp.sum(da * normed, axis=0, keepdims=True)
 
 
-def rows_back(dqkv_t, w_t, x_view, dx1, mod_blocks):
+def rows_back(dqkv, w_t, x_view, dx1, mod_blocks):
     rows, feat = dx1.shape
     blocks = rows // BLK
+    span = dqkv[0].shape[1]
     return pl.pallas_call(
         rows_back_kernel,
         grid=(blocks,),
         in_specs=[
-            pl.BlockSpec((3, feat, BLK), lambda k: (0, 0, k)),
             whole(3 * feat, feat),
             row_spec(x_view.shape),
             pl.BlockSpec((BLK, feat), lambda k: (k, 0)),
             pl.BlockSpec((1, 6, feat), lambda k: (k, 0, 0)),
-        ],
+        ]
+        + [pl.BlockSpec((3, span, BLK), lambda k: (0, 0, k))] * len(dqkv),
         out_specs=[row_spec(x_view.shape), pl.BlockSpec((1, 2, feat), lambda k: (k, 0, 0))],
         out_shape=[
             jax.ShapeDtypeStruct(x_view.shape, BF16),
@@ -608,20 +710,67 @@
         cost_estimate=pl.CostEstimate(
             flops=6 * feat * feat * rows, bytes_accessed=20 * 2**20, transcendentals=0
         ),
-    )(dqkv_t, w_t, x_view, dx1, mod_blocks)
+    )(w_t, x_view, dx1, mod_blocks, *dqkv)
+
+
+def mod_grad_kernel(
+    ids_ref, one_ref, two_ref, w_ref, gw_ref, gb_ref, dact_ref, bias_ref, act_ref, *, part, slots
+):
+    early = one_ref.shape[1]
+    feat = early // 2
+    rows = one_ref.shape[0]
+    first = lax.broadcasted_iota(jnp.int32, (rows, 1), 0) % (2 * slots) < slots
+    act = pltpu.roll(two_ref[:, :feat].astype(F32), rows - slots, 0)
+    act_ref[...] = jnp.where(first, act, 0.0).T
+    act = act_ref[pl.ds(pl.multiple_of(ids_ref[1] * part, 8), part), :].astype(BF16)
+    one, two = one_ref[...], two_ref[...]
+    gw_ref[:, :early] = dot(act, one, 1, 0)
+    gw_ref[:, early:] = dot(act, two, 1, 0)
+    one_wide = one.astype(F32)
+    gb_ref[:, :early] = jnp.sum(jnp.where(first, one_wide, 0.0), axis=0, keepdims=True)
+    gb_ref[:, early:] = jnp.sum(jnp.where(first, two.astype(F32), 0.0), axis=0, keepdims=True)
+    dact_ref[...] = dot(one, w_ref[:, :early], 1, 1) + dot(two, w_ref[:, early:], 1, 1)
+    bias_ref[...] = jnp.sum(one_wide.reshape(rows // (2 * slots), 2 * slots, early), axis=0)
+
+
+def mod_grad(group, me, one, two, w_mod, part, share, slots):
+    count, early = one.shape
+    feat, columns = w_mod.shape
+
+    def fixed(i, ids):
+        return (0, 0)
+
+    return pl.pallas_call(
+        functools.partial(mod_grad_kernel, part=part, slots=slots),
+        grid_spec=pltpu.PrefetchScalarGridSpec(
+            num_scalar_prefetch=1,
+            grid=(1,),
+            in_specs=[
+                pl.BlockSpec(one.shape, fixed),
+                pl.BlockSpec(two.shape, fixed),
+                pl.BlockSpec((share, columns), lambda i, ids: (ids[0], 0)),
+            ],
+            out_specs=[
+                pl.BlockSpec((part, columns), fixed),
+                pl.BlockSpec((1, columns), fixed),
+                pl.BlockSpec((count, share), fixed),
+                pl.BlockSpec((2 * slots, early), fixed),
+            ],
+            scratch_shapes=[pltpu.VMEM((feat, count), F32)],
+        ),
+        out_shape=[
+            jax.ShapeDtypeStruct((part, columns), F32),
+            jax.ShapeDtypeStruct((1, columns), F32),
+            jax.ShapeDtypeStruct((count, share), F32),
+            jax.ShapeDtypeStruct((2 * slots, early), F32),
+        ],
+        compiler_params=params(),
+    )(jnp.stack([group, me]), one, two, w_mod)
 
 
 def swap(values, axis, bit):
     count = lax.axis_size(axis)
     return lax.ppermute(values, axis, [(i, i ^ bit) for i in range(count)])
-
-
-def add_low(left, right):
-    return (left.astype(F32) + right.astype(F32)).astype(BF16)
-
-
-def pick(values, index, dim):
-    return lax.dynamic_index_in_dim(values, index, dim, keepdims=False)
 
 
 def bits_of(wide):
@@ -634,37 +783,133 @@
     return [near[i:] + near[:i] + far for i in range(3)]
 
 
-def scatter_chain(values, order):
-    wide = values.shape[0]
-    bits = bits_of(wide)
-    values = values.reshape((2,) * len(bits) + values.shape[1:])
-    dims = list(reversed(bits))
-    me = lax.axis_index("wide")
-    for bit in order:
-        dim = dims.index(bit)
-        own = (me // bit) % 2
-        got = swap(pick(values, 1 - own, dim), "wide", bit)
-        values = add_low(pick(values, own, dim), got)
-        dims.pop(dim)
-    return values
-
-
-def scatter_sum(send, keep):
-    got = swap(send, "narrow", 1)
-    wide, rows = keep.shape[:2]
-    third = rows // 3 // TILE * TILE
-    cuts = [0, third, 2 * third, rows]
-    parts = []
-    for i, order in enumerate(chain_orders(wide)):
-        cut = slice(cuts[i], cuts[i + 1])
-        parts.append(scatter_chain(add_low(keep[:, cut], got[:, cut]), order))
-    return jnp.concatenate(parts, axis=0)
-
-
-def gather_slots(values):
-    for bit in reversed(bits_of(lax.axis_size("wide"))):
-        values = jnp.concatenate([values, swap(values, "wide", bit)], axis=0)
-    return jnp.concatenate([values, swap(values, "narrow", 1)], axis=0)
+class Part:
+    def __init__(self, keep, got, start, rows, order):
+        wide, stride, columns = keep.shape
+        self.keep = (keep.reshape(wide * stride, columns), start, stride)
+        self.got = (got.reshape(wide * stride, columns), start, stride)
+        self.rows = rows
+        self.dims = list(reversed(bits_of(wide)))
+        self.order = list(order)
+
+
+def relay_kernel(me_ref, *refs, plan, inputs):
+    ins, outs = refs[:inputs], refs[inputs:]
+    for keep, got, rows, bit, inner, count, targets in plan:
+        k_ref, g_ref = ins[keep[0]], ins[got[0]]
+
+        def total(entry, keep=keep, got=got, rows=rows, k_ref=k_ref, g_ref=g_ref):
+            left = k_ref[pl.ds(pl.multiple_of(keep[1] + entry * keep[2], TILE), rows), :]
+            right = g_ref[pl.ds(pl.multiple_of(got[1] + entry * got[2], TILE), rows), :]
+            return left.astype(F32) + right.astype(F32)
+
+        if bit is None:
+            outs[targets[0][0]][...] = total(0)
+            continue
+        own = (me_ref[0] // bit) % 2
+
+        @pl.loop(0, count // 2)
+        def _(i, own=own, rows=rows, inner=inner, targets=targets, total=total):
+            outer = (i // inner) * 2 * inner + i % inner
+            for which, (out, base) in zip((1 - own, own), targets, strict=True):
+                to = pl.multiple_of(base + i * rows, TILE)
+                outs[out][pl.ds(to, rows), :] = total(outer + which * inner).astype(BF16)
+
+
+def relay(me, parts):
+    arrays, plan, shapes, buffers = [], [], [], {}
+
+    def index(array):
+        for i, known in enumerate(arrays):
+            if known is array:
+                return i
+        arrays.append(array)
+        return len(arrays) - 1
+
+    columns = parts[0].keep[0].shape[1]
+    bits = sorted({p.order[0] for p in parts if p.order})
+    sizes = {b: 0 for b in bits}
+    for p in parts:
+        keep, got = (index(p.keep[0]),) + p.keep[1:], (index(p.got[0]),) + p.got[1:]
+        count = 1 << len(p.dims)
+        if not p.order:
+            plan.append([keep, got, p.rows, None, 1, 1, [(len(bits) + len(shapes), 0)]])
+            shapes.append(jax.ShapeDtypeStruct((p.rows, columns), F32))
+            continue
+        bit = p.order[0]
+        at = p.dims.index(bit)
+        inner = 1 << (len(p.dims) - 1 - at)
+        targets = [(bits.index(bit), sizes[bit]), (len(bits) + len(shapes), 0)]
+        plan.append([keep, got, p.rows, bit, inner, count, targets])
+        p.got = (None, sizes[bit], p.rows)
+        sizes[bit] += count // 2 * p.rows
+        shapes.append(jax.ShapeDtypeStruct((count // 2 * p.rows, columns), BF16))
+        p.dims.pop(at)
+    sends = [jax.ShapeDtypeStruct((sizes[b], columns), BF16) for b in bits]
+    vmem = pl.BlockSpec(memory_space=pltpu.VMEM)
+    out = pl.pallas_call(
+        functools.partial(relay_kernel, plan=plan, inputs=len(arrays)),
+        in_specs=[pl.BlockSpec(memory_space=pltpu.SMEM)] + [vmem] * len(arrays),
+        out_specs=[vmem] * (len(sends) + len(shapes)),
+        out_shape=sends + shapes,
+        compiler_params=params(),
+    )(me, *arrays)
+    for p, kept in zip(parts, out[len(bits) :], strict=True):
+        p.keep = (kept, 0, p.rows)
+    return dict(zip(bits, out))
+
+
+class Sums:
+    def __init__(self, me, parts):
+        self.me, self.parts = me, parts
+        self.going = relay(me, parts)
+
+    def step(self):
+        came = {bit: swap(send, "wide", bit) for bit, send in self.going.items()}
+        for p in self.parts:
+            bit = p.order.pop(0)
+            p.got = (came[bit],) + p.got[1:]
+        self.going = relay(self.me, self.parts)
+
+    def arrays(self):
+        return tuple(self.going.values()) + tuple(p.keep[0] for p in self.parts)
+
+    def put(self, arrays):
+        count = len(self.going)
+        self.going = dict(zip(self.going, arrays[:count], strict=True))
+        for p, kept in zip(self.parts, arrays[count:], strict=True):
+            p.keep = (kept,) + p.keep[1:]
+
+
+class Gather:
+    def __init__(self, values):
+        self.values = values
+        self.done = []
+
+    def step(self, bit):
+        got = swap(self.values, "narrow", 1) if bit is None else swap(self.values, "wide", bit)
+        self.values = jnp.concatenate([self.values, got], axis=0)
+        self.done.append(bit)
+
+    def place(self, difference):
+        at = jnp.zeros_like(difference)
+        for i, bit in enumerate(self.done):
+            if bit is not None:
+                at = at + ((difference // bit) % 2) * (1 << i)
+        return at
+
+    def arrays(self):
+        return (self.values,)
+
+    def put(self, arrays):
+        (self.values,) = arrays
+
+
+def tie(values, moving):
+    out = lax.optimization_barrier((tuple(values), tuple(m.arrays() for m in moving)))
+    for one, kept in zip(moving, out[1], strict=True):
+        one.put(kept)
+    return out[0]
 
 
 def local(
@@ -711,8 +956,7 @@
     if not tiled:
         x_view = x_view.transpose(1, 0, 2, 3).reshape(1, blocks, BLK, feat)
 
-    act, silu_back = jax.vjp(jax.nn.silu, cond_in.astype(F32))
-    act_low = act.astype(BF16)
+    act_low = jax.nn.silu(cond_in.astype(F32)).astype(BF16)
     modulate = jnp.dot(act_low, w_mod, preferred_element_type=F32) + b_mod.astype(F32)
     slot_ids = jnp.arange(slots, dtype=jnp.int32)
     in_slot = seg[:, None] == slot_ids[None, :]
@@ -741,108 +985,150 @@
     attn, x1, a2, a2_t = proj_forward(
         o_t, w_proj, b_proj.astype(F32).reshape(1, feat), x_view, mod_blocks
     )
-    f, da2, d_fc1, d_fc2, grad_b_fc1 = mlp(
-        a2, a2_t, df, dg, w_fc1, w_fc2, b_fc1.astype(F32).reshape(1, hidden)
-    )
-
+    own, place = half.reshape(1), group.reshape(1)
     part = feat // devices
-    d_fc1 = d_fc1.reshape(hidden // feat, wide, halves, part, feat)
-    d_fc2 = d_fc2.reshape(wide, halves, hidden // devices, feat)
-
-    def mlp_half(which):
-        one = pick(d_fc1, which, 2).transpose(1, 0, 2, 3).reshape(wide, -1, feat)
-        return jnp.concatenate([pick(d_fc2, which, 1), one], axis=1)
-
-    mlp_sum = scatter_sum(mlp_half(1 - half), mlp_half(half))
-
-    y, dx1, do_t, d_proj, grad_b_proj, sums_two = middle(
-        f, b_fc2.astype(F32).reshape(1, feat), x1, attn, dy, da2, mod_blocks, o_t, w_proj
+    halved = Halves(wide, part)
+    both = ("wide", "narrow")
+    f, da2, grad_b_fc1, d_fc1, d_fc2 = mlp(
+        own, a2, a2_t, df, dg, w_fc1, w_fc2, b_fc1.astype(F32).reshape(1, hidden), halved
+    )
+
+    if halved.split:
+        fc2_got, fc1_got = swap(d_fc2[0], "narrow", 1), swap(d_fc1[0], "narrow", 1)
+    y, dx1, do_t, grad_b_proj, sums_two, d_proj = middle(
+        own, f, b_fc2.astype(F32).reshape(1, feat), x1, attn, dy, da2, mod_blocks, o_t, w_proj,
+        halved,
     )
     y_dest = (
         y.reshape(blocks, wide, per_block, feat).transpose(0, 2, 1, 3).reshape(rows, feat)
     )
-    dqkv_t = attend_back(seg, qkv_t, o_t, do_t, lse)
-
-    a1_parts = a1_t.reshape(wide, halves, part, rows)
-    d_proj = d_proj.reshape(wide, halves, part, feat)
-
-    def qkv_half(which):
-        mine = pick(a1_parts, which, 1).reshape(wide * part, rows)
-        three = lax.dot_general(
-            mine, dqkv_t, (((1,), (2,)), ((), ())), preferred_element_type=F32
+    in_slot_wide = in_slot[:, :, None, None]
+
+    def padded(by_slot):
+        return jnp.pad(by_slot, ((0, 0), (0, -slots % 8), (0, 0)))
+
+    def slot_sums(sums):
+        picked = jnp.where(in_slot_wide, sums[:, None], 0.0)
+        return jnp.sum(picked, axis=0).reshape(slots, -1).astype(BF16)
+
+    two = Gather(
+        jnp.concatenate(
+            [slot_sums(sums_two), jnp.pad(act_low, ((0, 0), (0, 3 * feat)))], axis=0
+        )[None]
+    )
+    near, far = bits_of(wide)[:3], bits_of(wide)[3:]
+    quarter = HEADS // 4
+    back_piece = functools.partial(attend_back, seg, qkv_t, o_t, lse=lse, count=quarter)
+    orders = chain_orders(wide)
+    if halved.split:
+        proj_got = swap(d_proj[0], "narrow", 1)
+        fc2_rows, fc1_rows = d_fc2[1].shape[1], d_fc1[1].shape[1]
+        cut = (fc2_rows + fc1_rows + part) // 3 // TILE * TILE
+        sums = Sums(
+            place,
+            [
+                Part(d_fc2[1], fc2_got, 0, cut, orders[0]),
+                Part(d_fc1[1], fc1_got, 0, cut, orders[1]),
+                Part(d_fc2[1], fc2_got, cut, fc2_rows - cut, orders[2]),
+                Part(d_fc1[1], fc1_got, cut, fc1_rows - cut, orders[2]),
+                Part(d_proj[1], proj_got, 0, part, orders[2]),
+            ],
         )
-        three = three.reshape(wide, part, 3, feat).transpose(0, 2, 1, 3)
-        return jnp.concatenate(
-            [three.astype(BF16).reshape(wide, 3 * part, feat), pick(d_proj, which, 1)], axis=1
-        )
-
-    qkv_sum = scatter_sum(qkv_half(1 - half), qkv_half(half))
-    sums_q = jnp.sum(dqkv_t.astype(F32), axis=2)
-    grad_b_qv = jnp.concatenate([sums_q[0], sums_q[2]])
-
-    drows, sums_one = rows_back(dqkv_t, w_qkv_t, x_view, dx1, mod_blocks)
+        (do_t,) = tie((do_t,), [sums, two])
+        two.step(None)
+        pieces = [back_piece(do_t, first=i * quarter) for i in range(3)]
+        sums.step()
+        (do_t, *pieces) = tie((do_t, *pieces), [sums, two])
+        for bit in far:
+            two.step(bit)
+        pieces.append(back_piece(do_t, first=3 * quarter))
+        sums.step()
+        (a1_t, *pieces) = tie((a1_t, *pieces), [sums, two])
+        d_qkv, sums_q = qkv_grad(own, a1_t, pieces, halved)
+        sums.step()
+        qkv_got = swap(d_qkv[0], "narrow", 1)
+        (dx1, *pieces) = tie((dx1, *pieces), [sums, two])
+    else:
+        for bit in [None] + far:
+            two.step(bit)
+        pieces = [back_piece(do_t, first=i * quarter) for i in range(4)]
+        d_qkv, sums_q = qkv_grad(own, a1_t, pieces, halved)
+    for bit in near:
+        two.step(bit)
+    drows, sums_one = rows_back(pieces, w_qkv_t, x_view, dx1, mod_blocks)
     back = drows
     if not tiled:
         back = back.reshape(blocks, wide, per_block, feat).transpose(1, 0, 2, 3)
-    back = exchange(back.reshape(wide, rows // wide, feat)).reshape(rows, feat)
-
-    by_slot = in_slot.astype(F32)
-
-    def slot_sums(sums):
-        count = sums.shape[1]
-        picked = jnp.where(in_slot[:, :, None, None], sums[:, None], 0.0)
-        return jnp.sum(picked, axis=0).reshape(slots, count * feat).astype(BF16)
-
-    dmod_two, dmod_one = slot_sums(sums_two), slot_sums(sums_one)
-    dact = dot(dmod_two, w_mod[:, 2 * feat :], 1, 1) + dot(dmod_one, w_mod[:, : 2 * feat], 1, 1)
-    dcond_in = silu_back(dact)[0].astype(BF16)
-    back_cond = exchange(
-        dcond_in.reshape(slots, wide, feat // wide).transpose(1, 0, 2)
-    ).reshape(places, feat // wide)
-    merge = restore if tiled else restore_any
-    dx_src, dcond = merge(src, cidx, back, back_cond)
-
-    me = group * halves + half
-    two_all = gather_slots(jnp.concatenate([act_low, dmod_two], axis=1))
-    one_all = gather_slots(dmod_one)
-    act_mine = lax.dynamic_slice_in_dim(two_all[:, :feat], me * part, part, axis=1)
-    dmod_all = jnp.concatenate([one_all, two_all[:, feat:]], axis=1)
-    grad_w_mod = dot(act_mine, dmod_all, 0, 0)
-    grad_b_mod = jnp.sum(
-        lax.dynamic_slice_in_dim(dmod_all, me * 6 * part, 6 * part, axis=1).astype(F32), axis=0
-    )
-
+    back = exchange(back.reshape(wide, rows // wide, feat))
     biases = jnp.concatenate(
         [
             grad_b_fc1.reshape(devices, -1),
             grad_b_fc2.reshape(devices, -1),
             grad_b_proj.reshape(devices, -1),
-            grad_b_qv.reshape(devices, -1),
+            jnp.concatenate([sums_q[0], sums_q[2]]).reshape(devices, -1),
         ],
         axis=1,
     )
-    biases = jnp.sum(
-        lax.all_to_all(biases, ("wide", "narrow"), split_axis=0, concat_axis=0, tiled=True), axis=0
-    )
-    at_two, at_proj, at_qv = 4 * part, 5 * part, 6 * part
-
-    fc2_rows = hidden // devices
-    grad_w_fc2 = mlp_sum[:fc2_rows].astype(F32)
-    grad_w_fc1 = (
-        mlp_sum[fc2_rows:]
-        .reshape(hidden // feat, part, feat)
-        .transpose(1, 0, 2)
-        .reshape(part, hidden)
-        .astype(F32)
-    )
-    grad_w_qkv = (
-        qkv_sum[: 3 * part]
-        .reshape(3, part, feat)
-        .transpose(1, 0, 2)
-        .reshape(part, 3 * feat)
-        .astype(F32)
-    )
-    grad_w_proj = qkv_sum[3 * part :].astype(F32)
+    per_device = biases.shape[1]
+    one = Gather(
+        jnp.concatenate(
+            [slot_sums(sums_one), biases.astype(BF16).reshape(slots, 2 * feat)], axis=0
+        )[None]
+    )
+    one.step(None)
+    if halved.split:
+        late = Sums(
+            place, [Part(d_qkv[1], qkv_got, i * part, part, orders[i]) for i in range(3)]
+        )
+        tie((), [late, one])
+        for i in range(len(orders[0])):
+            late.step()
+            if i == 0:
+                for bit in far:
+                    one.step(bit)
+            if i == BACK_ROUNDS:
+                (back,) = tie((back,), [late, one])
+            else:
+                tie((), [late, one])
+        sums.step()
+        for bit in near:
+            one.step(bit)
+        fc2_a, fc1_a, fc2_b, fc1_b, grad_w_proj = (p.keep[0] for p in sums.parts)
+        grad_w_fc2 = jnp.concatenate([fc2_a, fc2_b], axis=0)
+        grad_w_fc1 = jnp.concatenate([fc1_a, fc1_b], axis=0)
+        grad_w_fc1 = (
+            grad_w_fc1.reshape(hidden // feat, part, feat).transpose(1, 0, 2).reshape(part, hidden)
+        )
+        grad_w_qkv = jnp.concatenate([p.keep[0] for p in late.parts], axis=1)
+    else:
+        for bit in far + near:
+            one.step(bit)
+
+        def scattered(full):
+            return lax.psum_scatter(full, both, scatter_dimension=0, tiled=True).astype(F32)
+
+        grad_w_fc2 = scattered(d_fc2[0])
+        grad_w_fc1 = scattered(d_fc1[0].transpose(1, 0, 2).reshape(feat, hidden))
+        grad_w_proj = scattered(d_proj[0])
+        grad_w_qkv = scattered(d_qkv[0].transpose(1, 0, 2).reshape(feat, 3 * feat))
+    merge = restore if tiled else restore_any
+    dx_src = merge(src, back.reshape(rows, feat))
+
+    me = group * halves + half
+    count = 2 * slots * devices
+    grad_w_mod, grad_b_mod, dact, biases = mod_grad(
+        group, me, one.values.reshape(count, -1), two.values.reshape(count, -1), w_mod, part,
+        feat // wide, slots,
+    )
+    grad_b_mod = lax.dynamic_slice_in_dim(grad_b_mod[0], me * 6 * part, 6 * part)
+    biases = lax.dynamic_slice_in_dim(biases[slots:].reshape(-1), me * per_device, per_device)
+    spot = jnp.maximum(cidx, 0)
+    spot = one.place((spot // slots) ^ group) * 2 * slots + spot % slots
+    _, silu_back = jax.vjp(jax.nn.silu, cond.astype(F32))
+    dcond = silu_back(jnp.take(dact, spot, axis=0))[0].astype(BF16)
+    dcond = jnp.where(cidx[:, None] >= 0, dcond, jnp.zeros((), BF16))
+
+    at_two, at_proj, at_qv = hidden // devices, hidden // devices + part, hidden // devices + 2 * part
     return (
         y_dest,
         dx_src,

time: 684 us -> 526 us (0.77)
  waiting for transfers between devices: 211 us -> 75.8 us
  Pallas kernels: 211 us -> 294 us
  local copies, waits for them, and re-layouts: 79.8 us -> 44.7 us
  matrix products: 49 us -> 20.8 us
  other arithmetic: 47.9 us -> 20.9 us
  blocking collectives: 15.4 us -> 0 us
    ppermute x36 -> x34, waiting for transfers between devices: 201 us -> 69.2 us  [swap(): return lax.ppermute(values, axis, [(i, i ^ bit) for i in range(count)])]
    pallas_call x5 -> x18, Pallas kernels: 103 us -> 177 us  [the longest x1 62.9 us: mlp(): pl.pallas_call(functools.partial(mlp_kernel, first=first, second=second),...]
    concatenate x7 -> x2, local copies, waits for them, and re-layouts: 19.4 us -> 0.15 us  [local(): jnp.concatenate([sums_q[0], sums_q[2]]).reshape(devices, -1)]
    convert_element_type x32 -> x2, other arithmetic: 19.2 us -> 0.03 us  [local(): act_low = jax.nn.silu(cond_in.astype(F32)).astype(BF16)]
    dot_general x2 -> x0, matrix products: 16 us -> none  [qkv_half(): lax.dot_general(mine, dqkv_t, (((1,), (2,)), ((), ())), preferred_element...]
    all_to_all x1 -> x0, blocking collectives: 15.4 us -> none  [local(): came_cond = exchange(scond.reshape(wide, slots, feat // wide))]
    unnamed x78 -> x99, local copies, waits for them, and re-layouts: 12.1 us -> 27.4 us
    transpose x3 -> x0, local copies, waits for them, and re-layouts: 14.7 us -> none  [mlp_half(): one = pick(d_fc1, which, 2).transpose(1, 0, 2, 3).reshape(wide, -1, feat)]
  transfers between devices with their start and end apart: 40 -> 37, of which waited for: 23 -> 15; matrix products, arithmetic and copies ran while one was open for 22% -> 11% of each run, Pallas kernels for 12% -> 26%
where the time goes in v2:
time: 526 us; the launch traced here: 516 us
  Pallas kernels  294 us (56%)
  waiting for transfers between devices  75.8 us (14%)
  starting transfers between devices  58.9 us (11%)
  local copies, waits for them, and re-layouts  44.7 us (8%)
  other arithmetic  20.9 us (4%)
  matrix products  20.8 us (4%)
    ppermute x34, waiting for transfers between devices, swap(): return lax.ppermute(values, axis, [(i, i ^ bit) for i in range(count)])  69.2 us
    pallas_call x1, Pallas kernels, mlp(): pl.pallas_call(functools.partial(mlp_kernel, first=first, second=second),...  62.9 us
    pallas_call x4, Pallas kernels, attend_back(): pl.pallas_call(functools.partial(attend_back_kernel, blocks=rows // BLK,...  56.8 us
    pallas_call x10, Pallas kernels, relay(): pl.pallas_call(functools.partial(relay_kernel, plan=plan, inputs=len(arra...  52.6 us
    ppermute x34, starting transfers between devices, swap(): return lax.ppermute(values, axis, [(i, i ^ bit) for i in range(count)])  40.7 us
    pallas_call x1, Pallas kernels, attend(): pl.pallas_call(functools.partial(attend_kernel, blocks=rows // BLK, heads...  37.6 us
    unnamed x99, local copies, waits for them, and re-layouts  27.4 us
    pallas_call x1, Pallas kernels, middle(): pl.pallas_call(functools.partial(middle_kernel, halves=halves), grid=(blo...  17 us
  transfers between devices with their start and end apart: 37, of which 15 were waited for; matrix products, arithmetic and copies ran while one was open for 11% of the time, Pallas kernels for 26%

profile of v2, /device:TPU:0, one launch (start us, length us, event | category | flops | bytes accessed | tf_op | source)
XLA Modules:
  0.0 516.4 jit_solution(3256126832669135049)
XLA Ops:
  7.7 8.3 %all-to-all-start.1 = ((bf16[16,2,128]{2,1,0:T(2,128)(2,1)}), bf16[16,2,128]{2,1,0:T(2,128)(2,1)S(1)}, u32[]{:S(2)}, u32[]{:S(2)}) async-start(bf16[16,2,128]{2,1,0:T(2,128)(2,1)} %reshape.262), calls=%async_computation.1 | async-start | bytes 16384 | tf_op jit(solution)/shard_map/all_to_all | solution.py:953
  16.0 5.4 %shard_map.247 = (bf16[16,64,1024]{2,1,0:T(8,128)(2,1)}, s32[64]{0:T(128)}) custom-call(s32[64]{0:T(128)} %dynamic_slice.14.len_ref, s32[64]{0:T(128)} %dynamic_slice.15.buck_ref, bf16[1024,1024]{1,0:T(8,128)(2,1)} %x_ref.1), custom_call_target="tpu_custom_call" | custom-call | bytes 16777216 | tf_op jit(solution)/shard_map/pallas_call | solution.py:136
  23.2 5.2 %all-to-all-start = ((bf16[16,64,1024]{2,1,0:T(8,128)(2,1)}), bf16[16,64,1024]{2,1,0:T(8,128)(2,1)}, u32[]{:S(2)}, u32[]{:S(2)}) async-start(bf16[16,64,1024]{2,1,0:T(8,128)(2,1)} %get-tuple-element.190), calls=%async_computation | async-start | bytes 4194304 | tf_op jit(solution)/shard_map/all_to_all | solution.py:952
  30.2 8.6 %copy.40 = bf16[1024,3072]{0,1:T(8,128)(2,1)} copy(bf16[1024,3072]{1,0:T(8,128)(2,1)} %param.21) | data formatting | bytes 12582912 | tf_op args[6]
  43.2 6.3 %convolution_add_fusion = f32[4,6144]{1,0:T(4,128)S(1)} fusion(bf16[4,1024]{1,0:T(4,128)(2,1)S(1)} %fusion.11, bf16[1024,6144]{1,0:T(8,128)(2,1)} %w_ref.5, f32[6144]{0:T(1024)S(1)} %convert_element_type.74), kind=kOutput, calls=%fused_computation.1 | convolution fusion | flops 50356224 | bytes 12713984 | tf_op jit(solution)/shard_map/dot_general | solution.py:960
  52.1 14.5 %fusion.24.dg_ref = f32[1024,4096]{1,0:T(8,128)} fusion(bf16[1024,1024]{1,0:T(8,128)(2,1)S(1)} %fusion.df_ref, bf16[4096,1024]{1,0:T(8,128)(2,1)} %w2_ref.1), kind=kOutput, calls=%fused_computation.92 | convolution fusion | flops 8589934592 | bytes 27262976 | tf_op jit(solution)/shard_map/dot_general | solution.py:29
  71.4 13.5 %shard_map.248 = (bf16[3072,1024]{1,0:T(8,128)(2,1)}, bf16[1024,1024]{1,0:T(8,128)(2,1)}) custom-call(bf16[16,4,16,1024]{3,2,1,0:T(8,128)(2,1)} %bitcast.2.x_ref, f32[4,6,1024]{2,1,0:T(8,128)} %copy-done.14, bf16[3072,1024]{1,0:T(8,128)(2,1)} %bitcast.83, f32[3072,1]{1,0:T(8,128)} %copy.41.b_ref), custom_call_target="tpu_custom_call" | custom-call | flops 6442450944 | bytes 20971520 | tf_op jit(solution)/shard_map/pallas_call | solution.py:242
  85.0 37.6 %shard_map.249 = (bf16[1024,1024]{1,0:T(8,128)(2,1)}, f32[16,1,1024]{2,1,0:T(1,128)}) custom-call(s32[4]{0:T(128)} %get-tuple-element.189.seg_ref, bf16[3072,1024]{1,0:T(8,128)(2,1)} %get-tuple-element.192.q_ref.k_ref.v_ref, bf16[3072,1024]{1,0:T(8,128)(2,1)} %get-tuple-element.192.q_ref.k_ref.v_ref, bf16[3072,1024]{1,0:T(8,128)(2,1)} %get-tuple-element.192.q_ref.k_ref.v_ref), custom_call_target="tpu_custom_call" | custom-call | flops 17179869184 | bytes 8388608 | tf_op jit(solution)/shard_map/pallas_call | solution.py:304
  122.5 9.0 %shard_map.250 = (f32[1024,1024]{1,0:T(8,128)}, f32[1024,1024]{1,0:T(8,128)}, bf16[1024,1024]{1,0:T(8,128)(2,1)}, bf16[1024,1024]{1,0:T(8,128)(2,1)}) custom-call(bf16[1024,1024]{1,0:T(8,128)(2,1)} %get-tuple-element.193.o_ref, bf16[1024,1024]{1,0:T(8,128)(2,1)} %w_ref.4, f32[1,1024]{1,0:T(1,128)} %bitcast.103, bf16[16,4,16,1024]{3,2,1,0:T(8,128)(2,1)} %bitcast.2.x_ref, ...), custom_call_target="tpu_custom_call" | custom-call | flops 2147483648 | bytes 20971520 | tf_op jit(solution)/shard_map/pallas_call | solution.py:483
  131.6 62.9 %shard_map.251 = (f32[1024,1024]{1,0:T(8,128)}, f32[1024,1024]{1,0:T(8,128)}, f32[1,4096]{1,0:T(1,128)}, bf16[16,4,32,1024]{3,2,1,0:T(8,128)(2,1)}, bf16[16,4,32...) custom-call(s32[1]{0:T(128)} %bitcast.half_ref, ...), custom_call_target="tpu_custom_call" | custom-call | flops 42949672960 | bytes 67108864 | tf_op jit(solution)/shard_map/pallas_call | solution.py:569
  195.6 17.0 %shard_map.252 = (bf16[1024,1024]{1,0:T(8,128)(2,1)}, f32[1024,1024]{1,0:T(8,128)}, bf16[1024,1024]{1,0:T(8,128)(2,1)}, f32[1,1024]{1,0:T(1,128)}, f32[4,4,1024]...) custom-call(s32[1]{0:T(128)} %bitcast.half_ref, f32[1024,1024]{1,0:T(8,128)} %get-tuple-element.196.f_ref, ...), custom_call_target="tpu_custom_call" | custom-call | flops 4294967296 | bytes 33554432 | tf_op jit(solution)/shard_map/pallas_call | solution.py:643
  217.9 17.5 %shard_map.253 = (bf16[768,1024]{1,0:T(8,128)(2,1)}, bf16[768,1024]{1,0:T(8,128)(2,1)}, bf16[768,1024]{1,0:T(8,128)(2,1)}, bf16[768,1024]{1,0:T(8,128)(2,1)}, bf...) custom-call(s32[1]{0:T(128)} %bitcast.1.me_ref, ...), custom_call_target="tpu_custom_call" | custom-call | tf_op jit(solution)/shard_map/pallas_call | solution.py:850
  245.1 14.1 %shard_map.256.refs_2_ = bf16[3,256,1024]{2,1,0:T(8,128)(2,1)} custom-call(s32[4]{0:T(128)} %get-tuple-element.189.seg_ref, bf16[3072,1024]{1,0:T(8,128)(2,1)} %get-tuple-element.192.q_ref.k_ref.v_ref, bf16[3072,1024]{1,0:T(8,128)(2,1)} %get-tuple-element.192.q_ref.k_ref.v_ref, bf16[3072,1024]{1,0:T(8,128)(2,1)} %get-tuple-element.192.q_ref.k_ref.v_ref, ...), custom_call_target="tpu_custom_call" | custom-call | flops 6442450944 | bytes 4194304 | tf_op jit(solution)/shard_map/pallas_call | solution.py:370
  259.2 14.3 %shard_map.255.refs_1_ = bf16[3,256,1024]{2,1,0:T(8,128)(2,1)} custom-call(s32[4]{0:T(128)} %get-tuple-element.189.seg_ref, bf16[3072,1024]{1,0:T(8,128)(2,1)} %get-tuple-element.192.q_ref.k_ref.v_ref, bf16[3072,1024]{1,0:T(8,128)(2,1)} %get-tuple-element.192.q_ref.k_ref.v_ref, bf16[3072,1024]{1,0:T(8,128)(2,1)} %get-tuple-element.192.q_ref.k_ref.v_ref, ...), custom_call_target="tpu_custom_call" | custom-call | flops 6442450944 | bytes 4194304 | tf_op jit(solution)/shard_map/pallas_call | solution.py:370
  273.4 14.1 %shard_map.254.refs_0_ = bf16[3,256,1024]{2,1,0:T(8,128)(2,1)} custom-call(s32[4]{0:T(128)} %get-tuple-element.189.seg_ref, bf16[3072,1024]{1,0:T(8,128)(2,1)} %get-tuple-element.192.q_ref.k_ref.v_ref, bf16[3072,1024]{1,0:T(8,128)(2,1)} %get-tuple-element.192.q_ref.k_ref.v_ref, bf16[3072,1024]{1,0:T(8,128)(2,1)} %get-tuple-element.192.q_ref.k_ref.v_ref, ...), custom_call_target="tpu_custom_call" | custom-call | flops 6442450944 | bytes 4194304 | tf_op jit(solution)/shard_map/pallas_call | solution.py:370
  290.4 7.1 %shard_map.257 = (bf16[384,1024]{1,0:T(8,128)(2,1)}, bf16[384,1024]{1,0:T(8,128)(2,1)}, bf16[384,1024]{1,0:T(8,128)(2,1)}, bf16[384,1024]{1,0:T(8,128)(2,1)}, bf...) custom-call(s32[1]{0:T(128)} %bitcast.1.me_ref, ...), custom_call_target="tpu_custom_call" | custom-call | tf_op jit(solution)/shard_map/pallas_call | solution.py:850
  301.4 14.3 %shard_map.258.refs_3_ = bf16[3,256,1024]{2,1,0:T(8,128)(2,1)} custom-call(s32[4]{0:T(128)} %get-tuple-element.189.seg_ref, bf16[3072,1024]{1,0:T(8,128)(2,1)} %get-tuple-element.192.q_ref.k_ref.v_ref, bf16[3072,1024]{1,0:T(8,128)(2,1)} %get-tuple-element.192.q_ref.k_ref.v_ref, bf16[3072,1024]{1,0:T(8,128)(2,1)} %get-tuple-element.192.q_ref.k_ref.v_ref, ...), custom_call_target="tpu_custom_call" | custom-call | flops 6442450944 | bytes 4194304 | tf_op jit(solution)/shard_map/pallas_call | solution.py:370
  328.7 12.5 %shard_map.262 = (bf16[16,3,32,1024]{3,2,1,0:T(8,128)(2,1)}, bf16[16,3,32,1024]{3,2,1,0:T(8,128)(2,1)}, f32[3,8,1024]{2,1,0:T(8,128)}) custom-call(s32[1]{0:T(128)} %bitcast.half_ref, bf16[1024,1024]{1,0:T(8,128)(2,1)} %get-tuple-element.285.a_ref, bf16[3,256,1024]{2,1,0:T(8,128)(2,1)} %shard_map.254.refs_0_, bf16[3,256,1024]{2,1,0:T(8,128)(2,1)} %shard_map.255.refs_1_, ...), custom_call_target="tpu_custom_call" | custom-call | flops 6442450944 | bytes 12582912 | tf_op jit(solution)/shard_map/pallas_call | solution.py:449
  345.6 13.8 %shard_map.261 = (bf16[16,4,16,1024]{3,2,1,0:T(8,128)(2,1)}, f32[4,2,1024]{2,1,0:T(2,128)}) custom-call(bf16[3072,1024]{1,0:T(8,128)(2,1)} %bitcast.84, bf16[16,4,16,1024]{3,2,1,0:T(8,128)(2,1)} %bitcast.2.x_ref, f32[1024,1024]{1,0:T(8,128)} %get-tuple-element.279.dx_ref, f32[4,6,1024]{2,1,0:T(8,128)} %copy-done.14, ...), custom_call_target="tpu_custom_call" | custom-call | flops 6442450944 | bytes 20971520 | tf_op jit(solution)/shard_map/pallas_call | solution.py:694
  378.3 9.2 %shard_map.263 = (bf16[256,1024]{1,0:T(8,128)(2,1)}, bf16[256,1024]{1,0:T(8,128)(2,1)}, bf16[256,1024]{1,0:T(8,128)(2,1)}, bf16[256,1024]{1,0:T(8,128)(2,1)}, bf...) custom-call(s32[1]{0:T(128)} %bitcast.1.me_ref, bf16[1536,1024]{1,0:T(8,128)(2,1)} %bitcast.68, ...), custom_call_target="tpu_custom_call" | custom-call | tf_op jit(solution)/shard_map/pallas_call | solution.py:850
  394.1 21.8 %collective-permute-done.19 = bf16[2,8,2048]{2,1,0:T(8,128)(2,1)S(1)} collective-permute-done((bf16[2,8,2048]{2,1,0:T(8,128)(2,1)S(1)}, bf16[2,8,2048]{2,1,0:T(8,128)(2,1)S(1)}, u32[]{:S(2)}, u32[]{:S(2)}) %collective-permute-start.19) | collective-permute-done | bytes 65568 | tf_op jit(solution)/shard_map/ppermute | solution.py:773
  424.2 6.3 %collective-permute-done.20.refs_1_ = bf16[128,1024]{1,0:T(8,128)(2,1)S(1)} collective-permute-done((bf16[128,1024]{1,0:T(8,128)(2,1)}, bf16[128,1024]{1,0:T(8,128)(2,1)S(1)}, u32[]{:S(2)}, u32[]{:S(2)}) %collective-permute-start.20) | collective-permute-done | bytes 262176 | tf_op jit(solution)/shard_map/ppermute | solution.py:773
  449.8 24.3 %collective-permute-done.26.refs_1_ = bf16[96,1024]{1,0:T(8,128)(2,1)S(1)} collective-permute-done((bf16[96,1024]{1,0:T(8,128)(2,1)}, bf16[96,1024]{1,0:T(8,128)(2,1)S(1)}, u32[]{:S(2)}, u32[]{:S(2)}) %collective-permute-start.26) | collective-permute-done | bytes 196640 | tf_op jit(solution)/shard_map/ppermute | solution.py:773
  504.1 5.7 %shard_map.269 = (f32[32,6144]{1,0:T(8,128)}, f32[1,6144]{1,0:T(1,128)}, f32[256,64]{1,0:T(8,128)}, f32[8,2048]{1,0:T(8,128)}) custom-call(s32[2]{0:T(128)} %pad_add_fusion.ids_ref, bf16[256,2048]{1,0:T(8,128)(2,1)} %maximum_bitcast_fusion.1.one_ref, bf16[256,4096]{1,0:T(8,128)(2,1)} %maximum_bitcast_fusion.two_ref, bf16[1024,6144]{1,0:T(8,128)(2,1)} %w_ref.5), custom_call_target="tpu_custom_call" | custom-call | tf_op jit(solution)/shard_map/pallas_call | solution.py:743
  (236 shorter events, 151.5 us)
Async XLA Ops:
  7.7 15.5 %all-to-all-start.1 = ((bf16[16,2,128]{2,1,0:T(2,128)(2,1)}), bf16[16,2,128]{2,1,0:T(2,128)(2,1)S(1)}, u32[]{:S(2)}, u32[]{:S(2)}) async-start(bf16[16,2,128]{2,1,0:T(2,128)(2,1)} %reshape.262), calls=%async_computation.1 | async-start | bytes 16384 | tf_op jit(solution)/shard_map/all_to_all | solution.py:953
  23.2 48.2 %all-to-all-start = ((bf16[16,64,1024]{2,1,0:T(8,128)(2,1)}), bf16[16,64,1024]{2,1,0:T(8,128)(2,1)}, u32[]{:S(2)}, u32[]{:S(2)}) async-start(bf16[16,64,1024]{2,1,0:T(8,128)(2,1)} %get-tuple-element.190), calls=%async_computation | async-start | bytes 4194304 | tf_op jit(solution)/shard_map/all_to_all | solution.py:952
  194.4 21.1 %collective-permute-start = (bf16[16,128,1024]{2,1,0:T(8,128)(2,1)}, bf16[16,128,1024]{2,1,0:T(8,128)(2,1)S(1)}, u32[]{:S(2)}, u32[]{:S(2)}) collective-permute-start(bf16[16,128,1024]{2,1,0:T(8,128)(2,1)} %get-tuple-element.206), channel_id=1, source_target_pairs={{0,1},{1,0},{2,3},{3,2},{4,5},{5,4},{6,7},{7,6},{8,9},{9,8},{10,11... | collective-permute-start | bytes 12582920 | tf_op jit(solution)/shard_map/ppermute | solution.py:773
  194.5 21.0 %collective-permute-start.1 = (bf16[16,128,1024]{2,1,0:T(8,128)(2,1)}, bf16[16,128,1024]{2,1,0:T(8,128)(2,1)}, u32[]{:S(2)}, u32[]{:S(2)}) collective-permute-start(bf16[16,128,1024]{2,1,0:T(8,128)(2,1)} %bitcast.105), channel_id=1, source_target_pairs={{0,1},{1,0},{2,3},{3,2},{4,5},{5,4},{6,7},{7,6},{8,9},{9,8},{10,11... | collective-permute-start | bytes 12582920 | tf_op jit(solution)/shard_map/ppermute | solution.py:773
  235.4 52.1 %collective-permute-start.6 = (bf16[1,8,4096]{2,1,0:T(8,128)(2,1)S(1)}, bf16[1,8,4096]{2,1,0:T(8,128)(2,1)S(1)}, u32[]{:S(2)}, u32[]{:S(2)}) collective-permute-start(bf16[1,8,4096]{2,1,0:T(8,128)(2,1)S(1)} %fusion.4), channel_id=1, source_target_pairs={{0,1},{1,0},{2,3},{3,2},{4,5},{5,4},{6,7},{7,6},{8,9},{9,8},{10,11... | collective-permute-start | bytes 196616 | tf_op jit(solution)/shard_map/ppermute | solution.py:773
  235.6 52.0 %collective-permute-start.3 = (bf16[768,1024]{1,0:T(8,128)(2,1)}, bf16[768,1024]{1,0:T(8,128)(2,1)S(1)}, u32[]{:S(2)}, u32[]{:S(2)}) collective-permute-start(bf16[768,1024]{1,0:T(8,128)(2,1)} %get-tuple-element.223), channel_id=1, source_target_pairs={{0,2},{2,0},{4,6},{6,4},{8,10},{10,8},{12,14},{14,12},{16,18},{18,... | collective-permute-start | bytes 4718600 | tf_op jit(solution)/shard_map/ppermute | solution.py:773
  236.7 50.9 %collective-permute-start.4 = (bf16[768,1024]{1,0:T(8,128)(2,1)}, bf16[768,1024]{1,0:T(8,128)(2,1)S(1)}, u32[]{:S(2)}, u32[]{:S(2)}) collective-permute-start(bf16[768,1024]{1,0:T(8,128)(2,1)} %get-tuple-element.225), channel_id=1, source_target_pairs={{0,4},{2,6},{4,0},{6,2},{8,12},{10,14},{12,8},{14,10},{16,20},{18,... | collective-permute-start | bytes 4718600 | tf_op jit(solution)/shard_map/ppermute | solution.py:773
  240.0 47.6 %collective-permute-start.5 = (bf16[768,1024]{1,0:T(8,128)(2,1)}, bf16[768,1024]{1,0:T(8,128)(2,1)S(1)}, u32[]{:S(2)}, u32[]{:S(2)}) collective-permute-start(bf16[768,1024]{1,0:T(8,128)(2,1)} %get-tuple-element.227), channel_id=1, source_target_pairs={{0,8},{2,10},{4,12},{6,14},{8,0},{10,2},{12,4},{14,6},{16,24},{18,... | collective-permute-start | bytes 4718600 | tf_op jit(solution)/shard_map/ppermute | solution.py:773
  297.5 18.3 %collective-permute-start.10 = (bf16[2,8,4096]{2,1,0:T(8,128)(2,1)S(1)}, bf16[2,8,4096]{2,1,0:T(8,128)(2,1)S(1)}, u32[]{:S(2)}, u32[]{:S(2)}) collective-permute-start(bf16[2,8,4096]{2,1,0:T(8,128)(2,1)S(1)} %pad_maximum_fusion.8), channel_id=1, source_target_pairs={{0,16},{2,18},{4,20},{6,22},{8,24},{10,26},{12,28},{14,30},{16,0},... | collective-permute-start | bytes 393224 | tf_op jit(solution)/shard_map/ppermute | solution.py:773
  297.8 18.9 %collective-permute-start.7 = (bf16[384,1024]{1,0:T(8,128)(2,1)}, bf16[384,1024]{1,0:T(8,128)(2,1)S(1)}, u32[]{:S(2)}, u32[]{:S(2)}) collective-permute-start(bf16[384,1024]{1,0:T(8,128)(2,1)} %get-tuple-element.244), channel_id=1, source_target_pairs={{0,4},{2,6},{4,0},{6,2},{8,12},{10,14},{12,8},{14,10},{16,20},{18,... | collective-permute-start | bytes 2359304 | tf_op jit(solution)/shard_map/ppermute | solution.py:773
  298.5 21.7 %collective-permute-start.8 = (bf16[384,1024]{1,0:T(8,128)(2,1)}, bf16[384,1024]{1,0:T(8,128)(2,1)S(1)}, u32[]{:S(2)}, u32[]{:S(2)}) collective-permute-start(bf16[384,1024]{1,0:T(8,128)(2,1)} %get-tuple-element.246), channel_id=1, source_target_pairs={{0,8},{2,10},{4,12},{6,14},{8,0},{10,2},{12,4},{14,6},{16,24},{18,... | collective-permute-start | bytes 2359304 | tf_op jit(solution)/shard_map/ppermute | solution.py:773
  300.5 19.7 %collective-permute-start.9 = (bf16[384,1024]{1,0:T(8,128)(2,1)}, bf16[384,1024]{1,0:T(8,128)(2,1)S(1)}, u32[]{:S(2)}, u32[]{:S(2)}) collective-permute-start(bf16[384,1024]{1,0:T(8,128)(2,1)} %get-tuple-element.248), channel_id=1, source_target_pairs={{0,2},{2,0},{4,6},{6,4},{8,10},{10,8},{12,14},{14,12},{16,18},{18,... | collective-permute-start | bytes 2359304 | tf_op jit(solution)/shard_map/ppermute | solution.py:773
  326.3 14.9 %collective-permute-start.12 = (bf16[192,1024]{1,0:T(8,128)(2,1)}, bf16[192,1024]{1,0:T(8,128)(2,1)S(1)}, u32[]{:S(2)}, u32[]{:S(2)}) collective-permute-start(bf16[192,1024]{1,0:T(8,128)(2,1)} %get-tuple-element.267), channel_id=1, source_target_pairs={{0,2},{2,0},{4,6},{6,4},{8,10},{10,8},{12,14},{14,12},{16,18},{18,... | collective-permute-start | bytes 1179656 | tf_op jit(solution)/shard_map/ppermute | solution.py:773
  341.2 35.5 %collective-permute-start.14 = (bf16[16,96,1024]{2,1,0:T(8,128)(2,1)}, bf16[16,96,1024]{2,1,0:T(8,128)(2,1)S(1)}, u32[]{:S(2)}, u32[]{:S(2)}) collective-permute-start(bf16[16,96,1024]{2,1,0:T(8,128)(2,1)} %bitcast.106), channel_id=1, source_target_pairs={{0,1},{1,0},{2,3},{3,2},{4,5},{5,4},{6,7},{7,6},{8,9},{9,8},{10,11... | collective-permute-start | bytes 9437192 | tf_op jit(solution)/shard_map/ppermute | solution.py:773
  359.3 117.2 %all-to-all-start.2 = ((bf16[16,64,1024]{2,1,0:T(8,128)(2,1)}), bf16[16,64,1024]{2,1,0:T(8,128)(2,1)}, u32[]{:S(2)}, u32[]{:S(2)}) async-start(bf16[16,64,1024]{2,1,0:T(8,128)(2,1)} %bitcast.86), calls=%async_computation.2 | async-start | bytes 4194304 | tf_op jit(solution)/shard_map/all_to_all | solution.py:1062
  372.6 20.8 %collective-permute-start.30 = (bf16[4,8,4096]{2,1,0:T(8,128)(2,1)S(1)}, bf16[4,8,4096]{2,1,0:T(8,128)(2,1)S(1)}, u32[]{:S(2)}, u32[]{:S(2)}) collective-permute-start(bf16[4,8,4096]{2,1,0:T(8,128)(2,1)S(1)} %pad_maximum_fusion.6), channel_id=1, source_target_pairs={{0,2},{2,0},{4,6},{6,4},{8,10},{10,8},{12,14},{14,12},{16,18},{18,... | collective-permute-start | bytes 786440 | tf_op jit(solution)/shard_map/ppermute | solution.py:773
  387.5 28.4 %collective-permute-start.19 = (bf16[2,8,2048]{2,1,0:T(8,128)(2,1)S(1)}, bf16[2,8,2048]{2,1,0:T(8,128)(2,1)S(1)}, u32[]{:S(2)}, u32[]{:S(2)}) collective-permute-start(bf16[2,8,2048]{2,1,0:T(8,128)(2,1)S(1)} %pad_maximum_fusion.10), channel_id=1, source_target_pairs={{0,16},{2,18},{4,20},{6,22},{8,24},{10,26},{12,28},{14,30},{16,0},... | collective-permute-start | bytes 196616 | tf_op jit(solution)/shard_map/ppermute | solution.py:773
  389.9 26.0 %collective-permute-start.16 = (bf16[256,1024]{1,0:T(8,128)(2,1)}, bf16[256,1024]{1,0:T(8,128)(2,1)S(1)}, u32[]{:S(2)}, u32[]{:S(2)}) collective-permute-start(bf16[256,1024]{1,0:T(8,128)(2,1)} %get-tuple-element.299), channel_id=1, source_target_pairs={{0,2},{2,0},{4,6},{6,4},{8,10},{10,8},{12,14},{14,12},{16,18},{18,... | collective-permute-start | bytes 1572872 | tf_op jit(solution)/shard_map/ppermute | solution.py:773
  390.4 25.5 %collective-permute-start.17 = (bf16[256,1024]{1,0:T(8,128)(2,1)}, bf16[256,1024]{1,0:T(8,128)(2,1)S(1)}, u32[]{:S(2)}, u32[]{:S(2)}) collective-permute-start(bf16[256,1024]{1,0:T(8,128)(2,1)} %get-tuple-element.301), channel_id=1, source_target_pairs={{0,4},{2,6},{4,0},{6,2},{8,12},{10,14},{12,8},{14,10},{16,20},{18,... | collective-permute-start | bytes 1572872 | tf_op jit(solution)/shard_map/ppermute | solution.py:773
  391.9 24.1 %collective-permute-start.18 = (bf16[256,1024]{1,0:T(8,128)(2,1)}, bf16[256,1024]{1,0:T(8,128)(2,1)S(1)}, u32[]{:S(2)}, u32[]{:S(2)}) collective-permute-start(bf16[256,1024]{1,0:T(8,128)(2,1)} %get-tuple-element.303), channel_id=1, source_target_pairs={{0,8},{2,10},{4,12},{6,14},{8,0},{10,2},{12,4},{14,6},{16,24},{18,... | collective-permute-start | bytes 1572872 | tf_op jit(solution)/shard_map/ppermute | solution.py:773
  393.5 54.6 %collective-permute-start.31 = (bf16[8,8,4096]{2,1,0:T(8,128)(2,1)S(1)}, bf16[8,8,4096]{2,1,0:T(8,128)(2,1)S(1)}, u32[]{:S(2)}, u32[]{:S(2)}) collective-permute-start(bf16[8,8,4096]{2,1,0:T(8,128)(2,1)S(1)} %pad_maximum_fusion.2), channel_id=1, source_target_pairs={{0,4},{2,6},{4,0},{6,2},{8,12},{10,14},{12,8},{14,10},{16,20},{18,... | collective-permute-start | bytes 1572872 | tf_op jit(solution)/shard_map/ppermute | solution.py:773
  437.7 48.3 %collective-permute-start.33 = (bf16[288,1024]{1,0:T(8,128)(2,1)}, bf16[288,1024]{1,0:T(8,128)(2,1)}, u32[]{:S(2)}, u32[]{:S(2)}) collective-permute-start(bf16[288,1024]{1,0:T(8,128)(2,1)} %get-tuple-element.355), channel_id=1, source_target_pairs={{0,16},{2,18},{4,20},{6,22},{8,24},{10,26},{12,28},{14,30},{16,0},... | collective-permute-start | bytes 1769480 | tf_op jit(solution)/shard_map/ppermute | solution.py:773
  445.3 28.8 %collective-permute-start.26 = (bf16[96,1024]{1,0:T(8,128)(2,1)}, bf16[96,1024]{1,0:T(8,128)(2,1)S(1)}, u32[]{:S(2)}, u32[]{:S(2)}) collective-permute-start(bf16[96,1024]{1,0:T(8,128)(2,1)} %get-tuple-element.336), channel_id=1, source_target_pairs={{0,16},{2,18},{4,20},{6,22},{8,24},{10,26},{12,28},{14,30},{16,0},... | collective-permute-start | bytes 589832 | tf_op jit(solution)/shard_map/ppermute | solution.py:773
  449.2 42.9 %collective-permute-start.32 = (bf16[16,8,4096]{2,1,0:T(8,128)(2,1)}, bf16[16,8,4096]{2,1,0:T(8,128)(2,1)}, u32[]{:S(2)}, u32[]{:S(2)}) collective-permute-start(bf16[16,8,4096]{2,1,0:T(8,128)(2,1)} %pad_maximum_fusion), channel_id=1, source_target_pairs={{0,8},{2,10},{4,12},{6,14},{8,0},{10,2},{12,4},{14,6},{16,24},{18,... | collective-permute-start | bytes 3145736 | tf_op jit(solution)/shard_map/ppermute | solution.py:773
  (59 other events, 606.4 us)

commit v3 on v2

--- a/solution.py
+++ b/solution.py
@@ -16,7 +16,7 @@
 BLK = 256
 TILE = 16
 VMEM_LIMIT = 58 * 2**20
-BACK_ROUNDS = 3
+BRIEF = pl.CostEstimate(flops=1, bytes_accessed=1, transcendentals=0)
 BF16 = jnp.bfloat16
 F32 = jnp.float32
 
@@ -132,6 +132,7 @@
         ],
         scratch_shapes=counters + [pltpu.VMEM((places, part), F32), pltpu.VMEM((places, part), F32)],
         compiler_params=params(),
+        cost_estimate=BRIEF,
     )(lens, buck, me, cond)
     send, src = pl.pallas_call(
         functools.partial(regroup_rows_kernel, wide=wide),
@@ -143,7 +144,7 @@
         ],
         scratch_shapes=counters,
         compiler_params=params(),
-        cost_estimate=pl.CostEstimate(flops=0, bytes_accessed=16 * 2**20, transcendentals=0),
+        cost_estimate=BRIEF,
     )(lens, buck, x_src)
     return send, scond, seg, src, cidx
 
@@ -166,6 +167,7 @@
         out_specs=vmem,
         out_shape=jax.ShapeDtypeStruct(back.shape, BF16),
         compiler_params=params(),
+        cost_estimate=BRIEF,
     )(src, back)
 
 
@@ -257,9 +259,7 @@
             jax.ShapeDtypeStruct((feat, blocks * BLK), BF16),
         ],
         compiler_params=params(),
-        cost_estimate=pl.CostEstimate(
-            flops=6 * feat * feat * blocks * BLK, bytes_accessed=20 * 2**20, transcendentals=0
-        ),
+        cost_estimate=BRIEF,
     )(x_view, mod_blocks, w_t, bias)
 
 
@@ -321,9 +321,7 @@
             jax.ShapeDtypeStruct((feat // HEAD_DIM, 1, rows), F32),
         ],
         compiler_params=params(),
-        cost_estimate=pl.CostEstimate(
-            flops=16 * feat * rows * rows, bytes_accessed=8 * 2**20, transcendentals=16 * rows * rows
-        ),
+        cost_estimate=BRIEF,
     )(seg, qkv_t, qkv_t, qkv_t)
 
 
@@ -384,11 +382,7 @@
         ),
         out_shape=jax.ShapeDtypeStruct((3, count * HEAD_DIM, rows), BF16),
         compiler_params=params(),
-        cost_estimate=pl.CostEstimate(
-            flops=24 * count * HEAD_DIM * rows * rows,
-            bytes_accessed=count * 2**20,
-            transcendentals=count * rows * rows,
-        ),
+        cost_estimate=BRIEF,
     )(seg, qkv_t, qkv_t, qkv_t, o_t, do_t, lse)
 
 
@@ -444,20 +438,17 @@
 
 def qkv_grad(half, a1_t, dqkv, halves):
     feat, rows = a1_t.shape
-    span = dqkv[0].shape[1]
-    columns = span * len(dqkv)
+    columns = sum(d.shape[1] for d in dqkv)
     out = pl.pallas_call(
         functools.partial(qkv_grad_kernel, pieces=len(dqkv), halves=halves),
         grid=(3,),
         in_specs=[pl.BlockSpec(memory_space=pltpu.SMEM), whole(feat, rows)]
-        + [pl.BlockSpec((1, span, rows), lambda i: (i, 0, 0))] * len(dqkv),
+        + [pl.BlockSpec((1, d.shape[1], rows), lambda i: (i, 0, 0)) for d in dqkv],
         out_specs=halves.specs(1, columns, lambda i: (i, 0))
         + [pl.BlockSpec((1, 8, columns), lambda i: (i, 0, 0))],
         out_shape=halves.shapes((3,), columns) + [jax.ShapeDtypeStruct((3, 8, columns), F32)],
         compiler_params=params(),
-        cost_estimate=pl.CostEstimate(
-            flops=6 * feat * rows * columns, bytes_accessed=12 * 2**20, transcendentals=0
-        ),
+        cost_estimate=BRIEF,
     )(half, a1_t, *dqkv)
     return halves.finish(out[:-1]), out[-1][:, 0, :]
 
@@ -498,19 +489,16 @@
             jax.ShapeDtypeStruct((feat, rows), BF16),
         ],
         compiler_params=params(),
-        cost_estimate=pl.CostEstimate(
-            flops=2 * feat * feat * rows, bytes_accessed=20 * 2**20, transcendentals=0
-        ),
+        cost_estimate=BRIEF,
     )(o_t, w_proj, b_proj, x_view, mod_blocks)
 
 
 def gelu_both(u):
     c = math.sqrt(2.0 / math.pi)
     square = u * u
-    t = jnp.tanh(u * (c + (c * 0.044715) * square))
-    half = 0.5 + 0.5 * t
-    slope = half + (0.5 * u) * (1.0 - t * t) * (c + (3.0 * c * 0.044715) * square)
-    return u * half, slope
+    half = 0.5 + 0.5 * jnp.tanh(u * (c + (c * 0.044715) * square))
+    g = u * half
+    return g, half + (g - g * half) * (2.0 * c + (6.0 * c * 0.044715) * square)
 
 
 def mlp_kernel(
@@ -530,17 +518,19 @@
 
     w1, w2 = w1_ref[...], w2_ref[...]
     bias = jnp.zeros((1, w1.shape[1]), F32)
-    for r in range(rows // BLK):
-        rs = slice(r * BLK, (r + 1) * BLK)
-        u = dot(a_ref[rs, :], w1, 1, 0) + b1_ref[...]
-        g, slope = gelu_both(u)
-        g = g.astype(BF16)
-        du = (dg_ref[rs, :] * slope).astype(BF16)
-        g_ref[rs, :] = g
-        du_ref[rs, :] = du
-        bias = bias + jnp.sum(du.astype(F32), axis=0, keepdims=True)
-        f_ref[rs, :] += dot(g, w2, 1, 0)
-        da_ref[rs, :] += dot(du, w1, 1, 1)
+    cuts = [slice(r, r + BLK) for r in range(0, rows, BLK)]
+    u = dot(a_ref[cuts[0], :], w1, 1, 0)
+    for r, rs in enumerate(cuts):
+        later = dot(a_ref[cuts[r + 1], :], w1, 1, 0) if r + 1 < len(cuts) else None
+        g, slope = gelu_both(u + b1_ref[...])
+        du = dg_ref[rs, :] * slope
+        bias = bias + jnp.sum(du, axis=0, keepdims=True)
+        g_ref[rs, :] = g.astype(BF16)
+        du_ref[rs, :] = du.astype(BF16)
+        u = later
+        for past in cuts[r - 1 : r] if r + 1 < len(cuts) else cuts[max(r - 1, 0) :]:
+            f_ref[past, :] += dot(g_ref[past, :], w2, 1, 0)
+            da_ref[past, :] += dot(du_ref[past, :], w1, 1, 1)
     db_ref[...] = bias
     first.store(half_ref[0], dot(at_ref[...], du_ref[...], 1, 0), outs_one)
     second.store(half_ref[0], dot(g_ref[...], df_ref[...], 0, 0), outs_two)
@@ -591,9 +581,7 @@
         + two_shapes,
         scratch_shapes=[pltpu.VMEM((rows, width), BF16), pltpu.VMEM((rows, width), BF16)],
         compiler_params=params(),
-        cost_estimate=pl.CostEstimate(
-            flops=10 * rows * feat * hidden, bytes_accessed=64 * 2**20, transcendentals=rows * hidden
-        ),
+        cost_estimate=BRIEF,
     )(half, a2, a2_t, df, dg, w1, w2, b1)
     f, da2, bias = out[:3]
     rest = out[3:]
@@ -601,17 +589,27 @@
     return f, da2, bias, first.finish(rest[:count]), second.finish(rest[count:])
 
 
+def to_slot(ref, slot, slots, terms):
+    @pl.when(slot >= 0)
+    def _():
+        for i, term in enumerate(terms):
+            ref[pl.ds(2 * slots * i + slot, 1), :] += jnp.sum(term, axis=0, keepdims=True)
+
+
 def middle_kernel(
-    half_ref, f_ref, b2_ref, x1_ref, attn_ref, dy_ref, da_ref, mod_ref, o_ref, w_ref,
+    half_ref, seg_ref, f_ref, b2_ref, x1_ref, attn_ref, dy_ref, da_ref, mod_ref, o_ref, w_ref, act_ref,
     y_ref, dx_ref, do_ref, db_ref, sums_ref, *rest, halves,
 ):
     k = pl.program_id(0)
-    outs, acc_ref = rest[:-1], rest[-1]
+    outs, acc_ref, slot_ref = rest[:-2], rest[-2], rest[-1]
+    slots = act_ref.shape[0]
 
     @pl.when(k == 0)
     def _():
         acc_ref[...] = jnp.zeros_like(acc_ref)
         db_ref[...] = jnp.zeros_like(db_ref)
+        slot_ref[...] = jnp.zeros_like(slot_ref)
+        slot_ref[slots : 2 * slots, :] = act_ref[...].astype(F32)
 
     f = f_ref[...] + b2_ref[...]
     x1 = x1_ref[...]
@@ -623,122 +621,137 @@
     dx_ref[...] = dx1
     dattn = (mod_ref[0, 2:3, :] * dx1).astype(BF16)
     db_ref[...] += jnp.sum(dattn.astype(F32), axis=0, keepdims=True)
-    sums_ref[0, 0:1, :] = jnp.sum(dx1 * attn_ref[...], axis=0, keepdims=True)
-    sums_ref[0, 1:2, :] = jnp.sum(da, axis=0, keepdims=True)
-    sums_ref[0, 2:3, :] = jnp.sum(da * normed, axis=0, keepdims=True)
-    sums_ref[0, 3:4, :] = jnp.sum(dy * f, axis=0, keepdims=True)
+    to_slot(slot_ref, seg_ref[k], slots, [dx1 * attn_ref[...], da, da * normed, dy * f])
     do_ref[...] = dot(w_ref[...], dattn, 1, 1).astype(BF16)
     acc_ref[...] += dot(o_ref[...], dattn, 1, 0)
 
     @pl.when(k == pl.num_programs(0) - 1)
     def _():
         halves.store(half_ref[0], acc_ref[...], outs)
-
-
-def middle(half, f, b2, x1, attn, dy, da2, mod_blocks, o_t, w_proj, halves):
+        sums_ref[0] = slot_ref[...].astype(BF16)
+
+
+def middle(half, seg, act, f, b2, x1, attn, dy, da2, mod_blocks, o_t, w_proj, halves):
     rows, feat = x1.shape
     by_row = pl.BlockSpec((BLK, feat), lambda k: (k, 0))
     by_column = pl.BlockSpec((feat, BLK), lambda k: (0, k))
     blocks = rows // BLK
+    slots = act.shape[0]
     out = pl.pallas_call(
         functools.partial(middle_kernel, halves=halves),
         grid=(blocks,),
         in_specs=[
             pl.BlockSpec(memory_space=pltpu.SMEM),
+            pl.BlockSpec(memory_space=pltpu.SMEM),
             by_row, whole(1, feat), by_row, by_row, by_row, by_row,
             pl.BlockSpec((1, 6, feat), lambda k: (k, 0, 0)),
-            by_column, whole(feat, feat),
+            by_column, whole(feat, feat), whole(slots, feat),
         ],
         out_specs=[
             by_row, by_row, by_column, whole(1, feat),
-            pl.BlockSpec((1, 4, feat), lambda k: (k, 0, 0)),
+            whole(1, 8 * slots, feat),
         ] + halves.specs(0, feat, lambda k: (0,)),
         out_shape=[
             jax.ShapeDtypeStruct((rows, feat), BF16),
             jax.ShapeDtypeStruct((rows, feat), F32),
             jax.ShapeDtypeStruct((feat, rows), BF16),
             jax.ShapeDtypeStruct((1, feat), F32),
-            jax.ShapeDtypeStruct((blocks, 4, feat), F32),
+            jax.ShapeDtypeStruct((1, 8 * slots, feat), BF16),
         ]
         + halves.shapes((), feat),
-        scratch_shapes=[pltpu.VMEM((feat, feat), F32)],
+        scratch_shapes=[pltpu.VMEM((feat, feat), F32), pltpu.VMEM((8 * slots, feat), F32)],
         compiler_params=params(),
-        cost_estimate=pl.CostEstimate(
-            flops=4 * feat * feat * rows, bytes_accessed=32 * 2**20, transcendentals=0
-        ),
-    )(half, f, b2, x1, attn, dy, da2, mod_blocks, o_t, w_proj)
+        cost_estimate=BRIEF,
+    )(half, seg, f, b2, x1, attn, dy, da2, mod_blocks, o_t, w_proj, act)
     return tuple(out[:5]) + (halves.finish(out[5:]),)
 
 
-def rows_back_kernel(w_ref, x_ref, dx_ref, mod_ref, *refs):
-    out_ref, sums_ref = refs[-2:]
+def rows_back_kernel(seg_ref, w_ref, x_ref, dx_ref, mod_ref, bias_ref, *refs):
+    out_ref, sums_ref, slot_ref = refs[-3:]
+    slots = bias_ref.shape[0] // 2
+
+    @pl.when(pl.program_id(0) == 0)
+    def _():
+        slot_ref[...] = jnp.zeros_like(slot_ref)
+        slot_ref[slots : 2 * slots, :] = bias_ref[:slots, :]
+        slot_ref[3 * slots :, :] = bias_ref[slots:, :]
+
     feat = x_ref.shape[-1]
-    span = refs[0].shape[1]
     da = None
     for i in range(3):
-        for g, ref in enumerate(refs[:-2]):
-            at = i * feat + g * span
-            more = dot(ref[i], w_ref[at : at + span, :], 0, 0)
+        at = i * feat
+        for ref in refs[:-3]:
+            more = dot(ref[i], w_ref[at : at + ref.shape[1], :], 0, 0)
             da = more if da is None else da + more
+            at += ref.shape[1]
     normed, inverse = norm_parts(x_ref[...].reshape(BLK, feat).astype(F32))
     out = dx_ref[...] + norm_back(da * (1.0 + mod_ref[0, 1:2, :]), normed, inverse)
     out_ref[...] = out.astype(BF16).reshape(out_ref.shape)
-    sums_ref[0, 0:1, :] = jnp.sum(da, axis=0, keepdims=True)
-    sums_ref[0, 1:2, :] = jnp.sum(da * normed, axis=0, keepdims=True)
-
-
-def rows_back(dqkv, w_t, x_view, dx1, mod_blocks):
+    to_slot(slot_ref, seg_ref[pl.program_id(0)], slots, [da, da * normed])
+    sums_ref[0] = slot_ref[...].astype(BF16)
+
+
+def rows_back(seg, dqkv, w_t, x_view, dx1, mod_blocks, biases):
     rows, feat = dx1.shape
     blocks = rows // BLK
-    span = dqkv[0].shape[1]
     return pl.pallas_call(
         rows_back_kernel,
         grid=(blocks,),
         in_specs=[
+            pl.BlockSpec(memory_space=pltpu.SMEM),
             whole(3 * feat, feat),
             row_spec(x_view.shape),
             pl.BlockSpec((BLK, feat), lambda k: (k, 0)),
             pl.BlockSpec((1, 6, feat), lambda k: (k, 0, 0)),
+            whole(*biases.shape),
         ]
-        + [pl.BlockSpec((3, span, BLK), lambda k: (0, 0, k))] * len(dqkv),
-        out_specs=[row_spec(x_view.shape), pl.BlockSpec((1, 2, feat), lambda k: (k, 0, 0))],
+        + [pl.BlockSpec((3, d.shape[1], BLK), lambda k: (0, 0, k)) for d in dqkv],
+        out_specs=[row_spec(x_view.shape), whole(1, 2 * biases.shape[0], feat)],
         out_shape=[
             jax.ShapeDtypeStruct(x_view.shape, BF16),
-            jax.ShapeDtypeStruct((blocks, 2, feat), F32),
+            jax.ShapeDtypeStruct((1, 2 * biases.shape[0], feat), BF16),
         ],
+        scratch_shapes=[pltpu.VMEM((2 * biases.shape[0], feat), F32)],
         compiler_params=params(),
-        cost_estimate=pl.CostEstimate(
-            flops=6 * feat * feat * rows, bytes_accessed=20 * 2**20, transcendentals=0
-        ),
-    )(w_t, x_view, dx1, mod_blocks, *dqkv)
+        cost_estimate=BRIEF,
+    )(seg, w_t, x_view, dx1, mod_blocks, biases, *dqkv)
 
 
 def mod_grad_kernel(
     ids_ref, one_ref, two_ref, w_ref, gw_ref, gb_ref, dact_ref, bias_ref, act_ref, *, part, slots
 ):
-    early = one_ref.shape[1]
-    feat = early // 2
-    rows = one_ref.shape[0]
+    feat = one_ref.shape[-1]
+
+    def columns(ref):
+        wide = ref[...].astype(F32)
+        wide = wide.reshape(wide.shape[0], -1, 2 * slots, feat)
+        return [wide[:, i].reshape(-1, feat) for i in range(wide.shape[1])]
+
+    one, two = columns(one_ref), columns(two_ref)
+    rows = one[0].shape[0]
     first = lax.broadcasted_iota(jnp.int32, (rows, 1), 0) % (2 * slots) < slots
-    act = pltpu.roll(two_ref[:, :feat].astype(F32), rows - slots, 0)
-    act_ref[...] = jnp.where(first, act, 0.0).T
+    act_ref[...] = jnp.where(first, pltpu.roll(two[0], rows - slots, 0), 0.0).T
     act = act_ref[pl.ds(pl.multiple_of(ids_ref[1] * part, 8), part), :].astype(BF16)
-    one, two = one_ref[...], two_ref[...]
-    gw_ref[:, :early] = dot(act, one, 1, 0)
-    gw_ref[:, early:] = dot(act, two, 1, 0)
-    one_wide = one.astype(F32)
-    gb_ref[:, :early] = jnp.sum(jnp.where(first, one_wide, 0.0), axis=0, keepdims=True)
-    gb_ref[:, early:] = jnp.sum(jnp.where(first, two.astype(F32), 0.0), axis=0, keepdims=True)
-    dact_ref[...] = dot(one, w_ref[:, :early], 1, 1) + dot(two, w_ref[:, early:], 1, 1)
-    bias_ref[...] = jnp.sum(one_wide.reshape(rows // (2 * slots), 2 * slots, early), axis=0)
+    dact = None
+    for i, values in enumerate(one + two):
+        at = slice(i * feat, (i + 1) * feat)
+        low = values.astype(BF16)
+        gw_ref[:, at] = dot(act, low, 1, 0)
+        gb_ref[:, at] = jnp.sum(jnp.where(first, values, 0.0), axis=0, keepdims=True)
+        more = dot(low, w_ref[:, at], 1, 1)
+        dact = more if dact is None else dact + more
+    dact_ref[...] = dact
+    for i, values in enumerate(one):
+        sums = jnp.sum(values.reshape(-1, 2 * slots, feat), axis=0)
+        bias_ref[i * slots : (i + 1) * slots, :] = sums[slots:, :]
 
 
 def mod_grad(group, me, one, two, w_mod, part, share, slots):
-    count, early = one.shape
     feat, columns = w_mod.shape
-
-    def fixed(i, ids):
-        return (0, 0)
+    count = 2 * slots * one.shape[0]
+
+    def fixed(*shape):
+        return pl.BlockSpec(shape, lambda i, ids: (0,) * len(shape))
 
     return pl.pallas_call(
         functools.partial(mod_grad_kernel, part=part, slots=slots),
@@ -746,15 +759,15 @@
             num_scalar_prefetch=1,
             grid=(1,),
             in_specs=[
-                pl.BlockSpec(one.shape, fixed),
-                pl.BlockSpec(two.shape, fixed),
+                fixed(*one.shape),
+                fixed(*two.shape),
                 pl.BlockSpec((share, columns), lambda i, ids: (ids[0], 0)),
             ],
             out_specs=[
-                pl.BlockSpec((part, columns), fixed),
-                pl.BlockSpec((1, columns), fixed),
-                pl.BlockSpec((count, share), fixed),
-                pl.BlockSpec((2 * slots, early), fixed),
+                fixed(part, columns),
+                fixed(1, columns),
+                fixed(count, share),
+                fixed(2 * slots, feat),
             ],
             scratch_shapes=[pltpu.VMEM((feat, count), F32)],
         ),
@@ -762,9 +775,10 @@
             jax.ShapeDtypeStruct((part, columns), F32),
             jax.ShapeDtypeStruct((1, columns), F32),
             jax.ShapeDtypeStruct((count, share), F32),
-            jax.ShapeDtypeStruct((2 * slots, early), F32),
+            jax.ShapeDtypeStruct((2 * slots, feat), F32),
         ],
         compiler_params=params(),
+        cost_estimate=BRIEF,
     )(jnp.stack([group, me]), one, two, w_mod)
 
 
@@ -785,39 +799,80 @@
 
 class Part:
     def __init__(self, keep, got, start, rows, order):
-        wide, stride, columns = keep.shape
-        self.keep = (keep.reshape(wide * stride, columns), start, stride)
-        self.got = (got.reshape(wide * stride, columns), start, stride)
+        self.keep, self.got = (keep, start), (got, start)
         self.rows = rows
-        self.dims = list(reversed(bits_of(wide)))
+        self.dims = list(reversed(bits_of(keep.shape[0])))
         self.order = list(order)
 
 
-def relay_kernel(me_ref, *refs, plan, inputs):
-    ins, outs = refs[:inputs], refs[inputs:]
-    for keep, got, rows, bit, inner, count, targets in plan:
-        k_ref, g_ref = ins[keep[0]], ins[got[0]]
-
-        def total(entry, keep=keep, got=got, rows=rows, k_ref=k_ref, g_ref=g_ref):
-            left = k_ref[pl.ds(pl.multiple_of(keep[1] + entry * keep[2], TILE), rows), :]
-            right = g_ref[pl.ds(pl.multiple_of(got[1] + entry * got[2], TILE), rows), :]
-            return left.astype(F32) + right.astype(F32)
-
+class Rider:
+    def __init__(self, values, order):
+        self.keep, self.got = (values, 0), (None, 0)
+        self.rows = values.shape[1]
+        self.order, self.done = list(order), []
+
+    def place(self, difference):
+        at = jnp.zeros_like(difference)
+        for i, bit in enumerate(self.done):
+            at = at + ((difference // bit) % 2) * (1 << i)
+        return at
+
+
+def relay_kernel(me_ref, *refs, plan, inputs, outputs, streamed):
+    ins, outs, scratch = refs[:inputs], refs[inputs : inputs + outputs], refs[inputs + outputs :]
+    arriving, leaving = [], []
+    if streamed:
+        for i, (_, addends, rows, *_) in enumerate(plan):
+            for k, (source, start) in enumerate(addends):
+                copy = pltpu.make_async_copy(
+                    ins[source].at[:, pl.ds(start, rows), :], scratch[4 * i + k], scratch[-1].at[4 * i + k]
+                )
+                copy.start()
+                arriving.append(copy)
+    for i, (ride, addends, rows, bit, inner, count, targets) in enumerate(plan):
+        if ride:
+            for k, (source, start) in enumerate(addends):
+                piece = ins[source][0, start : start + rows, :]
+                for out, base in targets:
+                    outs[out][0, base + k * rows : base + (k + 1) * rows, :] = piece
+            continue
         if bit is None:
-            outs[targets[0][0]][...] = total(0)
+            left, right = (ins[a][0, start : start + rows, :] for a, start in addends)
+            outs[targets[0][0]][...] = left.astype(F32) + right.astype(F32)
             continue
+        if streamed:
+            arriving[2 * i].wait()
+            arriving[2 * i + 1].wait()
+            reads = [(scratch[4 * i], 0), (scratch[4 * i + 1], 0)]
+            writes = [(scratch[4 * i + 2], 0), (scratch[4 * i + 3], 0)]
+        else:
+            reads = [(ins[a], start) for a, start in addends]
+            writes = [(outs[out], base) for out, base in targets]
         own = (me_ref[0] // bit) % 2
 
         @pl.loop(0, count // 2)
-        def _(i, own=own, rows=rows, inner=inner, targets=targets, total=total):
-            outer = (i // inner) * 2 * inner + i % inner
-            for which, (out, base) in zip((1 - own, own), targets, strict=True):
-                to = pl.multiple_of(base + i * rows, TILE)
-                outs[out][pl.ds(to, rows), :] = total(outer + which * inner).astype(BF16)
-
-
-def relay(me, parts):
-    arrays, plan, shapes, buffers = [], [], [], {}
+        def _(e, own=own, rows=rows, inner=inner, reads=reads, writes=writes):
+            outer = (e // inner) * 2 * inner + e % inner
+            for which, (out, base) in zip((1 - own, own), writes, strict=True):
+                left, right = (r[outer + which * inner, a : a + rows, :] for r, a in reads)
+                out[e, base : base + rows, :] = left + right
+
+        if streamed:
+            for k, (out, base) in enumerate(targets):
+                copy = pltpu.make_async_copy(
+                    scratch[4 * i + 2 + k],
+                    outs[out].at[:, pl.ds(base, rows), :],
+                    scratch[-1].at[4 * i + 2 + k],
+                )
+                copy.start()
+                leaving.append(copy)
+    for copy in leaving:
+        copy.wait()
+
+
+def relay(me, moving, streamed=False):
+    arrays, plan, shapes, sends, keeps = [], [], [], {}, []
+    columns = moving[0].keep[0].shape[2]
 
     def index(array):
         for i, known in enumerate(arrays):
@@ -826,83 +881,85 @@
         arrays.append(array)
         return len(arrays) - 1
 
-    columns = parts[0].keep[0].shape[1]
-    bits = sorted({p.order[0] for p in parts if p.order})
-    sizes = {b: 0 for b in bits}
-    for p in parts:
-        keep, got = (index(p.keep[0]),) + p.keep[1:], (index(p.got[0]),) + p.got[1:]
-        count = 1 << len(p.dims)
-        if not p.order:
-            plan.append([keep, got, p.rows, None, 1, 1, [(len(bits) + len(shapes), 0)]])
-            shapes.append(jax.ShapeDtypeStruct((p.rows, columns), F32))
-            continue
-        bit = p.order[0]
-        at = p.dims.index(bit)
-        inner = 1 << (len(p.dims) - 1 - at)
-        targets = [(bits.index(bit), sizes[bit]), (len(bits) + len(shapes), 0)]
-        plan.append([keep, got, p.rows, bit, inner, count, targets])
-        p.got = (None, sizes[bit], p.rows)
-        sizes[bit] += count // 2 * p.rows
-        shapes.append(jax.ShapeDtypeStruct((count // 2 * p.rows, columns), BF16))
-        p.dims.pop(at)
-    sends = [jax.ShapeDtypeStruct((sizes[b], columns), BF16) for b in bits]
-    vmem = pl.BlockSpec(memory_space=pltpu.VMEM)
-    out = pl.pallas_call(
-        functools.partial(relay_kernel, plan=plan, inputs=len(arrays)),
-        in_specs=[pl.BlockSpec(memory_space=pltpu.SMEM)] + [vmem] * len(arrays),
-        out_specs=[vmem] * (len(sends) + len(shapes)),
-        out_shape=sends + shapes,
+    def out(*shape, dtype=BF16):
+        shapes.append(jax.ShapeDtypeStruct(shape, dtype))
+        return len(shapes) - 1
+
+    bits = [m.order[0] if m.order else None for m in moving]
+    for m, bit in zip(moving, bits, strict=True):
+        addends = [(index(a), start) for a, start in (m.keep, m.got) if a is not None]
+        ride = isinstance(m, Rider)
+        if ride:
+            keeps.append(out(1, m.rows * len(addends), m.keep[0].shape[2]))
+            plan.append((ride, addends, m.rows, None, 1, 1, [(keeps[-1], 0)]))
+            m.rows *= len(addends)
+            if bit is not None:
+                sends[ride, bit] = keeps[-1]
+        elif bit is None:
+            keeps.append(out(m.rows, columns, dtype=F32))
+            plan.append((ride, addends, m.rows, None, 1, 1, [(keeps[-1], 0)]))
+        else:
+            at = m.dims.index(bit)
+            count, inner = 1 << len(m.dims), 1 << (len(m.dims) - 1 - at)
+            same = [o for o, b in zip(moving, bits, strict=True) if b == bit and isinstance(o, Part)]
+            if (ride, bit) not in sends:
+                sends[ride, bit] = out(count // 2, sum(o.rows for o in same), columns)
+            base = sum(o.rows for o in same[: same.index(m)])
+            keeps.append(out(count // 2, m.rows, columns))
+            targets = [(sends[ride, bit], base), (keeps[-1], 0)]
+            plan.append((ride, addends, m.rows, bit, inner, count, targets))
+            m.got = (None, base)
+            m.dims.pop(at)
+    scratch = []
+    if streamed:
+        for _, _, rows, _, _, count, _ in plan:
+            scratch += [pltpu.VMEM((n, rows, columns), BF16) for n in (count, count, count // 2, count // 2)]
+        scratch.append(pltpu.SemaphoreType.DMA((len(scratch),)))
+    place = pl.BlockSpec(memory_space=pl.ANY if streamed else pltpu.VMEM)
+    out_arrays = pl.pallas_call(
+        functools.partial(
+            relay_kernel, plan=plan, inputs=len(arrays), outputs=len(shapes), streamed=streamed
+        ),
+        in_specs=[pl.BlockSpec(memory_space=pltpu.SMEM)] + [place] * len(arrays),
+        out_specs=[place] * len(shapes),
+        out_shape=shapes,
+        scratch_shapes=scratch,
         compiler_params=params(),
+        cost_estimate=BRIEF,
     )(me, *arrays)
-    for p, kept in zip(parts, out[len(bits) :], strict=True):
-        p.keep = (kept, 0, p.rows)
-    return dict(zip(bits, out))
+    for m, kept in zip(moving, keeps, strict=True):
+        m.keep = (out_arrays[kept], 0)
+    return {key: out_arrays[at] for key, at in sends.items()}
 
 
 class Sums:
-    def __init__(self, me, parts):
-        self.me, self.parts = me, parts
-        self.going = relay(me, parts)
+    def __init__(self, me, moving, streamed=False):
+        self.me, self.moving = me, list(moving)
+        self.going = relay(me, moving, streamed)
+
+    def join(self, rider):
+        self.moving.append(rider)
+        self.going[True, rider.order[0]] = rider.keep[0]
 
     def step(self):
-        came = {bit: swap(send, "wide", bit) for bit, send in self.going.items()}
-        for p in self.parts:
-            bit = p.order.pop(0)
-            p.got = (came[bit],) + p.got[1:]
-        self.going = relay(self.me, self.parts)
+        came = {key: swap(send, "wide", key[1]) for key, send in self.going.items()}
+        going = [m for m in self.moving if m.order]
+        for m in going:
+            bit = m.order.pop(0)
+            ride = isinstance(m, Rider)
+            m.got = (came[ride, bit], 0 if ride else m.got[1])
+            if ride:
+                m.done.append(bit)
+        self.going = relay(self.me, going)
 
     def arrays(self):
-        return tuple(self.going.values()) + tuple(p.keep[0] for p in self.parts)
+        return tuple(self.going.values()) + tuple(m.keep[0] for m in self.moving)
 
     def put(self, arrays):
         count = len(self.going)
         self.going = dict(zip(self.going, arrays[:count], strict=True))
-        for p, kept in zip(self.parts, arrays[count:], strict=True):
-            p.keep = (kept,) + p.keep[1:]
-
-
-class Gather:
-    def __init__(self, values):
-        self.values = values
-        self.done = []
-
-    def step(self, bit):
-        got = swap(self.values, "narrow", 1) if bit is None else swap(self.values, "wide", bit)
-        self.values = jnp.concatenate([self.values, got], axis=0)
-        self.done.append(bit)
-
-    def place(self, difference):
-        at = jnp.zeros_like(difference)
-        for i, bit in enumerate(self.done):
-            if bit is not None:
-                at = at + ((difference // bit) % 2) * (1 << i)
-        return at
-
-    def arrays(self):
-        return (self.values,)
-
-    def put(self, arrays):
-        (self.values,) = arrays
+        for m, kept in zip(self.moving, arrays[count:], strict=True):
+            m.keep = (kept,) + m.keep[1:]
 
 
 def tie(values, moving):
@@ -995,114 +1052,84 @@
 
     if halved.split:
         fc2_got, fc1_got = swap(d_fc2[0], "narrow", 1), swap(d_fc1[0], "narrow", 1)
-    y, dx1, do_t, grad_b_proj, sums_two, d_proj = middle(
-        own, f, b_fc2.astype(F32).reshape(1, feat), x1, attn, dy, da2, mod_blocks, o_t, w_proj,
+    y, dx1, do_t, grad_b_proj, two, d_proj = middle(
+        own, seg, act_low, f, b_fc2.astype(F32).reshape(1, feat), x1, attn, dy, da2, mod_blocks, o_t, w_proj,
         halved,
     )
     y_dest = (
         y.reshape(blocks, wide, per_block, feat).transpose(0, 2, 1, 3).reshape(rows, feat)
     )
-    in_slot_wide = in_slot[:, :, None, None]
-
-    def padded(by_slot):
-        return jnp.pad(by_slot, ((0, 0), (0, -slots % 8), (0, 0)))
-
-    def slot_sums(sums):
-        picked = jnp.where(in_slot_wide, sums[:, None], 0.0)
-        return jnp.sum(picked, axis=0).reshape(slots, -1).astype(BF16)
-
-    two = Gather(
-        jnp.concatenate(
-            [slot_sums(sums_two), jnp.pad(act_low, ((0, 0), (0, 3 * feat)))], axis=0
-        )[None]
-    )
     near, far = bits_of(wide)[:3], bits_of(wide)[3:]
-    quarter = HEADS // 4
-    back_piece = functools.partial(attend_back, seg, qkv_t, o_t, lse=lse, count=quarter)
     orders = chain_orders(wide)
+    pieces, head = [], 0
+
+    def attention(counts):
+        nonlocal head
+        for count in counts:
+            pieces.append(attend_back(seg, qkv_t, o_t, do_t, lse, first=head, count=count))
+            head += count
+
+    def bias_rows(sums_q):
+        sums = [grad_b_fc1[0], grad_b_fc2, grad_b_proj[0], sums_q[0], sums_q[2]]
+        return jnp.concatenate(sums).reshape(2 * slots, feat)
+
     if halved.split:
         proj_got = swap(d_proj[0], "narrow", 1)
         fc2_rows, fc1_rows = d_fc2[1].shape[1], d_fc1[1].shape[1]
         cut = (fc2_rows + fc1_rows + part) // 3 // TILE * TILE
-        sums = Sums(
-            place,
-            [
-                Part(d_fc2[1], fc2_got, 0, cut, orders[0]),
-                Part(d_fc1[1], fc1_got, 0, cut, orders[1]),
-                Part(d_fc2[1], fc2_got, cut, fc2_rows - cut, orders[2]),
-                Part(d_fc1[1], fc1_got, cut, fc1_rows - cut, orders[2]),
-                Part(d_proj[1], proj_got, 0, part, orders[2]),
-            ],
-        )
-        (do_t,) = tie((do_t,), [sums, two])
-        two.step(None)
-        pieces = [back_piece(do_t, first=i * quarter) for i in range(3)]
+        parts = [
+            Part(d_fc2[1], fc2_got, 0, cut, orders[0]),
+            Part(d_fc1[1], fc1_got, 0, cut, orders[1]),
+            Part(d_fc2[1], fc2_got, cut, fc2_rows - cut, orders[2]),
+            Part(d_fc1[1], fc1_got, cut, fc1_rows - cut, orders[2]),
+            Part(d_proj[1], proj_got, 0, part, orders[2]),
+        ]
+        two = Rider(two, far + near)
+        sums = Sums(place, parts, streamed=True)
+        sums.join(two)
+        for counts in ((4, 4, 2), (4,), (2,)):
+            (do_t, *pieces) = tie((do_t, *pieces), [sums])
+            attention(counts)
+            sums.step()
+        (a1_t, *pieces) = tie((a1_t, *pieces), [sums])
+        d_qkv, sums_q = qkv_grad(own, a1_t, pieces, halved)
+        qkv_got = swap(d_qkv[0], "narrow", 1)
+        biases = bias_rows(sums_q)
+        drows, one = rows_back(seg, pieces, w_qkv_t, x_view, dx1, mod_blocks, biases)
         sums.step()
-        (do_t, *pieces) = tie((do_t, *pieces), [sums, two])
-        for bit in far:
-            two.step(bit)
-        pieces.append(back_piece(do_t, first=3 * quarter))
-        sums.step()
-        (a1_t, *pieces) = tie((a1_t, *pieces), [sums, two])
+        qkv_parts = [Part(d_qkv[1], qkv_got, i * part, part, orders[i]) for i in range(3)]
+        late = Sums(place, qkv_parts)
+        (drows,) = tie((drows,), [sums])
+    else:
+        attention((4, 4, 4, 4))
         d_qkv, sums_q = qkv_grad(own, a1_t, pieces, halved)
-        sums.step()
-        qkv_got = swap(d_qkv[0], "narrow", 1)
-        (dx1, *pieces) = tie((dx1, *pieces), [sums, two])
-    else:
-        for bit in [None] + far:
-            two.step(bit)
-        pieces = [back_piece(do_t, first=i * quarter) for i in range(4)]
-        d_qkv, sums_q = qkv_grad(own, a1_t, pieces, halved)
-    for bit in near:
-        two.step(bit)
-    drows, sums_one = rows_back(pieces, w_qkv_t, x_view, dx1, mod_blocks)
+        drows, one = rows_back(seg, pieces, w_qkv_t, x_view, dx1, mod_blocks, bias_rows(sums_q))
     back = drows
     if not tiled:
         back = back.reshape(blocks, wide, per_block, feat).transpose(1, 0, 2, 3)
     back = exchange(back.reshape(wide, rows // wide, feat))
-    biases = jnp.concatenate(
-        [
-            grad_b_fc1.reshape(devices, -1),
-            grad_b_fc2.reshape(devices, -1),
-            grad_b_proj.reshape(devices, -1),
-            jnp.concatenate([sums_q[0], sums_q[2]]).reshape(devices, -1),
-        ],
-        axis=1,
-    )
-    per_device = biases.shape[1]
-    one = Gather(
-        jnp.concatenate(
-            [slot_sums(sums_one), biases.astype(BF16).reshape(slots, 2 * feat)], axis=0
-        )[None]
-    )
-    one.step(None)
     if halved.split:
-        late = Sums(
-            place, [Part(d_qkv[1], qkv_got, i * part, part, orders[i]) for i in range(3)]
+        one = Rider(one, far + near)
+        late.join(one)
+        tie((), [late])
+        late.step()
+        late.step()
+        (back,) = tie((back,), [late])
+        while late.going:
+            late.step()
+        one_all, two_all = (
+            jnp.concatenate([a, swap(a, "narrow", 1)], axis=0)
+            for a in (r.keep[0].reshape(wide, -1, feat) for r in (one, two))
         )
-        tie((), [late, one])
-        for i in range(len(orders[0])):
-            late.step()
-            if i == 0:
-                for bit in far:
-                    one.step(bit)
-            if i == BACK_ROUNDS:
-                (back,) = tie((back,), [late, one])
-            else:
-                tie((), [late, one])
-        sums.step()
-        for bit in near:
-            one.step(bit)
-        fc2_a, fc1_a, fc2_b, fc1_b, grad_w_proj = (p.keep[0] for p in sums.parts)
+        fc2_a, fc1_a, fc2_b, fc1_b, grad_w_proj = (p.keep[0] for p in parts)
         grad_w_fc2 = jnp.concatenate([fc2_a, fc2_b], axis=0)
         grad_w_fc1 = jnp.concatenate([fc1_a, fc1_b], axis=0)
         grad_w_fc1 = (
             grad_w_fc1.reshape(hidden // feat, part, feat).transpose(1, 0, 2).reshape(part, hidden)
         )
-        grad_w_qkv = jnp.concatenate([p.keep[0] for p in late.parts], axis=1)
+        grad_w_qkv = jnp.concatenate([p.keep[0] for p in qkv_parts], axis=1)
     else:
-        for bit in far + near:
-            one.step(bit)
+        one_all, two_all = (lax.all_gather(a, both, axis=0, tiled=True) for a in (one, two))
 
         def scattered(full):
             return lax.psum_scatter(full, both, scatter_dimension=0, tiled=True).astype(F32)
@@ -1115,20 +1142,29 @@
     dx_src = merge(src, back.reshape(rows, feat))
 
     me = group * halves + half
-    count = 2 * slots * devices
     grad_w_mod, grad_b_mod, dact, biases = mod_grad(
-        group, me, one.values.reshape(count, -1), two.values.reshape(count, -1), w_mod, part,
-        feat // wide, slots,
+        group, me, one_all, two_all, w_mod, part, feat // wide, slots
     )
     grad_b_mod = lax.dynamic_slice_in_dim(grad_b_mod[0], me * 6 * part, 6 * part)
-    biases = lax.dynamic_slice_in_dim(biases[slots:].reshape(-1), me * per_device, per_device)
+
+    def own_part(first, count):
+        rows_of = biases[first : first + count].reshape(-1)
+        share = rows_of.shape[0] // devices
+        return lax.dynamic_slice_in_dim(rows_of, me * share, share)
+
+    fc1_lines = hidden // feat
+    s_fc1, s_fc2, s_proj = own_part(0, fc1_lines), own_part(fc1_lines, 1), own_part(fc1_lines + 1, 1)
+    s_qv = own_part(fc1_lines + 2, 2)
     spot = jnp.maximum(cidx, 0)
-    spot = one.place((spot // slots) ^ group) * 2 * slots + spot % slots
+    bucket_of, slot_of = spot // slots, spot % slots
+    if halved.split:
+        spot = one.place(bucket_of ^ group) * 2 * slots + slot_of
+    else:
+        spot = (bucket_of * halves + half) * 2 * slots + slot_of
     _, silu_back = jax.vjp(jax.nn.silu, cond.astype(F32))
     dcond = silu_back(jnp.take(dact, spot, axis=0))[0].astype(BF16)
     dcond = jnp.where(cidx[:, None] >= 0, dcond, jnp.zeros((), BF16))
 
-    at_two, at_proj, at_qv = hidden // devices, hidden // devices + part, hidden // devices + 2 * part
     return (
         y_dest,
         dx_src,
@@ -1136,13 +1172,13 @@
         grad_w_mod,
         grad_b_mod,
         grad_w_qkv,
-        biases[at_qv:],
+        s_qv,
         grad_w_proj,
-        biases[at_proj:at_qv],
+        s_proj,
         grad_w_fc1,
-        biases[:at_two],
+        s_fc1,
         grad_w_fc2,
-        biases[at_two:at_proj],
+        s_fc2,
     )
 
 

time: 526 us -> 507 us (0.964)
  Pallas kernels: 294 us -> 285 us
  other arithmetic: 20.9 us -> 12.4 us
  waiting for transfers between devices: 75.8 us -> 69 us
    pallas_call x10, Pallas kernels: 52.6 us -> 41.6 us  [relay(): pl.pallas_call(functools.partial(relay_kernel, plan=plan, inputs=len(arra...]
    pallas_call x4 -> x5, Pallas kernels: 56.8 us -> 59.4 us  [attend_back(): pl.pallas_call(functools.partial(attend_back_kernel, blocks=rows // BLK,...]
    unnamed x99 -> x124, local copies, waits for them, and re-layouts: 27.4 us -> 29.4 us
  transfers between devices with their start and end apart: 37 -> 37, of which waited for: 15 -> 13; matrix products, arithmetic and copies ran while one was open for 11% -> 10% of each run, Pallas kernels for 26% -> 27%
where the time goes in v3:
time: 507 us; the launch traced here: 498 us
  Pallas kernels  285 us (56%)
  waiting for transfers between devices  69 us (14%)
  starting transfers between devices  59.2 us (12%)
  local copies, waits for them, and re-layouts  49.6 us (10%)
  matrix products  20.8 us (4%)
  other arithmetic  12.4 us (2%)
    ppermute x34, waiting for transfers between devices, swap(): return lax.ppermute(values, axis, [(i, i ^ bit) for i in range(count)])  65.4 us
    pallas_call x5, Pallas kernels, attend_back(): pl.pallas_call(functools.partial(attend_back_kernel, blocks=rows // BLK,...  59.4 us
    pallas_call x1, Pallas kernels, mlp(): pl.pallas_call(functools.partial(mlp_kernel, first=first, second=second),...  57.8 us
    pallas_call x10, Pallas kernels, relay(): pl.pallas_call(functools.partial(relay_kernel, plan=plan, inputs=len(arra...  41.6 us
    ppermute x34, starting transfers between devices, swap(): return lax.ppermute(values, axis, [(i, i ^ bit) for i in range(count)])  40.9 us
    pallas_call x1, Pallas kernels, attend(): pl.pallas_call(functools.partial(attend_kernel, blocks=rows // BLK, heads...  37.6 us
    unnamed x124, local copies, waits for them, and re-layouts  29.4 us
    pallas_call x1, Pallas kernels, middle(): pl.pallas_call(functools.partial(middle_kernel, halves=halves), grid=(blo...  17.6 us
  transfers between devices with their start and end apart: 37, of which 13 were waited for; matrix products, arithmetic and copies ran while one was open for 10% of the time, Pallas kernels for 27%

profile of v3, /device:TPU:0, one launch (start us, length us, event | category | flops | bytes accessed | tf_op | source)
XLA Modules:
  0.0 497.9 jit_solution(9718755000198522967)
XLA Ops:
  7.8 8.3 %all-to-all-start.1 = ((bf16[16,2,128]{2,1,0:T(2,128)(2,1)}), bf16[16,2,128]{2,1,0:T(2,128)(2,1)S(1)}, u32[]{:S(2)}, u32[]{:S(2)}) async-start(bf16[16,2,128]{2,1,0:T(2,128)(2,1)} %reshape.199), calls=%async_computation.1 | async-start | bytes 16384 | tf_op jit(solution)/shard_map/all_to_all | solution.py:1010
  16.2 5.5 %shard_map.247 = (bf16[16,64,1024]{2,1,0:T(8,128)(2,1)}, s32[64]{0:T(128)}) custom-call(s32[64]{0:T(128)} %dynamic_slice.27.len_ref, s32[64]{0:T(128)} %dynamic_slice.28.buck_ref, bf16[1024,1024]{1,0:T(8,128)(2,1)} %x_ref.1), custom_call_target="tpu_custom_call" | custom-call | flops 1 | bytes 1 | tf_op jit(solution)/shard_map/pallas_call | solution.py:137
  23.4 5.5 %all-to-all-start = ((bf16[16,64,1024]{2,1,0:T(8,128)(2,1)}), bf16[16,64,1024]{2,1,0:T(8,128)(2,1)S(1)}, u32[]{:S(2)}, u32[]{:S(2)}) async-start(bf16[16,64,1024]{2,1,0:T(8,128)(2,1)} %get-tuple-element.196), calls=%async_computation | async-start | bytes 4194304 | tf_op jit(solution)/shard_map/all_to_all | solution.py:1009
  35.8 8.7 %copy.46 = bf16[1024,3072]{0,1:T(8,128)(2,1)} copy(bf16[1024,3072]{1,0:T(8,128)(2,1)} %param.21) | data formatting | bytes 12582912 | tf_op args[6]
  44.8 6.3 %convolution_add_fusion = f32[4,6144]{1,0:T(4,128)S(1)} fusion(bf16[4,1024]{1,0:T(4,128)(2,1)S(1)} %fusion.7.act_ref, bf16[1024,6144]{1,0:T(8,128)(2,1)} %w_ref.5, f32[6144]{0:T(1024)S(1)} %convert_element_type.55), kind=kOutput, calls=%fused_computation.1 | convolution fusion | flops 50356224 | bytes 12713984 | tf_op jit(solution)/shard_map/dot_general | solution.py:1017
  55.1 14.5 %fusion.22.dg_ref = f32[1024,4096]{1,0:T(8,128)} fusion(bf16[1024,1024]{1,0:T(8,128)(2,1)S(1)} %fusion.df_ref, bf16[4096,1024]{1,0:T(8,128)(2,1)} %w2_ref.1), kind=kOutput, calls=%fused_computation.83 | convolution fusion | flops 8589934592 | bytes 27262976 | tf_op jit(solution)/shard_map/dot_general | solution.py:29
  73.0 13.5 %shard_map.248 = (bf16[3072,1024]{1,0:T(8,128)(2,1)}, bf16[1024,1024]{1,0:T(8,128)(2,1)}) custom-call(bf16[16,4,16,1024]{3,2,1,0:T(8,128)(2,1)} %bitcast.67, f32[4,6,1024]{2,1,0:T(8,128)} %copy-done.5, bf16[3072,1024]{1,0:T(8,128)(2,1)} %bitcast.65, f32[3072,1]{1,0:T(8,128)} %copy.47.b_ref), custom_call_target="tpu_custom_call" | custom-call | flops 1 | bytes 1 | tf_op jit(solution)/shard_map/pallas_call | solution.py:244
  86.5 37.6 %shard_map.249 = (bf16[1024,1024]{1,0:T(8,128)(2,1)}, f32[16,1,1024]{2,1,0:T(1,128)}) custom-call(s32[4]{0:T(128)} %get-tuple-element.195.seg_ref, bf16[3072,1024]{1,0:T(8,128)(2,1)} %get-tuple-element.198.q_ref.k_ref.v_ref, bf16[3072,1024]{1,0:T(8,128)(2,1)} %get-tuple-element.198.q_ref.k_ref.v_ref, bf16[3072,1024]{1,0:T(8,128)(2,1)} %get-tuple-element.198.q_ref.k_ref.v_ref), custom_call_target="tpu_custom_call" | custom-call | flops 1 | bytes 1 | tf_op jit(solution)/shard_map/pallas_call | solution.py:304
  124.1 9.0 %shard_map.250 = (f32[1024,1024]{1,0:T(8,128)}, f32[1024,1024]{1,0:T(8,128)}, bf16[1024,1024]{1,0:T(8,128)(2,1)}, bf16[1024,1024]{1,0:T(8,128)(2,1)}) custom-call(bf16[1024,1024]{1,0:T(8,128)(2,1)} %get-tuple-element.199.o_ref, bf16[1024,1024]{1,0:T(8,128)(2,1)} %w_ref.4, f32[1,1024]{1,0:T(1,128)} %bitcast.95, bf16[16,4,16,1024]{3,2,1,0:T(8,128)(2,1)} %bitcast.68, ...), custom_call_target="tpu_custom_call" | custom-call | flops 1 | bytes 1 | tf_op jit(solution)/shard_map/pallas_call | solution.py:474
  133.1 57.8 %shard_map.251 = (f32[1024,1024]{1,0:T(8,128)}, f32[1024,1024]{1,0:T(8,128)}, f32[1,4096]{1,0:T(1,128)}, bf16[16,4,32,1024]{3,2,1,0:T(8,128)(2,1)}, bf16[16,4,32...) custom-call(s32[1]{0:T(128)} %bitcast.half_ref, ...), custom_call_target="tpu_custom_call" | custom-call | flops 1 | bytes 1 | tf_op jit(solution)/shard_map/pallas_call | solution.py:559
  192.1 17.6 %shard_map.252 = (bf16[1024,1024]{1,0:T(8,128)(2,1)}, f32[1024,1024]{1,0:T(8,128)}, bf16[1024,1024]{1,0:T(8,128)(2,1)}, f32[1,1024]{1,0:T(1,128)}, bf16[1,32,102...) custom-call(s32[1]{0:T(128)} %bitcast.half_ref, s32[4]{0:T(128)} %get-tuple-element.195.seg_ref, ...), custom_call_target="tpu_custom_call" | custom-call | flops 1 | bytes 1 | tf_op jit(solution)/shard_map/pallas_call | solution.py:640
  215.1 9.9 %shard_map.253 = (bf16[8,96,1024]{2,1,0:T(8,128)(2,1)}, bf16[8,96,1024]{2,1,0:T(8,128)(2,1)}, bf16[8,96,1024]{2,1,0:T(8,128)(2,1)}, bf16[8,96,1024]{2,1,0:T(8,12...) custom-call(s32[1]{0:T(128)} %bitcast.1.me_ref, ...), custom_call_target="tpu_custom_call" | custom-call | flops 1 | bytes 1 | tf_op jit(solution)/shard_map/pallas_call | solution.py:919
  235.0 8.4 %shard_map.256.refs_2_ = bf16[3,128,1024]{2,1,0:T(8,128)(2,1)} custom-call(s32[4]{0:T(128)} %get-tuple-element.195.seg_ref, bf16[3072,1024]{1,0:T(8,128)(2,1)} %get-tuple-element.198.q_ref.k_ref.v_ref, bf16[3072,1024]{1,0:T(8,128)(2,1)} %get-tuple-element.198.q_ref.k_ref.v_ref, bf16[3072,1024]{1,0:T(8,128)(2,1)} %get-tuple-element.198.q_ref.k_ref.v_ref, ...), custom_call_target="tpu_custom_call" | custom-call | flops 1 | bytes 1 | tf_op jit(solution)/shard_map/pallas_call | solution.py:368
  243.4 14.3 %shard_map.255.refs_1_ = bf16[3,256,1024]{2,1,0:T(8,128)(2,1)} custom-call(s32[4]{0:T(128)} %get-tuple-element.195.seg_ref, bf16[3072,1024]{1,0:T(8,128)(2,1)} %get-tuple-element.198.q_ref.k_ref.v_ref, bf16[3072,1024]{1,0:T(8,128)(2,1)} %get-tuple-element.198.q_ref.k_ref.v_ref, bf16[3072,1024]{1,0:T(8,128)(2,1)} %get-tuple-element.198.q_ref.k_ref.v_ref, ...), custom_call_target="tpu_custom_call" | custom-call | flops 1 | bytes 1 | tf_op jit(solution)/shard_map/pallas_call | solution.py:368
  257.7 14.1 %shard_map.254.refs_0_ = bf16[3,256,1024]{2,1,0:T(8,128)(2,1)} custom-call(s32[4]{0:T(128)} %get-tuple-element.195.seg_ref, bf16[3072,1024]{1,0:T(8,128)(2,1)} %get-tuple-element.198.q_ref.k_ref.v_ref, bf16[3072,1024]{1,0:T(8,128)(2,1)} %get-tuple-element.198.q_ref.k_ref.v_ref, bf16[3072,1024]{1,0:T(8,128)(2,1)} %get-tuple-element.198.q_ref.k_ref.v_ref, ...), custom_call_target="tpu_custom_call" | custom-call | flops 1 | bytes 1 | tf_op jit(solution)/shard_map/pallas_call | solution.py:368
  274.6 6.5 %shard_map.257 = (bf16[4,96,1024]{2,1,0:T(8,128)(2,1)}, bf16[4,96,1024]{2,1,0:T(8,128)(2,1)}, bf16[4,96,1024]{2,1,0:T(8,128)(2,1)}, bf16[4,96,1024]{2,1,0:T(8,12...) custom-call(s32[1]{0:T(128)} %bitcast.1.me_ref, ...), custom_call_target="tpu_custom_call" | custom-call | flops 1 | bytes 1 | tf_op jit(solution)/shard_map/pallas_call | solution.py:919
  285.7 14.3 %shard_map.258.refs_3_ = bf16[3,256,1024]{2,1,0:T(8,128)(2,1)} custom-call(s32[4]{0:T(128)} %get-tuple-element.195.seg_ref, bf16[3072,1024]{1,0:T(8,128)(2,1)} %get-tuple-element.198.q_ref.k_ref.v_ref, bf16[3072,1024]{1,0:T(8,128)(2,1)} %get-tuple-element.198.q_ref.k_ref.v_ref, bf16[3072,1024]{1,0:T(8,128)(2,1)} %get-tuple-element.198.q_ref.k_ref.v_ref, ...), custom_call_target="tpu_custom_call" | custom-call | flops 1 | bytes 1 | tf_op jit(solution)/shard_map/pallas_call | solution.py:368
  315.2 8.4 %shard_map.260.refs_4_ = bf16[3,128,1024]{2,1,0:T(8,128)(2,1)} custom-call(s32[4]{0:T(128)} %get-tuple-element.195.seg_ref, bf16[3072,1024]{1,0:T(8,128)(2,1)} %get-tuple-element.198.q_ref.k_ref.v_ref, bf16[3072,1024]{1,0:T(8,128)(2,1)} %get-tuple-element.198.q_ref.k_ref.v_ref, bf16[3072,1024]{1,0:T(8,128)(2,1)} %get-tuple-element.198.q_ref.k_ref.v_ref, ...), custom_call_target="tpu_custom_call" | custom-call | flops 1 | bytes 1 | tf_op jit(solution)/shard_map/pallas_call | solution.py:368
  333.7 14.8 %shard_map.262 = (bf16[16,3,32,1024]{3,2,1,0:T(8,128)(2,1)}, bf16[16,3,32,1024]{3,2,1,0:T(8,128)(2,1)}, f32[3,8,1024]{2,1,0:T(8,128)}) custom-call(s32[1]{0:T(128)} %bitcast.half_ref, bf16[1024,1024]{1,0:T(8,128)(2,1)} %get-tuple-element.294.a_ref, bf16[3,256,1024]{2,1,0:T(8,128)(2,1)} %shard_map.254.refs_0_, bf16[3,256,1024]{2,1,0:T(8,128)(2,1)} %shard_map.255.refs_1_, ...), custom_call_target="tpu_custom_call" | custom-call | flops 1 | bytes 1 | tf_op jit(solution)/shard_map/pallas_call | solution.py:442
  349.9 15.6 %shard_map.263 = (bf16[16,4,16,1024]{3,2,1,0:T(8,128)(2,1)}, bf16[1,16,1024]{2,1,0:T(8,128)(2,1)}) custom-call(s32[4]{0:T(128)} %get-tuple-element.195.seg_ref, bf16[3072,1024]{1,0:T(8,128)(2,1)} %bitcast.66, bf16[16,4,16,1024]{3,2,1,0:T(8,128)(2,1)} %bitcast.69, f32[1024,1024]{1,0:T(8,128)} %get-tuple-element.208.dx_ref, f32[4,6,1024]{2,1,0:T(8,128)} %copy-done.5, ...), custom_call_target="tpu_custom_call" | custom-call | flops 1 | bytes 1 | tf_op jit(solution)/shard_map/pallas_call | solution.py:697
  386.9 37.6 %collective-permute-done.21.refs_7_ = bf16[1,16,1024]{2,1,0:T(8,128)(2,1)S(1)} collective-permute-done((bf16[1,16,1024]{2,1,0:T(8,128)(2,1)S(1)}, bf16[1,16,1024]{2,1,0:T(8,128)(2,1)S(1)}, u32[]{:S(2)}, u32[]{:S(2)}) %collective-permute-start.21) | collective-permute-done | bytes 32800 | tf_op jit(solution)/shard_map/ppermute | solution.py:787
  435.4 6.3 %collective-permute-done.25.refs_7_ = bf16[1,32,1024]{2,1,0:T(8,128)(2,1)S(1)} collective-permute-done((bf16[1,32,1024]{2,1,0:T(8,128)(2,1)}, bf16[1,32,1024]{2,1,0:T(8,128)(2,1)S(1)}, u32[]{:S(2)}, u32[]{:S(2)}) %collective-permute-start.25) | collective-permute-done | bytes 65568 | tf_op jit(solution)/shard_map/ppermute | solution.py:787
  458.9 6.6 %collective-permute-done.30.refs_1_ = bf16[1,96,1024]{2,1,0:T(8,128)(2,1)} collective-permute-done((bf16[1,96,1024]{2,1,0:T(8,128)(2,1)}, bf16[1,96,1024]{2,1,0:T(8,128)(2,1)}, u32[]{:S(2)}, u32[]{:S(2)}) %collective-permute-start.30) | collective-permute-done | bytes 196640 | tf_op jit(solution)/shard_map/ppermute | solution.py:787
  484.1 5.7 %shard_map.271 = (f32[32,6144]{1,0:T(8,128)}, f32[1,6144]{1,0:T(1,128)}, f32[256,64]{1,0:T(8,128)}, f32[8,1024]{1,0:T(8,128)}) custom-call(s32[2]{0:T(128)} %pad_add_fusion.ids_ref, bf16[32,16,1024]{2,1,0:T(8,128)(2,1)} %pad_maximum_fusion.1.one_ref, bf16[32,32,1024]{2,1,0:T(8,128)(2,1)} %pad_maximum_fusion.two_ref, bf16[1024,6144]{1,0:T(8,128)(2,1)} %w_ref.5), custom_call_target="tpu_custom_call" | custom-call | flops 1 | bytes 1 | tf_op jit(solution)/shard_map/pallas_call | solution.py:756
  (243 shorter events, 149.5 us)
Async XLA Ops:
  7.8 15.5 %all-to-all-start.1 = ((bf16[16,2,128]{2,1,0:T(2,128)(2,1)}), bf16[16,2,128]{2,1,0:T(2,128)(2,1)S(1)}, u32[]{:S(2)}, u32[]{:S(2)}) async-start(bf16[16,2,128]{2,1,0:T(2,128)(2,1)} %reshape.199), calls=%async_computation.1 | async-start | bytes 16384 | tf_op jit(solution)/shard_map/all_to_all | solution.py:1010
  23.4 48.3 %all-to-all-start = ((bf16[16,64,1024]{2,1,0:T(8,128)(2,1)}), bf16[16,64,1024]{2,1,0:T(8,128)(2,1)S(1)}, u32[]{:S(2)}, u32[]{:S(2)}) async-start(bf16[16,64,1024]{2,1,0:T(8,128)(2,1)} %get-tuple-element.196), calls=%async_computation | async-start | bytes 4194304 | tf_op jit(solution)/shard_map/all_to_all | solution.py:1009
  190.9 21.8 %collective-permute-start = (bf16[16,128,1024]{2,1,0:T(8,128)(2,1)}, bf16[16,128,1024]{2,1,0:T(8,128)(2,1)S(1)}, u32[]{:S(2)}, u32[]{:S(2)}) collective-permute-start(bf16[16,128,1024]{2,1,0:T(8,128)(2,1)} %get-tuple-element.214), channel_id=1, source_target_pairs={{0,1},{1,0},{2,3},{3,2},{4,5},{5,4},{6,7},{7,6},{8,9},{9,8},{10,11... | collective-permute-start | bytes 12582920 | tf_op jit(solution)/shard_map/ppermute | solution.py:787
  191.0 21.7 %collective-permute-start.1 = (bf16[16,128,1024]{2,1,0:T(8,128)(2,1)}, bf16[16,128,1024]{2,1,0:T(8,128)(2,1)}, u32[]{:S(2)}, u32[]{:S(2)}) collective-permute-start(bf16[16,128,1024]{2,1,0:T(8,128)(2,1)} %bitcast.99), channel_id=1, source_target_pairs={{0,1},{1,0},{2,3},{3,2},{4,5},{5,4},{6,7},{7,6},{8,9},{9,8},{10,11... | collective-permute-start | bytes 12582920 | tf_op jit(solution)/shard_map/ppermute | solution.py:787
  225.0 46.8 %collective-permute-start.3 = (bf16[8,96,1024]{2,1,0:T(8,128)(2,1)}, bf16[8,96,1024]{2,1,0:T(8,128)(2,1)S(1)}, u32[]{:S(2)}, u32[]{:S(2)}) collective-permute-start(bf16[8,96,1024]{2,1,0:T(8,128)(2,1)} %get-tuple-element.231), channel_id=1, source_target_pairs={{0,2},{2,0},{4,6},{6,4},{8,10},{10,8},{12,14},{14,12},{16,18},{18,... | collective-permute-start | bytes 4718600 | tf_op jit(solution)/shard_map/ppermute | solution.py:787
  225.9 45.9 %collective-permute-start.4 = (bf16[8,96,1024]{2,1,0:T(8,128)(2,1)}, bf16[8,96,1024]{2,1,0:T(8,128)(2,1)S(1)}, u32[]{:S(2)}, u32[]{:S(2)}) collective-permute-start(bf16[8,96,1024]{2,1,0:T(8,128)(2,1)} %get-tuple-element.233), channel_id=1, source_target_pairs={{0,4},{2,6},{4,0},{6,2},{8,12},{10,14},{12,8},{14,10},{16,20},{18,... | collective-permute-start | bytes 4718600 | tf_op jit(solution)/shard_map/ppermute | solution.py:787
  229.4 42.4 %collective-permute-start.5 = (bf16[8,96,1024]{2,1,0:T(8,128)(2,1)}, bf16[8,96,1024]{2,1,0:T(8,128)(2,1)S(1)}, u32[]{:S(2)}, u32[]{:S(2)}) collective-permute-start(bf16[8,96,1024]{2,1,0:T(8,128)(2,1)} %get-tuple-element.235), channel_id=1, source_target_pairs={{0,8},{2,10},{4,12},{6,14},{8,0},{10,2},{12,4},{14,6},{16,24},{18,... | collective-permute-start | bytes 4718600 | tf_op jit(solution)/shard_map/ppermute | solution.py:787
  234.7 37.0 %collective-permute-start.6 = (bf16[1,32,1024]{2,1,0:T(8,128)(2,1)S(1)}, bf16[1,32,1024]{2,1,0:T(8,128)(2,1)S(1)}, u32[]{:S(2)}, u32[]{:S(2)}) collective-permute-start(bf16[1,32,1024]{2,1,0:T(8,128)(2,1)S(1)} %copy-done.41), channel_id=1, source_target_pairs={{0,16},{2,18},{4,20},{6,22},{8,24},{10,26},{12,28},{14,30},{16,0},... | collective-permute-start | bytes 196616 | tf_op jit(solution)/shard_map/ppermute | solution.py:787
  281.1 23.4 %collective-permute-start.7 = (bf16[4,96,1024]{2,1,0:T(8,128)(2,1)}, bf16[4,96,1024]{2,1,0:T(8,128)(2,1)S(1)}, u32[]{:S(2)}, u32[]{:S(2)}) collective-permute-start(bf16[4,96,1024]{2,1,0:T(8,128)(2,1)} %get-tuple-element.254), channel_id=1, source_target_pairs={{0,4},{2,6},{4,0},{6,2},{8,12},{10,14},{12,8},{14,10},{16,20},{18,... | collective-permute-start | bytes 2359304 | tf_op jit(solution)/shard_map/ppermute | solution.py:787
  281.6 23.0 %collective-permute-start.8 = (bf16[4,96,1024]{2,1,0:T(8,128)(2,1)}, bf16[4,96,1024]{2,1,0:T(8,128)(2,1)S(1)}, u32[]{:S(2)}, u32[]{:S(2)}) collective-permute-start(bf16[4,96,1024]{2,1,0:T(8,128)(2,1)} %get-tuple-element.256), channel_id=1, source_target_pairs={{0,8},{2,10},{4,12},{6,14},{8,0},{10,2},{12,4},{14,6},{16,24},{18,... | collective-permute-start | bytes 2359304 | tf_op jit(solution)/shard_map/ppermute | solution.py:787
  283.7 20.9 %collective-permute-start.9 = (bf16[4,96,1024]{2,1,0:T(8,128)(2,1)}, bf16[4,96,1024]{2,1,0:T(8,128)(2,1)S(1)}, u32[]{:S(2)}, u32[]{:S(2)}) collective-permute-start(bf16[4,96,1024]{2,1,0:T(8,128)(2,1)} %get-tuple-element.258), channel_id=1, source_target_pairs={{0,2},{2,0},{4,6},{6,4},{8,10},{10,8},{12,14},{14,12},{16,18},{18,... | collective-permute-start | bytes 2359304 | tf_op jit(solution)/shard_map/ppermute | solution.py:787
  284.4 20.2 %collective-permute-start.10 = (bf16[1,64,1024]{2,1,0:T(8,128)(2,1)}, bf16[1,64,1024]{2,1,0:T(8,128)(2,1)S(1)}, u32[]{:S(2)}, u32[]{:S(2)}) collective-permute-start(bf16[1,64,1024]{2,1,0:T(8,128)(2,1)} %get-tuple-element.262.refs_8_), channel_id=1, source_target_pairs={{0,2},{2,0},{4,6},{6,4},{8,10},{10,8},{12,14},{14,12},{16,18},{18,... | collective-permute-start | bytes 393224 | tf_op jit(solution)/shard_map/ppermute | solution.py:787
  310.9 15.3 %collective-permute-start.11 = (bf16[2,96,1024]{2,1,0:T(8,128)(2,1)}, bf16[2,96,1024]{2,1,0:T(8,128)(2,1)S(1)}, u32[]{:S(2)}, u32[]{:S(2)}) collective-permute-start(bf16[2,96,1024]{2,1,0:T(8,128)(2,1)} %get-tuple-element.278), channel_id=1, source_target_pairs={{0,8},{2,10},{4,12},{6,14},{8,0},{10,2},{12,4},{14,6},{16,24},{18,... | collective-permute-start | bytes 1179656 | tf_op jit(solution)/shard_map/ppermute | solution.py:787
  311.2 15.0 %collective-permute-start.12 = (bf16[2,96,1024]{2,1,0:T(8,128)(2,1)}, bf16[2,96,1024]{2,1,0:T(8,128)(2,1)S(1)}, u32[]{:S(2)}, u32[]{:S(2)}) collective-permute-start(bf16[2,96,1024]{2,1,0:T(8,128)(2,1)} %get-tuple-element.280), channel_id=1, source_target_pairs={{0,2},{2,0},{4,6},{6,4},{8,10},{10,8},{12,14},{14,12},{16,18},{18,... | collective-permute-start | bytes 1179656 | tf_op jit(solution)/shard_map/ppermute | solution.py:787
  312.0 14.2 %collective-permute-start.13 = (bf16[2,96,1024]{2,1,0:T(8,128)(2,1)}, bf16[2,96,1024]{2,1,0:T(8,128)(2,1)S(1)}, u32[]{:S(2)}, u32[]{:S(2)}) collective-permute-start(bf16[2,96,1024]{2,1,0:T(8,128)(2,1)} %get-tuple-element.282), channel_id=1, source_target_pairs={{0,4},{2,6},{4,0},{6,2},{8,12},{10,14},{12,8},{14,10},{16,20},{18,... | collective-permute-start | bytes 1179656 | tf_op jit(solution)/shard_map/ppermute | solution.py:787
  330.9 34.6 %collective-permute-start.15 = (bf16[1,288,1024]{2,1,0:T(8,128)(2,1)}, bf16[1,288,1024]{2,1,0:T(8,128)(2,1)S(1)}, u32[]{:S(2)}, u32[]{:S(2)}) collective-permute-start(bf16[1,288,1024]{2,1,0:T(8,128)(2,1)} %get-tuple-element.303), channel_id=1, source_target_pairs={{0,16},{2,18},{4,20},{6,22},{8,24},{10,26},{12,28},{14,30},{16,0},... | collective-permute-start | bytes 1769480 | tf_op jit(solution)/shard_map/ppermute | solution.py:787
  333.1 32.5 %collective-permute-start.16 = (bf16[1,256,1024]{2,1,0:T(8,128)(2,1)}, bf16[1,256,1024]{2,1,0:T(8,128)(2,1)S(1)}, u32[]{:S(2)}, u32[]{:S(2)}) collective-permute-start(bf16[1,256,1024]{2,1,0:T(8,128)(2,1)} %get-tuple-element.309.refs_6_), channel_id=1, source_target_pairs={{0,8},{2,10},{4,12},{6,14},{8,0},{10,2},{12,4},{14,6},{16,24},{18,... | collective-permute-start | bytes 1572872 | tf_op jit(solution)/shard_map/ppermute | solution.py:787
  348.5 26.1 %collective-permute-start.17 = (bf16[16,96,1024]{2,1,0:T(8,128)(2,1)}, bf16[16,96,1024]{2,1,0:T(8,128)(2,1)}, u32[]{:S(2)}, u32[]{:S(2)}) collective-permute-start(bf16[16,96,1024]{2,1,0:T(8,128)(2,1)} %bitcast.100), channel_id=1, source_target_pairs={{0,1},{1,0},{2,3},{3,2},{4,5},{5,4},{6,7},{7,6},{8,9},{9,8},{10,11... | collective-permute-start | bytes 9437192 | tf_op jit(solution)/shard_map/ppermute | solution.py:787
  370.1 75.0 %all-to-all-start.2 = ((bf16[16,64,1024]{2,1,0:T(8,128)(2,1)}), bf16[16,64,1024]{2,1,0:T(8,128)(2,1)S(1)}, u32[]{:S(2)}, u32[]{:S(2)}) async-start(bf16[16,64,1024]{2,1,0:T(8,128)(2,1)} %bitcast.77), calls=%async_computation.2 | async-start | bytes 4194304 | tf_op jit(solution)/shard_map/all_to_all | solution.py:1110
  379.7 44.8 %collective-permute-start.18 = (bf16[8,32,1024]{2,1,0:T(8,128)(2,1)}, bf16[8,32,1024]{2,1,0:T(8,128)(2,1)S(1)}, u32[]{:S(2)}, u32[]{:S(2)}) collective-permute-start(bf16[8,32,1024]{2,1,0:T(8,128)(2,1)} %get-tuple-element.327), channel_id=1, source_target_pairs={{0,2},{2,0},{4,6},{6,4},{8,10},{10,8},{12,14},{14,12},{16,18},{18,... | collective-permute-start | bytes 1572872 | tf_op jit(solution)/shard_map/ppermute | solution.py:787
  381.6 42.9 %collective-permute-start.19 = (bf16[8,32,1024]{2,1,0:T(8,128)(2,1)}, bf16[8,32,1024]{2,1,0:T(8,128)(2,1)S(1)}, u32[]{:S(2)}, u32[]{:S(2)}) collective-permute-start(bf16[8,32,1024]{2,1,0:T(8,128)(2,1)} %get-tuple-element.329), channel_id=1, source_target_pairs={{0,4},{2,6},{4,0},{6,2},{8,12},{10,14},{12,8},{14,10},{16,20},{18,... | collective-permute-start | bytes 1572872 | tf_op jit(solution)/shard_map/ppermute | solution.py:787
  383.1 41.4 %collective-permute-start.20 = (bf16[8,32,1024]{2,1,0:T(8,128)(2,1)}, bf16[8,32,1024]{2,1,0:T(8,128)(2,1)S(1)}, u32[]{:S(2)}, u32[]{:S(2)}) collective-permute-start(bf16[8,32,1024]{2,1,0:T(8,128)(2,1)} %get-tuple-element.331), channel_id=1, source_target_pairs={{0,8},{2,10},{4,12},{6,14},{8,0},{10,2},{12,4},{14,6},{16,24},{18,... | collective-permute-start | bytes 1572872 | tf_op jit(solution)/shard_map/ppermute | solution.py:787
  384.5 39.9 %collective-permute-start.21 = (bf16[1,16,1024]{2,1,0:T(8,128)(2,1)S(1)}, bf16[1,16,1024]{2,1,0:T(8,128)(2,1)S(1)}, u32[]{:S(2)}, u32[]{:S(2)}) collective-permute-start(bf16[1,16,1024]{2,1,0:T(8,128)(2,1)S(1)} %copy-done.46), channel_id=1, source_target_pairs={{0,16},{2,18},{4,20},{6,22},{8,24},{10,26},{12,28},{14,30},{16,0},... | collective-permute-start | bytes 98312 | tf_op jit(solution)/shard_map/ppermute | solution.py:787
  434.6 41.1 %collective-permute-start.33 = (bf16[16,32,1024]{2,1,0:T(8,128)(2,1)S(1)}, bf16[16,32,1024]{2,1,0:T(8,128)(2,1)}, u32[]{:S(2)}, u32[]{:S(2)}) collective-permute-start(bf16[16,32,1024]{2,1,0:T(8,128)(2,1)S(1)} %bitcast.80), channel_id=1, source_target_pairs={{0,1},{1,0},{2,3},{3,2},{4,5},{5,4},{6,7},{7,6},{8,9},{9,8},{10,11... | collective-permute-start | bytes 3145736 | tf_op jit(solution)/shard_map/ppermute | solution.py:787
  (69 other events, 440.4 us)
